TPU v7x, 512 devices: a whole 4x8x8 slice. The times are simulated.
512 devices in a mesh: gx: 16 (over y, z_hi), gy: 8 (over x, core), gz: 4 (over z_lo).
Axes of the slice: x: 4, y: 8, z: 8 (z_hi: 2, z_lo: 4; z = z_hi * 4 + z_lo), core: 2. Of those that a mesh axis runs over, the one named last changes fastest.
Arguments:
- volume: bfloat16 [4, 32, 64, 512], P(None, 'gx', 'gy', 'gz'), may hold values from -6 to 6
- w_first: bfloat16 [32, 3, 3, 3, 4], replicated, may hold values from -0.625 to 0.625
- w_second: bfloat16 [32, 3, 3, 3, 32], replicated, may hold values from -0.21875 to 0.21875
- w_coarse: bfloat16 [64, 3, 3, 3, 32], replicated, may hold values from -0.21875 to 0.21875
- skip_cotangent: bfloat16 [32, 32, 64, 512], P(None, 'gx', 'gy', 'gz'), may hold values from -1.796875 to 1.796875
- coarse_cotangent: bfloat16 [64, 16, 32, 256], P('gz', 'gx', 'gy'), may hold values from -6 to 6
Outputs:
- skip: bfloat16 [32, 32, 64, 512], P(None, 'gx', 'gy', 'gz')
- coarse: bfloat16 [64, 16, 32, 256], P('gz', 'gx', 'gy')
- volume_grad: bfloat16 [4, 32, 64, 512], P(None, 'gx', 'gy', 'gz')
- first_wgrad: float32 [32, 3, 3, 3, 4], replicated
- second_wgrad: float32 [32, 3, 3, 3, 32], replicated
- coarse_wgrad: float32 [64, 3, 3, 3, 32], replicated
All inputs are finite; a program needn't handle non-finite values.
Results may differ from a plain program's by a relative error of at most 0.014.
Values may be sent and summed in bfloat16 or wider, within the bound.
No kernel may reach another device: no remote copies, remote signals or barrier semaphores. Data moves between devices by JAX's collectives and lax.ppermute only.
A program may use at most 64 MiB of HBM per device.

v0:
```python
import math

import jax
import jax.numpy as jnp
from jax import lax
from jax.experimental import pallas as pl
from jax.experimental.pallas import tpu as pltpu
from jax.sharding import PartitionSpec as P

AXES = ("gx", "gy", "gz")
LANES = 256
BF = jnp.bfloat16
F32 = jnp.float32


def shifted(block, axis, step):
    count = lax.axis_size(axis)
    pairs = [(i, i + step) for i in range(count) if 0 <= i + step < count]
    return lax.ppermute(block, axis, pairs)


def halo(cells, axis, dim, width):
    extent = cells.shape[dim]
    before, after = [], []
    for step in range(1, -(-width // extent) + 1):
        part = min(extent, width - (step - 1) * extent)
        tail = lax.slice_in_dim(cells, extent - part, extent, axis=dim)
        head = lax.slice_in_dim(cells, 0, part, axis=dim)
        before.insert(0, shifted(tail, axis, step))
        after.append(shifted(head, axis, -step))
    return jnp.concatenate(before + [cells] + after, axis=dim)


def slope(values):
    sigmoid_value = jax.nn.sigmoid(values)
    return sigmoid_value * (1.0 + values * (1.0 - sigmoid_value))


def silu(values):
    return values * jax.nn.sigmoid(values)


def store_taps(ref, place, values):
    chans, lanes = values.shape
    ref[place + (slice(0, chans),)] = pltpu.roll(values, 1, 1).astype(BF)
    ref[place + (slice(chans, 2 * chans),)] = values.astype(BF)
    ref[place + (slice(2 * chans, 3 * chans),)] = pltpu.roll(values, lanes - 1, 1).astype(BF)


def rows_at(ref, plane, row):
    part = ref[plane, row - 1 : row + 2]
    return part.reshape(part.shape[0] * part.shape[1], part.shape[2])


def dot(left, right):
    return jnp.dot(left, right, preferred_element_type=F32)


def dot_lanes(left, right):
    return lax.dot_general(left, right, (((1,), (1,)), ((), ())), preferred_element_type=F32)


def lane_mask(lanes, first, low, high):
    place = first + lax.broadcasted_iota(jnp.int32, (1, lanes), 1)
    return jnp.where((place >= low) & (place < high), 1.0, 0.0).astype(F32)


def keep(values, lanes_ok, *bounds):
    good = None
    for place, limit in bounds:
        here = (place >= 0) & (place < limit)
        good = here if good is None else good & here
    mask = lanes_ok * jnp.where(good, 1.0, 0.0).astype(F32)
    return jnp.where(mask > 0.5, values, 0.0)


def spread_conv(acc, weights, tapped, planes, rows, outputs, shift):
    matrix = weights[...]

    def one(n, carry):
        plane = planes[0] + n
        for row in range(*rows):
            summed = dot(matrix, rows_at(tapped, plane, row))
            for i in range(3):
                place = plane + shift - i
                acc[place, row] = acc[place, row] + summed[i * outputs : (i + 1) * outputs]
        return carry

    lax.fori_loop(0, planes[1] - planes[0], one, 0)


def clear(acc):
    def one(n, carry):
        acc[n] = jnp.zeros(acc.shape[1:], acc.dtype)
        return carry

    lax.fori_loop(0, acc.shape[0], one, 0)


def forward_kernel(
    sizes, offs, vol, w1, w2, w3, cot, pool,
    skip_o, coarse_o, cgrad_o, craw_o, fpre_o, spre_o, t1_o, t2_o,
    t1, acc1, t2, acc2, fine, t3,
):
    nx, ny, nz = sizes
    ox, oy, oz = offs[0], offs[1], offs[2]
    fine_ok = lane_mask(LANES, oz - 8, 0, nz)
    coarse_ok = lane_mask(128, oz // 2 - 4, 0, nz // 2)

    def volume_taps(x, carry):
        for y in range(16):
            store_taps(t1, (x, y), vol[x, y].astype(F32))
        return carry

    lax.fori_loop(0, 10, volume_taps, 0)
    clear(acc1)
    spread_conv(acc1, w1, t1, (0, 10), (1, 15), 32, 2)

    def first(n, carry):
        x = n + 1
        for y in range(1, 15):
            act = silu(acc1[x + 1, y])
            act = keep(act, fine_ok, (ox + x - 4, nx), (oy + y - 4, ny))
            store_taps(t2, (x, y), act.astype(BF).astype(F32))
        return carry

    lax.fori_loop(0, 8, first, 0)
    clear(acc2)
    spread_conv(acc2, w2, t2, (1, 9), (2, 14), 32, 2)

    def second(n, carry):
        for y in range(12):
            pre = acc2[n + 3, y + 2]
            spre_o[n, y] = pre
            fine[n, y] = silu(pre).astype(BF)
        return carry

    lax.fori_loop(0, 6, second, 0)

    def passed(n, carry):
        for y in range(10):
            fpre_o[n, y] = acc1[n + 4, y + 3]
            t1_o[n, y] = t1[n + 3, y + 3]
            t2_o[n, y] = t2[n + 3, y + 3]
        return carry

    lax.fori_loop(0, 4, passed, 0)
    for x in range(2):
        for y in range(8):
            whole = pltpu.roll(fine[x + 2, y + 2].astype(F32), LANES - 8, 1)
            skip_o[x, y] = whole[:, :128].astype(BF)

    matrix = pool[...]
    for x in range(3):
        for y in range(6):
            cube = fine[2 * x : 2 * x + 2, 2 * y : 2 * y + 2].reshape(128, LANES)
            parts = dot(cube, matrix)
            mean = (parts[0:32] + parts[32:64] + parts[64:96] + parts[96:128]) * 0.125
            mean = keep(mean, coarse_ok, (ox // 2 + x - 1, nx // 2), (oy // 2 + y - 1, ny // 2))
            store_taps(t3, (x, y), mean.astype(BF).astype(F32))

    own = lane_mask(128, 0, 4, 68)
    raw = [jnp.zeros((64, 288), F32) for _ in range(3)]
    for y in range(4):
        pre = jnp.zeros((64, 128), F32)
        for i in range(3):
            pre = pre + dot(w3[i], rows_at(t3, i, y + 1))
        coarse_o[y] = silu(pre).astype(BF)
        grad = cot[y].astype(F32) * slope(pre)
        cgrad_o[y] = grad.astype(BF)
        mine = jnp.where(own > 0.5, grad, 0.0).astype(BF)
        for i in range(3):
            raw[i] = raw[i] + dot_lanes(mine, rows_at(t3, i, y + 1))
    for i in range(3):
        craw_o[i * 64 : (i + 1) * 64] = raw[i]


def backward_kernel(
    sizes, offs, cgrad, spre, fpre, cot, t1, t2, w3, w2, w1, spread,
    vgrad_o, sraw_o, fraw_o,
    t4, acc4, t5, own5, acc5, t6, own6,
):
    nx, ny, nz = sizes
    ox, oy, oz = offs[0], offs[1], offs[2]
    fine_ok = lane_mask(LANES, oz - 8, 0, nz)
    own_ok = lane_mask(LANES, 0, 8, 136)

    for x in range(5):
        for y in range(8):
            store_taps(t4, (x, y), cgrad[x, y].astype(F32))
    clear(acc4)
    spread_conv(acc4, w3, t4, (0, 5), (1, 7), 32, 2)

    own5[0] = jnp.zeros(own5.shape[1:], BF)
    own5[1] = jnp.zeros(own5.shape[1:], BF)
    own5[4] = jnp.zeros(own5.shape[1:], BF)
    own5[5] = jnp.zeros(own5.shape[1:], BF)
    own6[0] = jnp.zeros(own6.shape[1:], BF)
    own6[1] = jnp.zeros(own6.shape[1:], BF)
    own6[4] = jnp.zeros(own6.shape[1:], BF)
    own6[5] = jnp.zeros(own6.shape[1:], BF)
    matrix = spread[...]

    def second(n, carry):
        for cy in range(6):
            value = acc4[n + 2, cy + 1]
            high = value.astype(BF)
            low = (value - high.astype(F32)).astype(BF)
            wide = dot(high, matrix) + dot(low, matrix)
            for dx in range(2):
                for dy in range(2):
                    x, y = 2 * n + dx, 2 * cy + dy
                    grad = (cot[x, y].astype(F32) + wide) * slope(spre[x, y])
                    grad = keep(grad, fine_ok, (ox + x - 2, nx), (oy + y - 2, ny))
                    store_taps(t5, (x, y), grad.astype(BF).astype(F32))
        return carry

    lax.fori_loop(0, 3, second, 0)
    for x in range(2):
        for y in range(8):
            mine = t5[x + 2, y + 2, 32:64].astype(F32)
            own5[x + 2, y] = jnp.where(own_ok > 0.5, mine, 0.0).astype(BF)

    clear(acc5)
    spread_conv(acc5, w2, t5, (0, 6), (1, 11), 32, 2)

    def first(n, carry):
        for y in range(10):
            grad = acc5[n + 2, y + 1] * slope(fpre[n, y])
            grad = keep(grad, fine_ok, (ox + n - 1, nx), (oy + y - 1, ny))
            store_taps(t6, (n, y), grad.astype(BF).astype(F32))
        return carry

    lax.fori_loop(0, 4, first, 0)
    for x in range(2):
        for y in range(8):
            mine = t6[x + 1, y + 1, 32:64].astype(F32)
            own6[x + 2, y] = jnp.where(own_ok > 0.5, mine, 0.0).astype(BF)

    sraw_o[...] = jnp.zeros(sraw_o.shape, F32)
    fraw_o[...] = jnp.zeros(fraw_o.shape, F32)

    def weight_grads(n, carry):
        second_sum = jnp.zeros(sraw_o.shape, F32)
        first_sum = jnp.zeros(fraw_o.shape, F32)
        for y in range(8):
            left = jnp.concatenate([own5[n + 2, y], own5[n + 1, y], own5[n, y]], axis=0)
            second_sum = second_sum + dot_lanes(left, rows_at(t2, n, y + 1))
            left = jnp.concatenate([own6[n + 2, y], own6[n + 1, y], own6[n, y]], axis=0)
            first_sum = first_sum + dot_lanes(left, rows_at(t1, n, y + 1))
        sraw_o[...] += second_sum
        fraw_o[...] += first_sum
        return carry

    lax.fori_loop(0, 4, weight_grads, 0)

    for x in range(2):
        for y in range(8):
            total = jnp.zeros((16, LANES), F32)
            for i in range(3):
                total = total + dot(w1[i], rows_at(t6, x + i, y + 1))
            vgrad_o[x, y] = pltpu.roll(total, LANES - 8, 1)[:, :128].astype(BF)


def flipped(weight):
    return jnp.transpose(weight[:, ::-1, ::-1, ::-1, :], (4, 1, 2, 3, 0))


def stacked(weight):
    outputs, chans = weight.shape[0], weight.shape[4]
    return jnp.transpose(weight, (1, 0, 2, 3, 4)).reshape(3, outputs, 9 * chans)


def swap(blocks, axes):
    return lax.all_to_all(blocks, axes, split_axis=0, concat_axis=0, tiled=True)


def added(blocks):
    return lax.optimization_barrier(jnp.sum(blocks.astype(F32), axis=0)).astype(BF)


def total_over_mesh(rows):
    plane = ("gy", "gz")
    count = lax.axis_size("gy") * lax.axis_size("gz")
    line = lax.axis_size("gx")
    share = -(-rows.shape[0] // (8 * count)) * 8
    rows = jnp.pad(rows.astype(BF), ((0, share * count - rows.shape[0]), (0, 0)))
    part = added(swap(rows.reshape(count, share, 128), plane))
    part = added(swap(jnp.broadcast_to(part, (line, share, 128)), "gx"))
    whole = swap(jnp.broadcast_to(part, (count, share, 128)), plane)
    return whole.reshape(count * share, 128).astype(F32)


def grads_over_mesh(first_raw, second_raw, coarse_raw):
    wide = jnp.concatenate([coarse_raw, second_raw], axis=0)
    height = wide.shape[0]
    piece = height // 4
    rest = jnp.concatenate(
        [wide[n * piece : (n + 1) * piece, 256:288] for n in range(4)], axis=1
    )
    thin = first_raw.reshape(96, 9, 16)[:, :, :4].reshape(96, 36)
    rows = jnp.concatenate(
        [wide[:, :128], wide[:, 128:256], rest, jnp.pad(thin, ((0, 0), (0, 92)))], axis=0
    )
    rows = total_over_mesh(rows)
    rest = rows[2 * height : 2 * height + piece]
    rest = jnp.concatenate([rest[:, 32 * n : 32 * n + 32] for n in range(4)], axis=0)
    wide = jnp.concatenate([rows[:height], rows[height : 2 * height], rest], axis=1)
    thin = rows[2 * height + piece : 2 * height + piece + 96, :36]
    return thin, wide[192:], wide[:192]


def weight_form(matrix, outputs, chans):
    return jnp.transpose(matrix.reshape(3, outputs, 3, 3, chans), (1, 0, 2, 3, 4))


def shape(dims, dtype):
    return jax.ShapeDtypeStruct(dims, dtype)


def local(volume, w_first, w_second, w_coarse, skip_cotangent, coarse_cotangent):
    counts = [lax.axis_size(axis) for axis in AXES]
    extents = volume.shape[1:]
    sizes = tuple(count * extent for count, extent in zip(counts, extents))
    offs = jnp.stack([lax.axis_index(axis) * extent for axis, extent in zip(AXES, extents)])
    offs = offs.astype(jnp.int32)

    wide_volume = halo(halo(halo(volume, "gx", 1, 4), "gy", 2, 4), "gz", 3, 8)
    wide_volume = jnp.pad(
        jnp.transpose(wide_volume, (1, 2, 0, 3)), ((0, 0), (0, 0), (0, 12), (0, LANES - 144))
    )
    sides = counts[2]
    depth = coarse_cotangent.shape[3] // sides
    guarded = jnp.pad(coarse_cotangent[:, 0], ((0, 0), (0, 0), (2, 2)))
    sent = jnp.stack([guarded[..., n * depth : n * depth + depth + 4] for n in range(sides)])
    returned = swap(sent, "gz")
    returned = jnp.transpose(returned, (2, 0, 1, 3)).reshape(4, 64, depth + 4)
    returned = jnp.pad(returned, ((0, 0), (0, 0), (2, 128 - 70)))
    rows_cotangent = jnp.transpose(skip_cotangent, (1, 2, 0, 3))
    wide_cotangent = halo(halo(halo(rows_cotangent, "gx", 0, 2), "gy", 1, 2), "gz", 3, 2)
    wide_cotangent = jnp.pad(wide_cotangent, ((0, 0), (0, 0), (0, 0), (6, LANES - 138)))

    fine_place = lax.broadcasted_iota(jnp.int32, (LANES, 128), 0)
    coarse_place = lax.broadcasted_iota(jnp.int32, (LANES, 128), 1)
    pool = jnp.where(fine_place // 2 == coarse_place, 1.0, 0.0).astype(BF)
    spread = jnp.transpose(pool) * 0.125

    thin_first = jnp.pad(w_first, ((0, 0), (0, 0), (0, 0), (0, 0), (0, 12)))
    smem = pl.BlockSpec(memory_space=pltpu.SMEM)
    vmem = pl.BlockSpec(memory_space=pltpu.VMEM)
    skip, coarse_local, coarse_grad, coarse_raw, first_pre, second_pre, taps1, taps2 = (
        pl.pallas_call(
            lambda *refs: forward_kernel(sizes, *refs),
            out_shape=(
                shape((2, 8, 32, 128), BF),
                shape((4, 64, 128), BF),
                shape((4, 64, 128), BF),
                shape((192, 288), F32),
                shape((4, 10, 32, LANES), F32),
                shape((6, 12, 32, LANES), F32),
                shape((4, 10, 48, LANES), BF),
                shape((4, 10, 96, LANES), BF),
            ),
            in_specs=[smem] + [vmem] * 6,
            out_specs=(vmem,) * 8,
            scratch_shapes=[
                pltpu.VMEM((10, 16, 48, LANES), BF),
                pltpu.VMEM((12, 16, 32, LANES), F32),
                pltpu.VMEM((10, 16, 96, LANES), BF),
                pltpu.VMEM((12, 16, 32, LANES), F32),
                pltpu.VMEM((6, 12, 32, LANES), BF),
                pltpu.VMEM((3, 6, 96, 128), BF),
            ],
            compiler_params=pltpu.CompilerParams(vmem_limit_bytes=52 * 2**20),
            cost_estimate=pl.CostEstimate(
                flops=4 * 10**9, bytes_accessed=12 * 10**6, transcendentals=10**6
            ),
            name="forward",
        )(
            offs,
            wide_volume,
            stacked(thin_first).reshape(96, 144),
            stacked(w_second).reshape(96, 288),
            stacked(w_coarse),
            returned,
            pool,
        )
    )
    coarse = coarse_local[:, :, 4 : 4 + depth].reshape(4, sides, 64 // sides, depth)
    coarse = swap(jnp.transpose(coarse, (1, 2, 0, 3)), "gz")
    coarse = jnp.transpose(coarse, (1, 2, 0, 3)).reshape(64 // sides, 1, 4, sides * depth)

    wide_grad = halo(halo(coarse_grad[None], "gx", 0, 2), "gy", 1, 2)
    back_first = jnp.pad(flipped(w_first), ((0, 12),) + ((0, 0),) * 4)
    volume_grad, second_raw, first_raw = pl.pallas_call(
        lambda *refs: backward_kernel(sizes, *refs),
        out_shape=(
            shape((2, 8, 16, 128), BF),
            shape((96, 288), F32),
            shape((96, 144), F32),
        ),
        in_specs=[smem] + [vmem] * 10,
        out_specs=(vmem,) * 3,
        scratch_shapes=[
            pltpu.VMEM((5, 8, 192, 128), BF),
            pltpu.VMEM((7, 8, 32, 128), F32),
            pltpu.VMEM((6, 12, 96, LANES), BF),
            pltpu.VMEM((6, 8, 32, LANES), BF),
            pltpu.VMEM((8, 12, 32, LANES), F32),
            pltpu.VMEM((4, 10, 96, LANES), BF),
            pltpu.VMEM((6, 8, 32, LANES), BF),
        ],
        compiler_params=pltpu.CompilerParams(vmem_limit_bytes=52 * 2**20),
        cost_estimate=pl.CostEstimate(
            flops=2 * 10**9, bytes_accessed=10 * 10**6, transcendentals=10**6
        ),
        name="backward",
    )(
        offs,
        wide_grad,
        second_pre,
        first_pre,
        wide_cotangent,
        taps1,
        taps2,
        stacked(flipped(w_coarse)).reshape(96, 576),
        stacked(flipped(w_second)).reshape(96, 288),
        stacked(back_first),
        spread,
    )

    skip = jnp.transpose(skip, (2, 0, 1, 3))
    volume_grad = jnp.transpose(volume_grad[:, :, :4], (2, 0, 1, 3))
    factor = 1.0 / math.sqrt(sizes[0] * sizes[1] * sizes[2])
    thin, second, wide = grads_over_mesh(first_raw, second_raw, coarse_raw)
    return (
        skip,
        coarse,
        volume_grad,
        weight_form(thin * factor, 32, 4),
        weight_form(second * factor, 32, 32),
        weight_form(wide * factor, 64, 32),
    )


def solution(mesh):
    in_specs = (
        P(None, "gx", "gy", "gz"),
        P(),
        P(),
        P(),
        P(None, "gx", "gy", "gz"),
        P("gz", "gx", "gy", None),
    )
    out_specs = (
        P(None, "gx", "gy", "gz"),
        P("gz", "gx", "gy", None),
        P(None, "gx", "gy", "gz"),
        P(),
        P(),
        P(),
    )
    return jax.shard_map(local, mesh=mesh, in_specs=in_specs, out_specs=out_specs, check_vma=False)
```

profile of v0, /device:TPU:1, one launch (start us, length us, event | category | flops | bytes accessed | tf_op | source)
XLA Modules:
  0.0 216.2 jit_solution(370855694369056965)
XLA Ops:
  4.0 12.1 %collective-permute-start.1 = (bf16[4,2,8,128]{3,0,2,1:T(4,128)(2,1)S(1)}, bf16[4,2,8,128]{3,0,2,1:T(4,128)(2,1)S(1)}, u32[]{:S(2)}, u32[]{:S(2)}) collective-permute-start(bf16[4,2,8,128]{3,0,2,1:T(4,128)(2,1)S(1)} %copy.173), channel_id=1, source_target_pairs={{0,32},{32,64},{64,96},{96,128},{128,160},{160,192},{192,224},{224... | collective-permute-start | bytes 49160 | tf_op jit(solution)/shard_map/ppermute | solution.py:19
  16.1 4.0 %collective-permute-start = (bf16[4,2,8,128]{3,0,2,1:T(4,128)(2,1)S(1)}, bf16[4,2,8,128]{3,0,2,1:T(4,128)(2,1)S(1)}, u32[]{:S(2)}, u32[]{:S(2)}) collective-permute-start(bf16[4,2,8,128]{3,0,2,1:T(4,128)(2,1)S(1)} %copy.173), channel_id=1, source_target_pairs={{0,64},{32,96},{64,128},{96,160},{128,192},{160,224},{192,256},{22... | collective-permute-start | bytes 49160 | tf_op jit(solution)/shard_map/ppermute | solution.py:19
  21.8 4.3 %all-to-all-start = ((bf16[4,16,4,68]{3,2,1,0:T(4,128)(2,1)}), bf16[4,16,4,68]{3,2,1,0:T(4,128)(2,1)S(1)}, u32[]{:S(2)}, u32[]{:S(2)}) async-start(bf16[4,16,4,68]{3,2,1,0:T(4,128)(2,1)} %pad_maximum_fusion.10), calls=%async_computation | async-start | bytes 131072 | tf_op jit(solution)/shard_map/all_to_all | solution.py:275
  27.1 1.3 collective-permute-start.15
  32.1 8.8 %collective-permute-start.14 = (bf16[2,8,32,128]{3,2,1,0:T(8,128)(2,1)S(1)}, bf16[2,8,32,128]{3,2,1,0:T(8,128)(2,1)S(1)}, u32[]{:S(2)}, u32[]{:S(2)}) collective-permute-start(bf16[2,8,32,128]{3,2,1,0:T(8,128)(2,1)S(1)} %bitcast.75), channel_id=1, source_target_pairs={{0,32},{32,64},{64,96},{96,128},{128,160},{160,192},{192,224},{224... | collective-permute-start | bytes 393224 | tf_op jit(solution)/shard_map/ppermute | solution.py:19
  41.0 5.4 %collective-permute-start.4 = (bf16[4,10,4,128]{3,0,2,1:T(4,128)(2,1)S(1)}, bf16[4,10,4,128]{3,0,2,1:T(4,128)(2,1)S(1)}, u32[]{:S(2)}, u32[]{:S(2)}) collective-permute-start(bf16[4,10,4,128]{3,0,2,1:T(4,128)(2,1)S(1)} %get-tuple-element.90), channel_id=1, source_target_pairs={{0,4},{4,8},{8,12},{12,16},{16,20},{20,24},{24,28},{1,5},{5,9},{9,... | collective-permute-start | bytes 122888 | tf_op jit(solution)/shard_map/ppermute | solution.py:19
  46.4 1.9 collective-permute-start.5
  48.4 3.3 %collective-permute-done.5 = bf16[4,10,4,128]{3,0,2,1:T(4,128)(2,1)S(1)} collective-permute-done((bf16[4,10,4,128]{3,0,2,1:T(4,128)(2,1)S(1)}, bf16[4,10,4,128]{3,0,2,1:T(4,128)(2,1)S(1)}, u32[]{:S(2)}, u32[]{:S(2)}) %collective-permute-start.5) | collective-permute-done | bytes 40992 | tf_op jit(solution)/shard_map/ppermute | solution.py:19
  52.0 3.7 %collective-permute-start.6 = (bf16[4,10,16,8]{3,0,2,1:T(4,128)(2,1)S(1)}, bf16[4,10,16,8]{3,0,2,1:T(4,128)(2,1)S(1)}, u32[]{:S(2)}, u32[]{:S(2)}) collective-permute-start(bf16[4,10,16,8]{3,0,2,1:T(4,128)(2,1)S(1)} %get-tuple-element.84), channel_id=1, source_target_pairs={{0,1},{1,2},{2,3},{4,5},{5,6},{6,7},{8,9},{9,10},{10,11},{12,13},{... | collective-permute-start | bytes 30728 | tf_op jit(solution)/shard_map/ppermute | solution.py:19
  55.7 1.3 collective-permute-start.7
  59.0 3.0 %collective-permute-done.7 = bf16[4,10,16,8]{3,0,2,1:T(4,128)(2,1)S(1)} collective-permute-done((bf16[4,10,16,8]{3,0,2,1:T(4,128)(2,1)S(1)}, bf16[4,10,16,8]{3,0,2,1:T(4,128)(2,1)S(1)}, u32[]{:S(2)}, u32[]{:S(2)}) %collective-permute-start.7) | collective-permute-done | bytes 10272 | tf_op jit(solution)/shard_map/ppermute | solution.py:19
  63.8 17.8 %forward.1 = (bf16[2,8,32,128]{3,2,1,0:T(8,128)(2,1)S(1)}, bf16[4,64,128]{2,1,0:T(8,128)(2,1)S(1)}, bf16[4,64,128]{2,1,0:T(8,128)(2,1)S(1)}, f32[192,288]{1,0:T(...) custom-call(s32[3]{0:T(128)S(1)} %pad_add_fusion.refs_0_, ...), custom_call_target="tpu_custom_call" | custom-call | flops 4000000000 | bytes 12000000 | tf_op jit(solution)/shard_map/forward/pallas_call | solution.py:352
  82.9 1.3 collective-permute-start.10
  84.2 9.1 %collective-permute-start.9 = (bf16[1,4,64,128]{3,2,1,0:T(8,128)(2,1)S(1)}, bf16[1,4,64,128]{3,2,1,0:T(8,128)(2,1)S(1)}, u32[]{:S(2)}, u32[]{:S(2)}) collective-permute-start(bf16[1,4,64,128]{3,2,1,0:T(8,128)(2,1)S(1)} %bitcast.70), channel_id=1, source_target_pairs={{0,32},{32,64},{64,96},{96,128},{128,160},{160,192},{192,224},{224... | collective-permute-start | bytes 196616 | tf_op jit(solution)/shard_map/ppermute | solution.py:19
  93.3 4.0 %collective-permute-start.8 = (bf16[1,4,64,128]{3,2,1,0:T(8,128)(2,1)S(1)}, bf16[1,4,64,128]{3,2,1,0:T(8,128)(2,1)S(1)}, u32[]{:S(2)}, u32[]{:S(2)}) collective-permute-start(bf16[1,4,64,128]{3,2,1,0:T(8,128)(2,1)S(1)} %bitcast.71), channel_id=1, source_target_pairs={{0,64},{32,96},{64,128},{96,160},{128,192},{160,224},{192,256},{22... | collective-permute-start | bytes 196616 | tf_op jit(solution)/shard_map/ppermute | solution.py:19
  97.3 5.4 %collective-permute-start.16 = (bf16[6,2,32,128]{3,2,1,0:T(8,128)(2,1)S(1)}, bf16[6,2,32,128]{3,2,1,0:T(8,128)(2,1)S(1)}, u32[]{:S(2)}, u32[]{:S(2)}) collective-permute-start(bf16[6,2,32,128]{3,2,1,0:T(8,128)(2,1)S(1)} %get-tuple-element.76), channel_id=1, source_target_pairs={{0,4},{4,8},{8,12},{12,16},{16,20},{20,24},{24,28},{1,5},{5,9},{9,... | collective-permute-start | bytes 294920 | tf_op jit(solution)/shard_map/ppermute | solution.py:19
  102.7 1.9 collective-permute-start.17
  104.8 3.9 %collective-permute-done.17 = bf16[6,2,32,128]{3,2,1,0:T(8,128)(2,1)S(1)} collective-permute-done((bf16[6,2,32,128]{3,2,1,0:T(8,128)(2,1)S(1)}, bf16[6,2,32,128]{3,2,1,0:T(8,128)(2,1)S(1)}, u32[]{:S(2)}, u32[]{:S(2)}) %collective-permute-start.17) | collective-permute-done | bytes 98336 | tf_op jit(solution)/shard_map/ppermute | solution.py:19
  110.0 1.3 collective-permute-start.19
  111.3 4.0 %collective-permute-start.18 = (bf16[6,12,32,2]{2,3,1,0:T(2,128)(2,1)S(1)}, bf16[6,12,32,2]{2,3,1,0:T(2,128)(2,1)S(1)}, u32[]{:S(2)}, u32[]{:S(2)}) collective-permute-start(bf16[6,12,32,2]{2,3,1,0:T(2,128)(2,1)S(1)} %copy.186), channel_id=1, source_target_pairs={{0,1},{1,2},{2,3},{4,5},{5,6},{6,7},{8,9},{9,10},{10,11},{12,13},{... | collective-permute-start | bytes 27656 | tf_op jit(solution)/shard_map/ppermute | solution.py:19
  116.0 2.4 %collective-permute-start.12 = (bf16[5,2,64,128]{3,2,1,0:T(8,128)(2,1)}, bf16[5,2,64,128]{3,2,1,0:T(8,128)(2,1)S(1)}, u32[]{:S(2)}, u32[]{:S(2)}) collective-permute-start(bf16[5,2,64,128]{3,2,1,0:T(8,128)(2,1)} %get-tuple-element.78), channel_id=1, source_target_pairs={{0,4},{4,8},{8,12},{12,16},{16,20},{20,24},{24,28},{1,5},{5,9},{9,... | collective-permute-start | bytes 491528 | tf_op jit(solution)/shard_map/ppermute | solution.py:19
  118.4 2.1 collective-permute-start.13
  121.6 2.7 %select_maximum_fusion.refs_4_ = bf16[6,12,32,256]{3,2,1,0:T(8,128)(2,1)} fusion(bf16[6,12,32,2]{3,2,1,0:T(8,128)(2,1)S(1)} %copy.189, bf16[6,12,32,2]{3,2,1,0:T(8,128)(2,1)S(1)} %copy.188, bf16[6,2,32,128]{3,2,1,0:T(8,128)(2,1)S(1)} %collective-permute-done.17, bf16[6,2,32,128]{3,2,1,0:T(8,128)(2,1)S(1)} %collective-permute-done.16, ...), kind=kLoop, calls=%fused_computation.3 | loop fusion | flops 14155776 | bytes 1787904 | tf_op jit(solution)/shard_map/concatenate | solution.py:31
  126.1 15.8 %backward.1 = (bf16[2,8,16,128]{3,2,1,0:T(8,128)(2,1)S(1)}, f32[96,288]{1,0:T(8,128)S(1)}, f32[96,144]{1,0:T(8,128)S(1)}) custom-call(s32[3]{0:T(128)S(1)} %pad_add_fusion.refs_0_, bf16[5,8,64,128]{3,2,1,0:T(8,128)(2,1)S(1)} %pad_maximum_fusion.refs_1_, f32[6,12,32,256]{3,2,1,0:T(8,128)} %get-tuple-element.20.refs_2_, ...), custom_call_target="tpu_custom_call" | custom-call | flops 2000000000 | bytes 10000000 | tf_op jit(solution)/shard_map/backward/pallas_call | solution.py:395
  143.1 6.3 %all-to-all-start.2 = ((bf16[32,24,128]{2,1,0:T(8,128)(2,1)}), bf16[32,24,128]{2,1,0:T(8,128)(2,1)S(1)}, u32[]{:S(2)}, u32[]{:S(2)}) async-start(bf16[32,24,128]{2,1,0:T(8,128)(2,1)} %bitcast.27), calls=%async_computation.2 | async-start | bytes 393216 | tf_op jit(solution)/shard_map/all_to_all | solution.py:275
  150.3 9.1 %all-to-all-done.2 = bf16[32,24,128]{2,1,0:T(8,128)(2,1)S(1)} async-done(((bf16[32,24,128]{2,1,0:T(8,128)(2,1)}), bf16[32,24,128]{2,1,0:T(8,128)(2,1)S(1)}, u32[]{:S(2)}, u32[]{:S(2)}) %all-to-all-start.2) | async-done | bytes 196640 | tf_op jit(solution)/shard_map/all_to_all | solution.py:275
  159.3 3.3 %all-to-all-start.1 = ((bf16[4,2,2048]{2,1,0:T(2,128)(2,1)}), bf16[4,2,2048]{2,1,0:T(2,128)(2,1)S(1)}, u32[]{:S(2)}, u32[]{:S(2)}) async-start(bf16[4,2,2048]{2,1,0:T(2,128)(2,1)} %reshape.63), calls=%async_computation.1 | async-start | bytes 65536 | tf_op jit(solution)/shard_map/all_to_all | solution.py:275
  162.7 4.5 %all-to-all-done.1 = bf16[4,2,2048]{2,1,0:T(2,128)(2,1)S(1)} async-done(((bf16[4,2,2048]{2,1,0:T(2,128)(2,1)}), bf16[4,2,2048]{2,1,0:T(2,128)(2,1)S(1)}, u32[]{:S(2)}, u32[]{:S(2)}) %all-to-all-start.1) | async-done | bytes 32800 | tf_op jit(solution)/shard_map/all_to_all | solution.py:275
  167.8 15.8 %all-to-all-start.3 = ((bf16[16,24,128]{2,1,0:T(8,128)(2,1)}), bf16[16,24,128]{2,1,0:T(8,128)(2,1)S(1)}, u32[]{:S(2)}, u32[]{:S(2)}) async-start(bf16[16,24,128]{2,1,0:T(8,128)(2,1)} %broadcast_in_dim.26), calls=%async_computation.3 | async-start | bytes 196608 | tf_op jit(solution)/shard_map/all_to_all | solution.py:275
  184.4 11.3 %all-to-all-done.3 = bf16[16,24,128]{2,1,0:T(8,128)(2,1)S(1)} async-done(((bf16[16,24,128]{2,1,0:T(8,128)(2,1)}), bf16[16,24,128]{2,1,0:T(8,128)(2,1)S(1)}, u32[]{:S(2)}, u32[]{:S(2)}) %all-to-all-start.3) | async-done | bytes 98336 | tf_op jit(solution)/shard_map/all_to_all | solution.py:275
  196.5 6.4 %all-to-all-start.4 = ((bf16[32,24,128]{2,1,0:T(8,128)(2,1)}), bf16[32,24,128]{2,1,0:T(8,128)(2,1)S(1)}, u32[]{:S(2)}, u32[]{:S(2)}) async-start(bf16[32,24,128]{2,1,0:T(8,128)(2,1)} %broadcast_in_dim.27), calls=%async_computation.4 | async-start | bytes 393216 | tf_op jit(solution)/shard_map/all_to_all | solution.py:275
  204.3 8.6 %all-to-all-done.4 = bf16[32,24,128]{2,1,0:T(8,128)(2,1)S(1)} async-done(((bf16[32,24,128]{2,1,0:T(8,128)(2,1)}), bf16[32,24,128]{2,1,0:T(8,128)(2,1)S(1)}, u32[]{:S(2)}, u32[]{:S(2)}) %all-to-all-start.4) | async-done | bytes 196640 | tf_op jit(solution)/shard_map/all_to_all | solution.py:275
  (122 shorter events, 28.8 us)
Async XLA Ops:
  0.6 40.3 %copy-start.3 = (bf16[4,2,8,128]{3,2,1,0:T(8,128)(2,1)S(1)}, bf16[4,2,8,128]{3,2,1,0:T(8,128)(2,1)}, u32[]{:S(2)}) copy-start(bf16[4,2,8,128]{3,2,1,0:T(8,128)(2,1)} %param.6) | copy-start | bytes 49156
  1.4 39.5 %collective-permute-start.2 = (bf16[4,2,8,128]{3,0,2,1:T(4,128)(2,1)S(1)}, bf16[4,2,8,128]{3,0,2,1:T(4,128)(2,1)S(1)}, u32[]{:S(2)}, u32[]{:S(2)}) collective-permute-start(bf16[4,2,8,128]{3,0,2,1:T(4,128)(2,1)S(1)} %copy.173), channel_id=1, source_target_pairs={{32,0},{64,32},{96,64},{128,96},{160,128},{192,160},{224,192},{256... | collective-permute-start | bytes 49160 | tf_op jit(solution)/shard_map/ppermute | solution.py:19
  2.7 38.3 %collective-permute-start.3 = (bf16[4,2,8,128]{3,0,2,1:T(4,128)(2,1)S(1)}, bf16[4,2,8,128]{3,0,2,1:T(4,128)(2,1)S(1)}, u32[]{:S(2)}, u32[]{:S(2)}) collective-permute-start(bf16[4,2,8,128]{3,0,2,1:T(4,128)(2,1)S(1)} %copy.173), channel_id=1, source_target_pairs={{64,0},{96,32},{128,64},{160,96},{192,128},{224,160},{256,192},{28... | collective-permute-start | bytes 49160 | tf_op jit(solution)/shard_map/ppermute | solution.py:19
  4.0 36.9 %collective-permute-start.1 = (bf16[4,2,8,128]{3,0,2,1:T(4,128)(2,1)S(1)}, bf16[4,2,8,128]{3,0,2,1:T(4,128)(2,1)S(1)}, u32[]{:S(2)}, u32[]{:S(2)}) collective-permute-start(bf16[4,2,8,128]{3,0,2,1:T(4,128)(2,1)S(1)} %copy.173), channel_id=1, source_target_pairs={{0,32},{32,64},{64,96},{96,128},{128,160},{160,192},{192,224},{224... | collective-permute-start | bytes 49160 | tf_op jit(solution)/shard_map/ppermute | solution.py:19
  16.1 15.9 %collective-permute-start = (bf16[4,2,8,128]{3,0,2,1:T(4,128)(2,1)S(1)}, bf16[4,2,8,128]{3,0,2,1:T(4,128)(2,1)S(1)}, u32[]{:S(2)}, u32[]{:S(2)}) collective-permute-start(bf16[4,2,8,128]{3,0,2,1:T(4,128)(2,1)S(1)} %copy.173), channel_id=1, source_target_pairs={{0,64},{32,96},{64,128},{96,160},{128,192},{160,224},{192,256},{22... | collective-permute-start | bytes 49160 | tf_op jit(solution)/shard_map/ppermute | solution.py:19
  21.8 37.1 %all-to-all-start = ((bf16[4,16,4,68]{3,2,1,0:T(4,128)(2,1)}), bf16[4,16,4,68]{3,2,1,0:T(4,128)(2,1)S(1)}, u32[]{:S(2)}, u32[]{:S(2)}) async-start(bf16[4,16,4,68]{3,2,1,0:T(4,128)(2,1)} %pad_maximum_fusion.10), calls=%async_computation | async-start | bytes 131072 | tf_op jit(solution)/shard_map/all_to_all | solution.py:275
  26.1 31.5 %copy-start.1 = (bf16[64,3,3,3,32]{0,4,3,2,1:T(8,128)(2,1)S(1)}, bf16[64,3,3,3,32]{0,4,3,2,1:T(8,128)(2,1)}, u32[]{:S(2)}) copy-start(bf16[64,3,3,3,32]{0,4,3,2,1:T(8,128)(2,1)} %param.9) | copy-start | bytes 331780
  27.1 66.2 %collective-permute-start.15 = (bf16[2,8,32,128]{3,2,1,0:T(8,128)(2,1)S(1)}, bf16[2,8,32,128]{3,2,1,0:T(8,128)(2,1)S(1)}, u32[]{:S(2)}, u32[]{:S(2)}) collective-permute-start(bf16[2,8,32,128]{3,2,1,0:T(8,128)(2,1)S(1)} %bitcast.74), channel_id=1, source_target_pairs={{32,0},{64,32},{96,64},{128,96},{160,128},{192,160},{224,192},{256... | collective-permute-start | bytes 393224 | tf_op jit(solution)/shard_map/ppermute | solution.py:19
  32.1 65.2 %collective-permute-start.14 = (bf16[2,8,32,128]{3,2,1,0:T(8,128)(2,1)S(1)}, bf16[2,8,32,128]{3,2,1,0:T(8,128)(2,1)S(1)}, u32[]{:S(2)}, u32[]{:S(2)}) collective-permute-start(bf16[2,8,32,128]{3,2,1,0:T(8,128)(2,1)S(1)} %bitcast.75), channel_id=1, source_target_pairs={{0,32},{32,64},{64,96},{96,128},{128,160},{160,192},{192,224},{224... | collective-permute-start | bytes 393224 | tf_op jit(solution)/shard_map/ppermute | solution.py:19
  41.0 7.3 %collective-permute-start.4 = (bf16[4,10,4,128]{3,0,2,1:T(4,128)(2,1)S(1)}, bf16[4,10,4,128]{3,0,2,1:T(4,128)(2,1)S(1)}, u32[]{:S(2)}, u32[]{:S(2)}) collective-permute-start(bf16[4,10,4,128]{3,0,2,1:T(4,128)(2,1)S(1)} %get-tuple-element.90), channel_id=1, source_target_pairs={{0,4},{4,8},{8,12},{12,16},{16,20},{20,24},{24,28},{1,5},{5,9},{9,... | collective-permute-start | bytes 122888 | tf_op jit(solution)/shard_map/ppermute | solution.py:19
  46.4 5.3 %collective-permute-start.5 = (bf16[4,10,4,128]{3,0,2,1:T(4,128)(2,1)S(1)}, bf16[4,10,4,128]{3,0,2,1:T(4,128)(2,1)S(1)}, u32[]{:S(2)}, u32[]{:S(2)}) collective-permute-start(bf16[4,10,4,128]{3,0,2,1:T(4,128)(2,1)S(1)} %get-tuple-element.91), channel_id=1, source_target_pairs={{4,0},{8,4},{12,8},{16,12},{20,16},{24,20},{28,24},{5,1},{9,5},{13... | collective-permute-start | bytes 122888 | tf_op jit(solution)/shard_map/ppermute | solution.py:19
  51.9 6.7 %copy-start.2 = (bf16[32,3,3,3,32]{4,0,3,2,1:T(8,128)(2,1)S(1)}, bf16[32,3,3,3,32]{4,0,3,2,1:T(8,128)(2,1)}, u32[]{:S(2)}) copy-start(bf16[32,3,3,3,32]{4,0,3,2,1:T(8,128)(2,1)} %param.8) | copy-start | bytes 165892
  52.0 7.0 %collective-permute-start.6 = (bf16[4,10,16,8]{3,0,2,1:T(4,128)(2,1)S(1)}, bf16[4,10,16,8]{3,0,2,1:T(4,128)(2,1)S(1)}, u32[]{:S(2)}, u32[]{:S(2)}) collective-permute-start(bf16[4,10,16,8]{3,0,2,1:T(4,128)(2,1)S(1)} %get-tuple-element.84), channel_id=1, source_target_pairs={{0,1},{1,2},{2,3},{4,5},{5,6},{6,7},{8,9},{9,10},{10,11},{12,13},{... | collective-permute-start | bytes 30728 | tf_op jit(solution)/shard_map/ppermute | solution.py:19
  55.7 6.4 %collective-permute-start.7 = (bf16[4,10,16,8]{3,0,2,1:T(4,128)(2,1)S(1)}, bf16[4,10,16,8]{3,0,2,1:T(4,128)(2,1)S(1)}, u32[]{:S(2)}, u32[]{:S(2)}) collective-permute-start(bf16[4,10,16,8]{3,0,2,1:T(4,128)(2,1)S(1)} %get-tuple-element.85), channel_id=1, source_target_pairs={{1,0},{2,1},{3,2},{5,4},{6,5},{7,6},{9,8},{10,9},{11,10},{13,12},{... | collective-permute-start | bytes 30728 | tf_op jit(solution)/shard_map/ppermute | solution.py:19
  81.6 27.4 %copy-start = (bf16[4,10,48,256]{3,2,1,0:T(8,128)(2,1)}, bf16[4,10,48,256]{3,2,1,0:T(8,128)(2,1)S(1)}, u32[]{:S(2)}) copy-start(bf16[4,10,48,256]{3,2,1,0:T(8,128)(2,1)S(1)} %get-tuple-element.22.refs_5_) | copy-start | bytes 2949124
  81.6 23.1 %collective-permute-start.11 = (bf16[1,4,64,128]{3,2,1,0:T(8,128)(2,1)S(1)}, bf16[1,4,64,128]{3,2,1,0:T(8,128)(2,1)S(1)}, u32[]{:S(2)}, u32[]{:S(2)}) collective-permute-start(bf16[1,4,64,128]{3,2,1,0:T(8,128)(2,1)S(1)} %bitcast.68), channel_id=1, source_target_pairs={{64,0},{96,32},{128,64},{160,96},{192,128},{224,160},{256,192},{28... | collective-permute-start | bytes 196616 | tf_op jit(solution)/shard_map/ppermute | solution.py:19
  82.9 21.8 %collective-permute-start.10 = (bf16[1,4,64,128]{3,2,1,0:T(8,128)(2,1)S(1)}, bf16[1,4,64,128]{3,2,1,0:T(8,128)(2,1)S(1)}, u32[]{:S(2)}, u32[]{:S(2)}) collective-permute-start(bf16[1,4,64,128]{3,2,1,0:T(8,128)(2,1)S(1)} %bitcast.69), channel_id=1, source_target_pairs={{32,0},{64,32},{96,64},{128,96},{160,128},{192,160},{224,192},{256... | collective-permute-start | bytes 196616 | tf_op jit(solution)/shard_map/ppermute | solution.py:19
  84.2 20.5 %collective-permute-start.9 = (bf16[1,4,64,128]{3,2,1,0:T(8,128)(2,1)S(1)}, bf16[1,4,64,128]{3,2,1,0:T(8,128)(2,1)S(1)}, u32[]{:S(2)}, u32[]{:S(2)}) collective-permute-start(bf16[1,4,64,128]{3,2,1,0:T(8,128)(2,1)S(1)} %bitcast.70), channel_id=1, source_target_pairs={{0,32},{32,64},{64,96},{96,128},{128,160},{160,192},{192,224},{224... | collective-permute-start | bytes 196616 | tf_op jit(solution)/shard_map/ppermute | solution.py:19
  93.3 9.4 %collective-permute-start.8 = (bf16[1,4,64,128]{3,2,1,0:T(8,128)(2,1)S(1)}, bf16[1,4,64,128]{3,2,1,0:T(8,128)(2,1)S(1)}, u32[]{:S(2)}, u32[]{:S(2)}) collective-permute-start(bf16[1,4,64,128]{3,2,1,0:T(8,128)(2,1)S(1)} %bitcast.71), channel_id=1, source_target_pairs={{0,64},{32,96},{64,128},{96,160},{128,192},{160,224},{192,256},{22... | collective-permute-start | bytes 196616 | tf_op jit(solution)/shard_map/ppermute | solution.py:19
  97.3 7.4 %collective-permute-start.16 = (bf16[6,2,32,128]{3,2,1,0:T(8,128)(2,1)S(1)}, bf16[6,2,32,128]{3,2,1,0:T(8,128)(2,1)S(1)}, u32[]{:S(2)}, u32[]{:S(2)}) collective-permute-start(bf16[6,2,32,128]{3,2,1,0:T(8,128)(2,1)S(1)} %get-tuple-element.76), channel_id=1, source_target_pairs={{0,4},{4,8},{8,12},{12,16},{16,20},{20,24},{24,28},{1,5},{5,9},{9,... | collective-permute-start | bytes 294920 | tf_op jit(solution)/shard_map/ppermute | solution.py:19
  102.7 5.9 %collective-permute-start.17 = (bf16[6,2,32,128]{3,2,1,0:T(8,128)(2,1)S(1)}, bf16[6,2,32,128]{3,2,1,0:T(8,128)(2,1)S(1)}, u32[]{:S(2)}, u32[]{:S(2)}) collective-permute-start(bf16[6,2,32,128]{3,2,1,0:T(8,128)(2,1)S(1)} %get-tuple-element.77), channel_id=1, source_target_pairs={{4,0},{8,4},{12,8},{16,12},{20,16},{24,20},{28,24},{5,1},{9,5},{13... | collective-permute-start | bytes 294920 | tf_op jit(solution)/shard_map/ppermute | solution.py:19
  110.0 11.1 %collective-permute-start.19 = (bf16[6,12,32,2]{2,3,1,0:T(2,128)(2,1)S(1)}, bf16[6,12,32,2]{2,3,1,0:T(2,128)(2,1)S(1)}, u32[]{:S(2)}, u32[]{:S(2)}) collective-permute-start(bf16[6,12,32,2]{2,3,1,0:T(2,128)(2,1)S(1)} %copy.187), channel_id=1, source_target_pairs={{1,0},{2,1},{3,2},{5,4},{6,5},{7,6},{9,8},{10,9},{11,10},{13,12},{... | collective-permute-start | bytes 27656 | tf_op jit(solution)/shard_map/ppermute | solution.py:19
  111.3 9.2 %collective-permute-start.18 = (bf16[6,12,32,2]{2,3,1,0:T(2,128)(2,1)S(1)}, bf16[6,12,32,2]{2,3,1,0:T(2,128)(2,1)S(1)}, u32[]{:S(2)}, u32[]{:S(2)}) collective-permute-start(bf16[6,12,32,2]{2,3,1,0:T(2,128)(2,1)S(1)} %copy.186), channel_id=1, source_target_pairs={{0,1},{1,2},{2,3},{4,5},{5,6},{6,7},{8,9},{9,10},{10,11},{12,13},{... | collective-permute-start | bytes 27656 | tf_op jit(solution)/shard_map/ppermute | solution.py:19
  116.0 8.4 %collective-permute-start.12 = (bf16[5,2,64,128]{3,2,1,0:T(8,128)(2,1)}, bf16[5,2,64,128]{3,2,1,0:T(8,128)(2,1)S(1)}, u32[]{:S(2)}, u32[]{:S(2)}) collective-permute-start(bf16[5,2,64,128]{3,2,1,0:T(8,128)(2,1)} %get-tuple-element.78), channel_id=1, source_target_pairs={{0,4},{4,8},{8,12},{12,16},{16,20},{20,24},{24,28},{1,5},{5,9},{9,... | collective-permute-start | bytes 491528 | tf_op jit(solution)/shard_map/ppermute | solution.py:19
  118.4 6.7 %collective-permute-start.13 = (bf16[5,2,64,128]{3,2,1,0:T(8,128)(2,1)S(1)}, bf16[5,2,64,128]{3,2,1,0:T(8,128)(2,1)}, u32[]{:S(2)}, u32[]{:S(2)}) collective-permute-start(bf16[5,2,64,128]{3,2,1,0:T(8,128)(2,1)S(1)} %get-tuple-element.79), channel_id=1, source_target_pairs={{4,0},{8,4},{12,8},{16,12},{20,16},{24,20},{28,24},{5,1},{9,5},{13... | collective-permute-start | bytes 491528 | tf_op jit(solution)/shard_map/ppermute | solution.py:19
  143.1 16.2 %all-to-all-start.2 = ((bf16[32,24,128]{2,1,0:T(8,128)(2,1)}), bf16[32,24,128]{2,1,0:T(8,128)(2,1)S(1)}, u32[]{:S(2)}, u32[]{:S(2)}) async-start(bf16[32,24,128]{2,1,0:T(8,128)(2,1)} %bitcast.27), calls=%async_computation.2 | async-start | bytes 393216 | tf_op jit(solution)/shard_map/all_to_all | solution.py:275
  159.3 7.8 %all-to-all-start.1 = ((bf16[4,2,2048]{2,1,0:T(2,128)(2,1)}), bf16[4,2,2048]{2,1,0:T(2,128)(2,1)S(1)}, u32[]{:S(2)}, u32[]{:S(2)}) async-start(bf16[4,2,2048]{2,1,0:T(2,128)(2,1)} %reshape.63), calls=%async_computation.1 | async-start | bytes 65536 | tf_op jit(solution)/shard_map/all_to_all | solution.py:275
  167.8 27.9 %all-to-all-start.3 = ((bf16[16,24,128]{2,1,0:T(8,128)(2,1)}), bf16[16,24,128]{2,1,0:T(8,128)(2,1)S(1)}, u32[]{:S(2)}, u32[]{:S(2)}) async-start(bf16[16,24,128]{2,1,0:T(8,128)(2,1)} %broadcast_in_dim.26), calls=%async_computation.3 | async-start | bytes 196608 | tf_op jit(solution)/shard_map/all_to_all | solution.py:275
  196.5 16.4 %all-to-all-start.4 = ((bf16[32,24,128]{2,1,0:T(8,128)(2,1)}), bf16[32,24,128]{2,1,0:T(8,128)(2,1)S(1)}, u32[]{:S(2)}, u32[]{:S(2)}) async-start(bf16[32,24,128]{2,1,0:T(8,128)(2,1)} %broadcast_in_dim.27), calls=%async_computation.4 | async-start | bytes 393216 | tf_op jit(solution)/shard_map/all_to_all | solution.py:275
where the time goes:
time: 218 us; the launch traced here: 216 us
  starting transfers between devices  110 us (50%)
  waiting for transfers between devices  44.5 us (20%)
  Pallas kernels  33.6 us (15%)
  local copies, waits for them, and re-layouts  21.2 us (10%)
  other arithmetic  5.73 us (3%)
    ppermute x20, starting transfers between devices, shifted(): return lax.ppermute(block, axis, pairs)  73.7 us
    all_to_all x5, starting transfers between devices, swap(): return lax.all_to_all(blocks, axes, split_axis=0, concat_axis=0, tiled=True)  36 us
    all_to_all x5, waiting for transfers between devices, swap(): return lax.all_to_all(blocks, axes, split_axis=0, concat_axis=0, tiled=True)  33.5 us
    pallas_call x1, Pallas kernels, local(): pl.pallas_call(lambda *refs: forward_kernel(sizes, *refs), out_shape=(sha...  17.8 us
    pallas_call x1, Pallas kernels, local(): pl.pallas_call(lambda *refs: backward_kernel(sizes, *refs), out_shape=(sh...  15.8 us
    ppermute x20, waiting for transfers between devices, shifted(): return lax.ppermute(block, axis, pairs)  11.1 us
    unnamed x28, local copies, waits for them, and re-layouts  7.17 us
  transfers between devices with their start and end apart: 25, of which 8 were waited for; matrix products, arithmetic and copies ran while one was open for 8% of the time, Pallas kernels for 8%

commit v1 on v0

--- a/solution.py
+++ b/solution.py
@@ -81,7 +81,8 @@
         plane = planes[0] + n
         for row in range(*rows):
             summed = dot(matrix, rows_at(tapped, plane, row))
-            for i in range(3):
+            acc[plane + shift, row] = summed[:outputs]
+            for i in (1, 2):
                 place = plane + shift - i
                 acc[place, row] = acc[place, row] + summed[i * outputs : (i + 1) * outputs]
         return carry
@@ -89,16 +90,8 @@
     lax.fori_loop(0, planes[1] - planes[0], one, 0)
 
 
-def clear(acc):
-    def one(n, carry):
-        acc[n] = jnp.zeros(acc.shape[1:], acc.dtype)
-        return carry
-
-    lax.fori_loop(0, acc.shape[0], one, 0)
-
-
 def forward_kernel(
-    sizes, offs, vol, w1, w2, w3, cot, pool,
+    sizes, offs, vol, w1, w2, w3, cot, pool, unread,
     skip_o, coarse_o, cgrad_o, craw_o, fpre_o, spre_o, t1_o, t2_o,
     t1, acc1, t2, acc2, fine, t3,
 ):
@@ -113,7 +106,6 @@
         return carry
 
     lax.fori_loop(0, 10, volume_taps, 0)
-    clear(acc1)
     spread_conv(acc1, w1, t1, (0, 10), (1, 15), 32, 2)
 
     def first(n, carry):
@@ -125,7 +117,6 @@
         return carry
 
     lax.fori_loop(0, 8, first, 0)
-    clear(acc2)
     spread_conv(acc2, w2, t2, (1, 9), (2, 14), 32, 2)
 
     def second(n, carry):
@@ -175,10 +166,8 @@
         craw_o[i * 64 : (i + 1) * 64] = raw[i]
 
 
-def backward_kernel(
-    sizes, offs, cgrad, spre, fpre, cot, t1, t2, w3, w2, w1, spread,
-    vgrad_o, sraw_o, fraw_o,
-    t4, acc4, t5, own5, acc5, t6, own6,
+def second_kernel(
+    sizes, offs, cgrad, spre, cot, t2, w3, spread, t5, sraw_o, t4, acc4, own5
 ):
     nx, ny, nz = sizes
     ox, oy, oz = offs[0], offs[1], offs[2]
@@ -188,17 +177,9 @@
     for x in range(5):
         for y in range(8):
             store_taps(t4, (x, y), cgrad[x, y].astype(F32))
-    clear(acc4)
     spread_conv(acc4, w3, t4, (0, 5), (1, 7), 32, 2)
-
-    own5[0] = jnp.zeros(own5.shape[1:], BF)
-    own5[1] = jnp.zeros(own5.shape[1:], BF)
-    own5[4] = jnp.zeros(own5.shape[1:], BF)
-    own5[5] = jnp.zeros(own5.shape[1:], BF)
-    own6[0] = jnp.zeros(own6.shape[1:], BF)
-    own6[1] = jnp.zeros(own6.shape[1:], BF)
-    own6[4] = jnp.zeros(own6.shape[1:], BF)
-    own6[5] = jnp.zeros(own6.shape[1:], BF)
+    for x in (0, 1, 4, 5):
+        own5[x] = jnp.zeros(own5.shape[1:], BF)
     matrix = spread[...]
 
     def second(n, carry):
@@ -220,8 +201,30 @@
         for y in range(8):
             mine = t5[x + 2, y + 2, 32:64].astype(F32)
             own5[x + 2, y] = jnp.where(own_ok > 0.5, mine, 0.0).astype(BF)
-
-    clear(acc5)
+    weight_sums(sraw_o, own5, t2)
+
+
+def weight_sums(out, own, tapped):
+    out[...] = jnp.zeros(out.shape, F32)
+
+    def one(n, carry):
+        total = jnp.zeros(out.shape, F32)
+        for y in range(8):
+            left = jnp.concatenate([own[n + 2, y], own[n + 1, y], own[n, y]], axis=0)
+            total = total + dot_lanes(left, rows_at(tapped, n, y + 1))
+        out[...] += total
+        return carry
+
+    lax.fori_loop(0, 4, one, 0)
+
+
+def first_kernel(sizes, offs, t5, fpre, t1, w2, w1, vgrad_o, fraw_o, acc5, t6, own6):
+    nx, ny, nz = sizes
+    ox, oy, oz = offs[0], offs[1], offs[2]
+    fine_ok = lane_mask(LANES, oz - 8, 0, nz)
+    own_ok = lane_mask(LANES, 0, 8, 136)
+    for x in (0, 1, 4, 5):
+        own6[x] = jnp.zeros(own6.shape[1:], BF)
     spread_conv(acc5, w2, t5, (0, 6), (1, 11), 32, 2)
 
     def first(n, carry):
@@ -236,24 +239,7 @@
         for y in range(8):
             mine = t6[x + 1, y + 1, 32:64].astype(F32)
             own6[x + 2, y] = jnp.where(own_ok > 0.5, mine, 0.0).astype(BF)
-
-    sraw_o[...] = jnp.zeros(sraw_o.shape, F32)
-    fraw_o[...] = jnp.zeros(fraw_o.shape, F32)
-
-    def weight_grads(n, carry):
-        second_sum = jnp.zeros(sraw_o.shape, F32)
-        first_sum = jnp.zeros(fraw_o.shape, F32)
-        for y in range(8):
-            left = jnp.concatenate([own5[n + 2, y], own5[n + 1, y], own5[n, y]], axis=0)
-            second_sum = second_sum + dot_lanes(left, rows_at(t2, n, y + 1))
-            left = jnp.concatenate([own6[n + 2, y], own6[n + 1, y], own6[n, y]], axis=0)
-            first_sum = first_sum + dot_lanes(left, rows_at(t1, n, y + 1))
-        sraw_o[...] += second_sum
-        fraw_o[...] += first_sum
-        return carry
-
-    lax.fori_loop(0, 4, weight_grads, 0)
-
+    weight_sums(fraw_o, own6, t1)
     for x in range(2):
         for y in range(8):
             total = jnp.zeros((16, LANES), F32)
@@ -279,35 +265,41 @@
     return lax.optimization_barrier(jnp.sum(blocks.astype(F32), axis=0)).astype(BF)
 
 
-def total_over_mesh(rows):
-    plane = ("gy", "gz")
-    count = lax.axis_size("gy") * lax.axis_size("gz")
-    line = lax.axis_size("gx")
-    share = -(-rows.shape[0] // (8 * count)) * 8
-    rows = jnp.pad(rows.astype(BF), ((0, share * count - rows.shape[0]), (0, 0)))
-    part = added(swap(rows.reshape(count, share, 128), plane))
-    part = added(swap(jnp.broadcast_to(part, (line, share, 128)), "gx"))
-    whole = swap(jnp.broadcast_to(part, (count, share, 128)), plane)
-    return whole.reshape(count * share, 128).astype(F32)
-
-
-def grads_over_mesh(first_raw, second_raw, coarse_raw):
-    wide = jnp.concatenate([coarse_raw, second_raw], axis=0)
-    height = wide.shape[0]
-    piece = height // 4
-    rest = jnp.concatenate(
-        [wide[n * piece : (n + 1) * piece, 256:288] for n in range(4)], axis=1
-    )
-    thin = first_raw.reshape(96, 9, 16)[:, :, :4].reshape(96, 36)
-    rows = jnp.concatenate(
-        [wide[:, :128], wide[:, 128:256], rest, jnp.pad(thin, ((0, 0), (0, 92)))], axis=0
-    )
-    rows = total_over_mesh(rows)
+def spread_rows(coarse_raw, second_raw):
+    wide = jnp.concatenate([coarse_raw, second_raw], axis=0).astype(BF)
+    piece = wide.shape[0] // 4
+    rest = [wide[n * piece : (n + 1) * piece, 256:288] for n in range(4)]
+    return jnp.concatenate(
+        [wide[:, :128], wide[:, 128:256], jnp.concatenate(rest, axis=1)], axis=0
+    )
+
+
+def gathered_rows(rows):
+    height, piece = 288, 72
     rest = rows[2 * height : 2 * height + piece]
     rest = jnp.concatenate([rest[:, 32 * n : 32 * n + 32] for n in range(4)], axis=0)
     wide = jnp.concatenate([rows[:height], rows[height : 2 * height], rest], axis=1)
-    thin = rows[2 * height + piece : 2 * height + piece + 96, :36]
-    return thin, wide[192:], wide[:192]
+    return wide[192:], wide[:192]
+
+
+def plane_blocks(blocks):
+    count = lax.axis_size("gy")
+    place = lax.broadcasted_iota(jnp.int32, (count, 1, 1, 1), 0)
+    mine = jnp.where(place == lax.axis_index("gy"), blocks[None], jnp.zeros((), blocks.dtype))
+    return mine.reshape((count * blocks.shape[0],) + blocks.shape[1:])
+
+
+def total_over_line(part):
+    count = lax.axis_size("gx")
+    other = lax.ppermute(part, "gx", [(i, i ^ 1) for i in range(count)])
+    part = added(jnp.stack([part, other]))
+    groups = [list(range(n, count, 2)) for n in range(2)]
+    sent = jnp.broadcast_to(part, (count // 2,) + part.shape)
+    return added(
+        lax.all_to_all(
+            sent, "gx", split_axis=0, concat_axis=0, tiled=True, axis_index_groups=groups
+        )
+    )
 
 
 def weight_form(matrix, outputs, chans):
@@ -325,7 +317,8 @@
     offs = jnp.stack([lax.axis_index(axis) * extent for axis, extent in zip(AXES, extents)])
     offs = offs.astype(jnp.int32)
 
-    wide_volume = halo(halo(halo(volume, "gx", 1, 4), "gy", 2, 4), "gz", 3, 8)
+    line_volume = halo(volume, "gx", 1, 4)
+    wide_volume = halo(halo(line_volume, "gy", 2, 4), "gz", 3, 8)
     wide_volume = jnp.pad(
         jnp.transpose(wide_volume, (1, 2, 0, 3)), ((0, 0), (0, 0), (0, 12), (0, LANES - 144))
     )
@@ -336,7 +329,8 @@
     returned = swap(sent, "gz")
     returned = jnp.transpose(returned, (2, 0, 1, 3)).reshape(4, 64, depth + 4)
     returned = jnp.pad(returned, ((0, 0), (0, 0), (2, 128 - 70)))
-    rows_cotangent = jnp.transpose(skip_cotangent, (1, 2, 0, 3))
+    later = line_volume[0, 0, 0, 0] * 0 + line_volume[0, 9, 0, 0] * 0
+    rows_cotangent = jnp.transpose(skip_cotangent, (1, 2, 0, 3)) + later
     wide_cotangent = halo(halo(halo(rows_cotangent, "gx", 0, 2), "gy", 1, 2), "gz", 3, 2)
     wide_cotangent = jnp.pad(wide_cotangent, ((0, 0), (0, 0), (0, 0), (6, LANES - 138)))
 
@@ -361,7 +355,7 @@
                 shape((4, 10, 48, LANES), BF),
                 shape((4, 10, 96, LANES), BF),
             ),
-            in_specs=[smem] + [vmem] * 6,
+            in_specs=[smem] + [vmem] * 6 + [pl.BlockSpec(memory_space=pl.ANY)],
             out_specs=(vmem,) * 8,
             scratch_shapes=[
                 pltpu.VMEM((10, 16, 48, LANES), BF),
@@ -384,55 +378,91 @@
             stacked(w_coarse),
             returned,
             pool,
+            wide_cotangent,
         )
     )
-    coarse = coarse_local[:, :, 4 : 4 + depth].reshape(4, sides, 64 // sides, depth)
-    coarse = swap(jnp.transpose(coarse, (1, 2, 0, 3)), "gz")
-    coarse = jnp.transpose(coarse, (1, 2, 0, 3)).reshape(64 // sides, 1, 4, sides * depth)
-
     wide_grad = halo(halo(coarse_grad[None], "gx", 0, 2), "gy", 1, 2)
-    back_first = jnp.pad(flipped(w_first), ((0, 12),) + ((0, 0),) * 4)
-    volume_grad, second_raw, first_raw = pl.pallas_call(
-        lambda *refs: backward_kernel(sizes, *refs),
-        out_shape=(
-            shape((2, 8, 16, 128), BF),
-            shape((96, 288), F32),
-            shape((96, 144), F32),
-        ),
-        in_specs=[smem] + [vmem] * 10,
-        out_specs=(vmem,) * 3,
+    taps5, second_raw = pl.pallas_call(
+        lambda *refs: second_kernel(sizes, *refs),
+        out_shape=(shape((6, 12, 96, LANES), BF), shape((96, 288), F32)),
+        in_specs=[smem] + [vmem] * 6,
+        out_specs=(vmem,) * 2,
         scratch_shapes=[
             pltpu.VMEM((5, 8, 192, 128), BF),
             pltpu.VMEM((7, 8, 32, 128), F32),
-            pltpu.VMEM((6, 12, 96, LANES), BF),
             pltpu.VMEM((6, 8, 32, LANES), BF),
+        ],
+        compiler_params=pltpu.CompilerParams(vmem_limit_bytes=48 * 2**20),
+        cost_estimate=pl.CostEstimate(
+            flops=10**9, bytes_accessed=10 * 10**6, transcendentals=10**6
+        ),
+        name="second",
+    )(
+        offs,
+        wide_grad,
+        second_pre,
+        wide_cotangent,
+        taps2,
+        stacked(flipped(w_coarse)).reshape(96, 576),
+        spread,
+    )
+
+    plane = ("gy", "gz")
+    count = counts[1] * counts[2]
+    rows = spread_rows(coarse_raw, second_raw)
+    share = -(-rows.shape[0] // (8 * count)) * 8
+    rows = jnp.pad(rows, ((0, share * count - rows.shape[0]), (0, 0)))
+    blocks = coarse_local[:, :, 4 : 4 + depth].reshape(4, sides, 64 // sides, depth)
+    blocks = jnp.transpose(blocks, (1, 0, 2, 3)).reshape(sides, -1, depth)
+    half = blocks.shape[1] // 2
+    blocks = jnp.concatenate([blocks[:, :half], blocks[:, half:]], axis=2)
+    arrived = swap(
+        jnp.concatenate([rows.reshape(count, share, 128), plane_blocks(blocks)], axis=1), plane
+    )
+
+    back_first = jnp.pad(flipped(w_first), ((0, 12),) + ((0, 0),) * 4)
+    volume_grad, first_raw = pl.pallas_call(
+        lambda *refs: first_kernel(sizes, *refs),
+        out_shape=(shape((2, 8, 16, 128), BF), shape((96, 144), F32)),
+        in_specs=[smem] + [vmem] * 5,
+        out_specs=(vmem,) * 2,
+        scratch_shapes=[
             pltpu.VMEM((8, 12, 32, LANES), F32),
             pltpu.VMEM((4, 10, 96, LANES), BF),
             pltpu.VMEM((6, 8, 32, LANES), BF),
         ],
-        compiler_params=pltpu.CompilerParams(vmem_limit_bytes=52 * 2**20),
+        compiler_params=pltpu.CompilerParams(vmem_limit_bytes=48 * 2**20),
         cost_estimate=pl.CostEstimate(
             flops=2 * 10**9, bytes_accessed=10 * 10**6, transcendentals=10**6
         ),
-        name="backward",
+        name="first",
     )(
         offs,
-        wide_grad,
-        second_pre,
+        taps5,
         first_pre,
-        wide_cotangent,
         taps1,
-        taps2,
-        stacked(flipped(w_coarse)).reshape(96, 576),
         stacked(flipped(w_second)).reshape(96, 288),
         stacked(back_first),
-        spread,
-    )
+    )
+
+    part = added(arrived[:, :share])
+    own_row = lax.axis_index("gy") * sides
+    coarse = lax.dynamic_slice_in_dim(arrived[:, share:], own_row, sides, axis=0)
+    coarse = jnp.concatenate([coarse[:, :, :depth], coarse[:, :, depth:]], axis=1)
+    coarse = coarse.reshape(sides, 4, 64 // sides, depth)
+    coarse = jnp.transpose(coarse, (2, 1, 0, 3)).reshape(64 // sides, 1, 4, sides * depth)
+
+    thin = first_raw.reshape(3, 32, 9, 16)[..., :4].reshape(3, 32, 36).astype(BF)
+    thin = jnp.pad(jnp.concatenate([thin[0], thin[1], thin[2]], axis=1), ((0, 0), (0, 20)))
+    part = total_over_line(jnp.concatenate([part, thin], axis=0))
+    whole = swap(jnp.broadcast_to(part, (count,) + part.shape), plane)
+    second, wide = gathered_rows(whole[:, :share].reshape(count * share, 128).astype(F32))
+    thin = jnp.sum(whole[:, share:].astype(F32), axis=0)
+    thin = jnp.stack([thin[:, 36 * n : 36 * n + 36] for n in range(3)])
 
     skip = jnp.transpose(skip, (2, 0, 1, 3))
     volume_grad = jnp.transpose(volume_grad[:, :, :4], (2, 0, 1, 3))
     factor = 1.0 / math.sqrt(sizes[0] * sizes[1] * sizes[2])
-    thin, second, wide = grads_over_mesh(first_raw, second_raw, coarse_raw)
     return (
         skip,
         coarse,

time: 218 us -> 213 us (0.977)
  blocking collectives: 0 us -> 17.7 us
  starting transfers between devices: 110 us -> 94.8 us
  waiting for transfers between devices: 44.5 us -> 33 us
    all_to_all x5 -> x3, waiting for transfers between devices: 33.5 us -> 15.7 us  [swap(): return lax.all_to_all(blocks, axes, split_axis=0, concat_axis=0, tiled=True)]
    all_to_all x0 -> x1, blocking collectives: none -> 17.7 us  [total_over_line(): lax.all_to_all(sent, 'gx', split_axis=0, concat_axis=0, tiled=True, axis_...]
    all_to_all x5 -> x3, starting transfers between devices: 36 us -> 18.3 us  [swap(): return lax.all_to_all(blocks, axes, split_axis=0, concat_axis=0, tiled=True)]
    ppermute x0 -> x1, starting transfers between devices: none -> 4.84 us  [total_over_line(): other = lax.ppermute(part, 'gx', [(i, i ^ 1) for i in range(count)])]
    ppermute x0 -> x1, waiting for transfers between devices: none -> 3.52 us  [total_over_line(): other = lax.ppermute(part, 'gx', [(i, i ^ 1) for i in range(count)])]
    ppermute x20, waiting for transfers between devices: 11.1 us -> 13.8 us  [shifted(): return lax.ppermute(block, axis, pairs)]
    pallas_call x1 -> x2, Pallas kernels: 15.8 us -> 16.4 us  [the longest x1 9.33 us: local(): pl.pallas_call(lambda *refs: second_kernel(sizes, *refs), out_shape=(shap...]
    unnamed x28 -> x30, local copies, waits for them, and re-layouts: 7.17 us -> 7.46 us
  transfers between devices with their start and end apart: 25 -> 24, of which waited for: 8 -> 9; matrix products, arithmetic and copies ran while one was open for 8% -> 9% of each run, Pallas kernels for 8% -> 3%
where the time goes in v1:
time: 213 us; the launch traced here: 212 us
  starting transfers between devices  94.8 us (45%)
  Pallas kernels  33.4 us (16%)
  waiting for transfers between devices  33 us (15%)
  local copies, waits for them, and re-layouts  22.6 us (11%)
  blocking collectives  17.7 us (8%)
  other arithmetic  7.6 us (4%)
  between operations  2.8 us (1%)
    ppermute x20, starting transfers between devices, shifted(): return lax.ppermute(block, axis, pairs)  71.7 us
    all_to_all x3, starting transfers between devices, swap(): return lax.all_to_all(blocks, axes, split_axis=0, concat_axis=0, tiled=True)  18.3 us
    all_to_all x1, blocking collectives, total_over_line(): lax.all_to_all(sent, 'gx', split_axis=0, concat_axis=0, tiled=True, axis_...  17.7 us
    pallas_call x1, Pallas kernels, local(): pl.pallas_call(lambda *refs: forward_kernel(sizes, *refs), out_shape=(sha...  17 us
    all_to_all x3, waiting for transfers between devices, swap(): return lax.all_to_all(blocks, axes, split_axis=0, concat_axis=0, tiled=True)  15.7 us
    ppermute x20, waiting for transfers between devices, shifted(): return lax.ppermute(block, axis, pairs)  13.8 us
    pallas_call x1, Pallas kernels, local(): pl.pallas_call(lambda *refs: second_kernel(sizes, *refs), out_shape=(shap...  9.33 us
    unnamed x30, local copies, waits for them, and re-layouts  7.46 us
  transfers between devices with their start and end apart: 24, of which 9 were waited for; matrix products, arithmetic and copies ran while one was open for 9% of the time, Pallas kernels for 3%

profile of v1, /device:TPU:1, one launch (start us, length us, event | category | flops | bytes accessed | tf_op | source)
XLA Modules:
  0.0 212.0 jit_solution(17141391587237828227)
XLA Ops:
  1.4 4.0 %collective-permute-start = (bf16[4,2,8,128]{3,0,2,1:T(4,128)(2,1)S(1)}, bf16[4,2,8,128]{3,0,2,1:T(4,128)(2,1)S(1)}, u32[]{:S(2)}, u32[]{:S(2)}) collective-permute-start(bf16[4,2,8,128]{3,0,2,1:T(4,128)(2,1)S(1)} %copy.146), channel_id=1, source_target_pairs={{0,64},{32,96},{64,128},{96,160},{128,192},{160,224},{192,256},{22... | collective-permute-start | bytes 49160 | tf_op jit(solution)/shard_map/ppermute | solution.py:19
  5.4 1.3 collective-permute-start.3
  6.7 10.6 %collective-permute-start.1 = (bf16[4,2,8,128]{3,0,2,1:T(4,128)(2,1)S(1)}, bf16[4,2,8,128]{3,0,2,1:T(4,128)(2,1)S(1)}, u32[]{:S(2)}, u32[]{:S(2)}) collective-permute-start(bf16[4,2,8,128]{3,0,2,1:T(4,128)(2,1)S(1)} %copy.146), channel_id=1, source_target_pairs={{0,32},{32,64},{64,96},{96,128},{128,160},{160,192},{192,224},{224... | collective-permute-start | bytes 49160 | tf_op jit(solution)/shard_map/ppermute | solution.py:19
  17.4 1.3 collective-permute-start.2
  20.4 4.3 %all-to-all-start = ((bf16[4,16,4,68]{3,2,1,0:T(4,128)(2,1)}), bf16[4,16,4,68]{3,2,1,0:T(4,128)(2,1)S(1)}, u32[]{:S(2)}, u32[]{:S(2)}) async-start(bf16[4,16,4,68]{3,2,1,0:T(4,128)(2,1)} %pad_maximum_fusion.11), calls=%async_computation | async-start | bytes 131072 | tf_op jit(solution)/shard_map/all_to_all | solution.py:261
  29.9 7.9 %collective-permute-start.8 = (bf16[2,8,32,128]{3,2,1,0:T(8,128)(2,1)S(1)}, bf16[2,8,32,128]{3,2,1,0:T(8,128)(2,1)S(1)}, u32[]{:S(2)}, u32[]{:S(2)}) collective-permute-start(bf16[2,8,32,128]{3,2,1,0:T(8,128)(2,1)S(1)} %fusion.22), channel_id=1, source_target_pairs={{0,32},{32,64},{64,96},{96,128},{128,160},{160,192},{192,224},{224... | collective-permute-start | bytes 393224 | tf_op jit(solution)/shard_map/ppermute | solution.py:19
  37.8 1.3 collective-permute-start.9
  40.0 5.1 %collective-permute-start.4 = (bf16[4,10,4,128]{3,0,2,1:T(4,128)(2,1)S(1)}, bf16[4,10,4,128]{3,0,2,1:T(4,128)(2,1)S(1)}, u32[]{:S(2)}, u32[]{:S(2)}) collective-permute-start(bf16[4,10,4,128]{3,0,2,1:T(4,128)(2,1)S(1)} %get-tuple-element.89), channel_id=1, source_target_pairs={{0,4},{4,8},{8,12},{12,16},{16,20},{20,24},{24,28},{1,5},{5,9},{9,... | collective-permute-start | bytes 122888 | tf_op jit(solution)/shard_map/ppermute | solution.py:19
  45.1 1.9 collective-permute-start.5
  50.9 4.1 %collective-permute-start.10 = (bf16[6,2,32,128]{3,2,1,0:T(8,128)(2,1)S(1)}, bf16[6,2,32,128]{3,2,1,0:T(8,128)(2,1)S(1)}, u32[]{:S(2)}, u32[]{:S(2)}) collective-permute-start(bf16[6,2,32,128]{3,2,1,0:T(8,128)(2,1)S(1)} %get-tuple-element.77), channel_id=1, source_target_pairs={{0,4},{4,8},{8,12},{12,16},{16,20},{20,24},{24,28},{1,5},{5,9},{9,... | collective-permute-start | bytes 294920 | tf_op jit(solution)/shard_map/ppermute | solution.py:19
  55.0 1.9 collective-permute-start.11
  57.1 3.7 %collective-permute-start.6 = (bf16[4,10,16,8]{3,0,2,1:T(4,128)(2,1)S(1)}, bf16[4,10,16,8]{3,0,2,1:T(4,128)(2,1)S(1)}, u32[]{:S(2)}, u32[]{:S(2)}) collective-permute-start(bf16[4,10,16,8]{3,0,2,1:T(4,128)(2,1)S(1)} %get-tuple-element.85), channel_id=1, source_target_pairs={{0,1},{1,2},{2,3},{4,5},{5,6},{6,7},{8,9},{9,10},{10,11},{12,13},{... | collective-permute-start | bytes 30728 | tf_op jit(solution)/shard_map/ppermute | solution.py:19
  63.0 4.0 %collective-permute-start.12 = (bf16[6,12,32,2]{2,3,1,0:T(2,128)(2,1)S(1)}, bf16[6,12,32,2]{2,3,1,0:T(2,128)(2,1)S(1)}, u32[]{:S(2)}, u32[]{:S(2)}) collective-permute-start(bf16[6,12,32,2]{2,3,1,0:T(2,128)(2,1)S(1)} %copy.155), channel_id=1, source_target_pairs={{0,1},{1,2},{2,3},{4,5},{5,6},{6,7},{8,9},{9,10},{10,11},{12,13},{... | collective-permute-start | bytes 27656 | tf_op jit(solution)/shard_map/ppermute | solution.py:19
  67.5 1.3 collective-permute-start.13
  72.7 2.8 %select_maximum_fusion.refs_7_.refs_3_ = bf16[6,12,32,256]{3,2,1,0:T(8,128)(2,1)} fusion(bf16[6,12,32,2]{3,2,1,0:T(8,128)(2,1)S(1)} %copy.158, bf16[6,12,32,2]{3,2,1,0:T(8,128)(2,1)S(1)} %copy.157, bf16[6,2,32,128]{3,2,1,0:T(8,128)(2,1)S(1)} %collective-permute-done.11, bf16[6,2,32,128]{3,2,1,0:T(8,128)(2,1)S(1)} %collective-permute-done.10, ...), kind=kLoop, calls=%fused_computation.3 | loop fusion | flops 14155776 | bytes 1787904 | tf_op jit(solution)/shard_map/concatenate | solution.py:31
  75.5 17.0 %forward.1 = (bf16[2,8,32,128]{3,2,1,0:T(8,128)(2,1)S(1)}, bf16[4,64,128]{2,1,0:T(8,128)(2,1)S(1)}, bf16[4,64,128]{2,1,0:T(8,128)(2,1)S(1)}, f32[192,288]{1,0:T(...) custom-call(s32[3]{0:T(128)S(1)} %pad_add_fusion.refs_0_, ...), custom_call_target="tpu_custom_call" | custom-call | flops 4000000000 | bytes 12000000 | tf_op jit(solution)/shard_map/forward/pallas_call | solution.py:346
  92.5 5.3 %collective-permute-start.14 = (bf16[1,4,64,128]{3,2,1,0:T(8,128)(2,1)S(1)}, bf16[1,4,64,128]{3,2,1,0:T(8,128)(2,1)S(1)}, u32[]{:S(2)}, u32[]{:S(2)}) collective-permute-start(bf16[1,4,64,128]{3,2,1,0:T(8,128)(2,1)S(1)} %bitcast.77), channel_id=1, source_target_pairs={{0,64},{32,96},{64,128},{96,160},{128,192},{160,224},{192,256},{22... | collective-permute-start | bytes 196616 | tf_op jit(solution)/shard_map/ppermute | solution.py:19
  97.8 5.9 %collective-permute-start.15 = (bf16[1,4,64,128]{3,2,1,0:T(8,128)(2,1)S(1)}, bf16[1,4,64,128]{3,2,1,0:T(8,128)(2,1)S(1)}, u32[]{:S(2)}, u32[]{:S(2)}) collective-permute-start(bf16[1,4,64,128]{3,2,1,0:T(8,128)(2,1)S(1)} %bitcast.78), channel_id=1, source_target_pairs={{0,32},{32,64},{64,96},{96,128},{128,160},{160,192},{192,224},{224... | collective-permute-start | bytes 196616 | tf_op jit(solution)/shard_map/ppermute | solution.py:19
  106.7 6.6 %collective-permute-done.16 = bf16[1,4,64,128]{3,2,1,0:T(8,128)(2,1)S(1)} collective-permute-done((bf16[1,4,64,128]{3,2,1,0:T(8,128)(2,1)S(1)}, bf16[1,4,64,128]{3,2,1,0:T(8,128)(2,1)S(1)}, u32[]{:S(2)}, u32[]{:S(2)}) %collective-permute-start.16) | collective-permute-done | bytes 65568 | tf_op jit(solution)/shard_map/ppermute | solution.py:19
  113.6 6.3 %collective-permute-start.18 = (bf16[5,2,64,128]{3,2,1,0:T(8,128)(2,1)S(1)}, bf16[5,2,64,128]{3,2,1,0:T(8,128)(2,1)S(1)}, u32[]{:S(2)}, u32[]{:S(2)}) collective-permute-start(bf16[5,2,64,128]{3,2,1,0:T(8,128)(2,1)S(1)} %get-tuple-element.79), channel_id=1, source_target_pairs={{0,4},{4,8},{8,12},{12,16},{16,20},{20,24},{24,28},{1,5},{5,9},{9,... | collective-permute-start | bytes 491528 | tf_op jit(solution)/shard_map/ppermute | solution.py:19
  119.9 1.9 collective-permute-start.19
  122.1 4.4 %collective-permute-done.19 = bf16[5,2,64,128]{3,2,1,0:T(8,128)(2,1)S(1)} collective-permute-done((bf16[5,2,64,128]{3,2,1,0:T(8,128)(2,1)S(1)}, bf16[5,2,64,128]{3,2,1,0:T(8,128)(2,1)S(1)}, u32[]{:S(2)}, u32[]{:S(2)}) %collective-permute-start.19) | collective-permute-done | bytes 163872 | tf_op jit(solution)/shard_map/ppermute | solution.py:19
  126.6 9.3 %second.1 = (bf16[6,12,96,256]{3,2,1,0:T(8,128)(2,1)}, f32[96,288]{1,0:T(8,128)S(1)}) custom-call(s32[3]{0:T(128)S(1)} %pad_add_fusion.refs_0_, bf16[5,8,64,128]{3,2,1,0:T(8,128)(2,1)S(1)} %pad_maximum_fusion.refs_1_, f32[6,12,32,256]{3,2,1,0:T(8,128)} %get-tuple-element.21.refs_2_, bf16[6,12,32,256]{3,2,1,0:T(8,128)(2,1)S(1)} %copy-done, ...), custom_call_target="tpu_custom_call" | custom-call | flops 1000000000 | bytes 10000000 | tf_op jit(solution)/shard_map/second/pallas_call | solution.py:385
  137.0 6.5 %all-to-all-start.1 = ((bf16[32,56,128]{2,1,0:T(8,128)(2,1)}), bf16[32,56,128]{2,1,0:T(8,128)(2,1)S(1)}, u32[]{:S(2)}, u32[]{:S(2)}) async-start(bf16[32,56,128]{2,1,0:T(8,128)(2,1)} %pad_maximum_fusion.2), calls=%async_computation.1 | async-start | bytes 917504 | tf_op jit(solution)/shard_map/all_to_all | solution.py:261
  145.8 2.0 copy-done.2
  147.8 7.1 %first.1 = (bf16[2,8,16,128]{3,2,1,0:T(8,128)(2,1)S(1)}, f32[96,144]{1,0:T(8,128)S(1)}) custom-call(s32[3]{0:T(128)S(1)} %pad_add_fusion.refs_0_, bf16[6,12,96,256]{3,2,1,0:T(8,128)(2,1)S(1)} %copy-done.2, f32[4,10,32,256]{3,2,1,0:T(8,128)S(1)} %copy-done.3, bf16[4,10,48,256]{3,2,1,0:T(8,128)(2,1)S(1)} %get-tuple-element.27.refs_3_, ...), custom_call_target="tpu_custom_call" | custom-call | flops 2000000000 | bytes 10000000 | tf_op jit(solution)/shard_map/first/pallas_call | solution.py:424
  155.7 2.8 %all-to-all-done.1 = bf16[32,56,128]{2,1,0:T(8,128)(2,1)S(1)} async-done(((bf16[32,56,128]{2,1,0:T(8,128)(2,1)}), bf16[32,56,128]{2,1,0:T(8,128)(2,1)S(1)}, u32[]{:S(2)}, u32[]{:S(2)}) %all-to-all-start.1) | async-done | bytes 458784 | tf_op jit(solution)/shard_map/all_to_all | solution.py:261
  158.6 4.8 %collective-permute-start.20 = (bf16[56,128]{1,0:T(8,128)(2,1)S(1)}, bf16[56,128]{1,0:T(8,128)(2,1)S(1)}, u32[]{:S(2)}, u32[]{:S(2)}) collective-permute-start(bf16[56,128]{1,0:T(8,128)(2,1)S(1)} %get-tuple-element.101), channel_id=1, source_target_pairs={{0,32},{32,0},{64,96},{96,64},{128,160},{160,128},{192,224},{224,1... | collective-permute-start | bytes 43016 | tf_op jit(solution)/shard_map/ppermute | solution.py:294
  163.5 3.5 %collective-permute-done.20 = bf16[56,128]{1,0:T(8,128)(2,1)S(1)} collective-permute-done((bf16[56,128]{1,0:T(8,128)(2,1)S(1)}, bf16[56,128]{1,0:T(8,128)(2,1)S(1)}, u32[]{:S(2)}, u32[]{:S(2)}) %collective-permute-start.20) | collective-permute-done | bytes 14368 | tf_op jit(solution)/shard_map/ppermute | solution.py:294
  167.3 17.7 %all_to_all.20 = bf16[8,56,128]{2,1,0:T(8,128)(2,1)S(1)} all-to-all(bf16[8,56,128]{2,1,0:T(8,128)(2,1)S(1)} %broadcast_in_dim.59), channel_id=1, replica_groups={{0,64,128,192,256,320,384,448},{32,96,160,224,288,352,416,480},{1,65,12..., dimensions={0} | all-to-all | bytes 229376 | tf_op jit(solution)/shard_map/all_to_all | solution.py:299
  185.8 7.5 %all-to-all-start.3 = ((bf16[32,56,128]{2,1,0:T(8,128)(2,1)}), bf16[32,56,128]{2,1,0:T(8,128)(2,1)S(1)}, u32[]{:S(2)}, u32[]{:S(2)}) async-start(bf16[32,56,128]{2,1,0:T(8,128)(2,1)} %broadcast_in_dim.60), calls=%async_computation.3 | async-start | bytes 917504 | tf_op jit(solution)/shard_map/all_to_all | solution.py:261
  195.6 12.9 %all-to-all-done.3 = bf16[32,56,128]{2,1,0:T(8,128)(2,1)S(1)} async-done(((bf16[32,56,128]{2,1,0:T(8,128)(2,1)}), bf16[32,56,128]{2,1,0:T(8,128)(2,1)S(1)}, u32[]{:S(2)}, u32[]{:S(2)}) %all-to-all-start.3) | async-done | bytes 458784 | tf_op jit(solution)/shard_map/all_to_all | solution.py:261
  (152 shorter events, 32.1 us)
Async XLA Ops:
  0.6 48.0 %copy-start.4 = (bf16[64,3,3,3,32]{0,4,3,2,1:T(8,128)(2,1)S(1)}, bf16[64,3,3,3,32]{0,4,3,2,1:T(8,128)(2,1)}, u32[]{:S(2)}) copy-start(bf16[64,3,3,3,32]{0,4,3,2,1:T(8,128)(2,1)} %param.9) | copy-start | bytes 331780
  1.4 25.2 %collective-permute-start = (bf16[4,2,8,128]{3,0,2,1:T(4,128)(2,1)S(1)}, bf16[4,2,8,128]{3,0,2,1:T(4,128)(2,1)S(1)}, u32[]{:S(2)}, u32[]{:S(2)}) collective-permute-start(bf16[4,2,8,128]{3,0,2,1:T(4,128)(2,1)S(1)} %copy.146), channel_id=1, source_target_pairs={{0,64},{32,96},{64,128},{96,160},{128,192},{160,224},{192,256},{22... | collective-permute-start | bytes 49160 | tf_op jit(solution)/shard_map/ppermute | solution.py:19
  5.4 21.7 %collective-permute-start.3 = (bf16[4,2,8,128]{3,0,2,1:T(4,128)(2,1)S(1)}, bf16[4,2,8,128]{3,0,2,1:T(4,128)(2,1)S(1)}, u32[]{:S(2)}, u32[]{:S(2)}) collective-permute-start(bf16[4,2,8,128]{3,0,2,1:T(4,128)(2,1)S(1)} %copy.146), channel_id=1, source_target_pairs={{64,0},{96,32},{128,64},{160,96},{192,128},{224,160},{256,192},{28... | collective-permute-start | bytes 49160 | tf_op jit(solution)/shard_map/ppermute | solution.py:19
  6.7 32.4 %collective-permute-start.1 = (bf16[4,2,8,128]{3,0,2,1:T(4,128)(2,1)S(1)}, bf16[4,2,8,128]{3,0,2,1:T(4,128)(2,1)S(1)}, u32[]{:S(2)}, u32[]{:S(2)}) collective-permute-start(bf16[4,2,8,128]{3,0,2,1:T(4,128)(2,1)S(1)} %copy.146), channel_id=1, source_target_pairs={{0,32},{32,64},{64,96},{96,128},{128,160},{160,192},{192,224},{224... | collective-permute-start | bytes 49160 | tf_op jit(solution)/shard_map/ppermute | solution.py:19
  17.4 22.5 %collective-permute-start.2 = (bf16[4,2,8,128]{3,0,2,1:T(4,128)(2,1)S(1)}, bf16[4,2,8,128]{3,0,2,1:T(4,128)(2,1)S(1)}, u32[]{:S(2)}, u32[]{:S(2)}) collective-permute-start(bf16[4,2,8,128]{3,0,2,1:T(4,128)(2,1)S(1)} %copy.146), channel_id=1, source_target_pairs={{32,0},{64,32},{96,64},{128,96},{160,128},{192,160},{224,192},{256... | collective-permute-start | bytes 49160 | tf_op jit(solution)/shard_map/ppermute | solution.py:19
  20.4 29.1 %all-to-all-start = ((bf16[4,16,4,68]{3,2,1,0:T(4,128)(2,1)}), bf16[4,16,4,68]{3,2,1,0:T(4,128)(2,1)S(1)}, u32[]{:S(2)}, u32[]{:S(2)}) async-start(bf16[4,16,4,68]{3,2,1,0:T(4,128)(2,1)} %pad_maximum_fusion.11), calls=%async_computation | async-start | bytes 131072 | tf_op jit(solution)/shard_map/all_to_all | solution.py:261
  29.9 20.9 %collective-permute-start.8 = (bf16[2,8,32,128]{3,2,1,0:T(8,128)(2,1)S(1)}, bf16[2,8,32,128]{3,2,1,0:T(8,128)(2,1)S(1)}, u32[]{:S(2)}, u32[]{:S(2)}) collective-permute-start(bf16[2,8,32,128]{3,2,1,0:T(8,128)(2,1)S(1)} %fusion.22), channel_id=1, source_target_pairs={{0,32},{32,64},{64,96},{96,128},{128,160},{160,192},{192,224},{224... | collective-permute-start | bytes 393224 | tf_op jit(solution)/shard_map/ppermute | solution.py:19
  37.8 13.0 %collective-permute-start.9 = (bf16[2,8,32,128]{3,2,1,0:T(8,128)(2,1)S(1)}, bf16[2,8,32,128]{3,2,1,0:T(8,128)(2,1)S(1)}, u32[]{:S(2)}, u32[]{:S(2)}) collective-permute-start(bf16[2,8,32,128]{3,2,1,0:T(8,128)(2,1)S(1)} %fusion.22), channel_id=1, source_target_pairs={{32,0},{64,32},{96,64},{128,96},{160,128},{192,160},{224,192},{256... | collective-permute-start | bytes 393224 | tf_op jit(solution)/shard_map/ppermute | solution.py:19
  40.0 9.5 %collective-permute-start.4 = (bf16[4,10,4,128]{3,0,2,1:T(4,128)(2,1)S(1)}, bf16[4,10,4,128]{3,0,2,1:T(4,128)(2,1)S(1)}, u32[]{:S(2)}, u32[]{:S(2)}) collective-permute-start(bf16[4,10,4,128]{3,0,2,1:T(4,128)(2,1)S(1)} %get-tuple-element.89), channel_id=1, source_target_pairs={{0,4},{4,8},{8,12},{12,16},{16,20},{20,24},{24,28},{1,5},{5,9},{9,... | collective-permute-start | bytes 122888 | tf_op jit(solution)/shard_map/ppermute | solution.py:19
  45.1 5.6 %collective-permute-start.5 = (bf16[4,10,4,128]{3,0,2,1:T(4,128)(2,1)S(1)}, bf16[4,10,4,128]{3,0,2,1:T(4,128)(2,1)S(1)}, u32[]{:S(2)}, u32[]{:S(2)}) collective-permute-start(bf16[4,10,4,128]{3,0,2,1:T(4,128)(2,1)S(1)} %get-tuple-element.90), channel_id=1, source_target_pairs={{4,0},{8,4},{12,8},{16,12},{20,16},{24,20},{28,24},{5,1},{9,5},{13... | collective-permute-start | bytes 122888 | tf_op jit(solution)/shard_map/ppermute | solution.py:19
  50.9 11.2 %collective-permute-start.10 = (bf16[6,2,32,128]{3,2,1,0:T(8,128)(2,1)S(1)}, bf16[6,2,32,128]{3,2,1,0:T(8,128)(2,1)S(1)}, u32[]{:S(2)}, u32[]{:S(2)}) collective-permute-start(bf16[6,2,32,128]{3,2,1,0:T(8,128)(2,1)S(1)} %get-tuple-element.77), channel_id=1, source_target_pairs={{0,4},{4,8},{8,12},{12,16},{16,20},{20,24},{24,28},{1,5},{5,9},{9,... | collective-permute-start | bytes 294920 | tf_op jit(solution)/shard_map/ppermute | solution.py:19
  55.0 7.1 %collective-permute-start.11 = (bf16[6,2,32,128]{3,2,1,0:T(8,128)(2,1)S(1)}, bf16[6,2,32,128]{3,2,1,0:T(8,128)(2,1)S(1)}, u32[]{:S(2)}, u32[]{:S(2)}) collective-permute-start(bf16[6,2,32,128]{3,2,1,0:T(8,128)(2,1)S(1)} %get-tuple-element.78), channel_id=1, source_target_pairs={{4,0},{8,4},{12,8},{16,12},{20,16},{24,20},{28,24},{5,1},{9,5},{13... | collective-permute-start | bytes 294920 | tf_op jit(solution)/shard_map/ppermute | solution.py:19
  57.1 11.7 %collective-permute-start.6 = (bf16[4,10,16,8]{3,0,2,1:T(4,128)(2,1)S(1)}, bf16[4,10,16,8]{3,0,2,1:T(4,128)(2,1)S(1)}, u32[]{:S(2)}, u32[]{:S(2)}) collective-permute-start(bf16[4,10,16,8]{3,0,2,1:T(4,128)(2,1)S(1)} %get-tuple-element.85), channel_id=1, source_target_pairs={{0,1},{1,2},{2,3},{4,5},{5,6},{6,7},{8,9},{9,10},{10,11},{12,13},{... | collective-permute-start | bytes 30728 | tf_op jit(solution)/shard_map/ppermute | solution.py:19
  60.8 8.0 %collective-permute-start.7 = (bf16[4,10,16,8]{3,0,2,1:T(4,128)(2,1)S(1)}, bf16[4,10,16,8]{3,0,2,1:T(4,128)(2,1)S(1)}, u32[]{:S(2)}, u32[]{:S(2)}) collective-permute-start(bf16[4,10,16,8]{3,0,2,1:T(4,128)(2,1)S(1)} %get-tuple-element.86), channel_id=1, source_target_pairs={{1,0},{2,1},{3,2},{5,4},{6,5},{7,6},{9,8},{10,9},{11,10},{13,12},{... | collective-permute-start | bytes 30728 | tf_op jit(solution)/shard_map/ppermute | solution.py:19
  63.0 7.6 %collective-permute-start.12 = (bf16[6,12,32,2]{2,3,1,0:T(2,128)(2,1)S(1)}, bf16[6,12,32,2]{2,3,1,0:T(2,128)(2,1)S(1)}, u32[]{:S(2)}, u32[]{:S(2)}) collective-permute-start(bf16[6,12,32,2]{2,3,1,0:T(2,128)(2,1)S(1)} %copy.155), channel_id=1, source_target_pairs={{0,1},{1,2},{2,3},{4,5},{5,6},{6,7},{8,9},{9,10},{10,11},{12,13},{... | collective-permute-start | bytes 27656 | tf_op jit(solution)/shard_map/ppermute | solution.py:19
  67.5 4.7 %collective-permute-start.13 = (bf16[6,12,32,2]{2,3,1,0:T(2,128)(2,1)S(1)}, bf16[6,12,32,2]{2,3,1,0:T(2,128)(2,1)S(1)}, u32[]{:S(2)}, u32[]{:S(2)}) collective-permute-start(bf16[6,12,32,2]{2,3,1,0:T(2,128)(2,1)S(1)} %copy.156), channel_id=1, source_target_pairs={{1,0},{2,1},{3,2},{5,4},{6,5},{7,6},{9,8},{10,9},{11,10},{13,12},{... | collective-permute-start | bytes 27656 | tf_op jit(solution)/shard_map/ppermute | solution.py:19
  92.5 14.2 %collective-permute-start.14 = (bf16[1,4,64,128]{3,2,1,0:T(8,128)(2,1)S(1)}, bf16[1,4,64,128]{3,2,1,0:T(8,128)(2,1)S(1)}, u32[]{:S(2)}, u32[]{:S(2)}) collective-permute-start(bf16[1,4,64,128]{3,2,1,0:T(8,128)(2,1)S(1)} %bitcast.77), channel_id=1, source_target_pairs={{0,64},{32,96},{64,128},{96,160},{128,192},{160,224},{192,256},{22... | collective-permute-start | bytes 196616 | tf_op jit(solution)/shard_map/ppermute | solution.py:19
  97.8 8.9 %collective-permute-start.15 = (bf16[1,4,64,128]{3,2,1,0:T(8,128)(2,1)S(1)}, bf16[1,4,64,128]{3,2,1,0:T(8,128)(2,1)S(1)}, u32[]{:S(2)}, u32[]{:S(2)}) collective-permute-start(bf16[1,4,64,128]{3,2,1,0:T(8,128)(2,1)S(1)} %bitcast.78), channel_id=1, source_target_pairs={{0,32},{32,64},{64,96},{96,128},{128,160},{160,192},{192,224},{224... | collective-permute-start | bytes 196616 | tf_op jit(solution)/shard_map/ppermute | solution.py:19
  103.7 9.6 %collective-permute-start.16 = (bf16[1,4,64,128]{3,2,1,0:T(8,128)(2,1)S(1)}, bf16[1,4,64,128]{3,2,1,0:T(8,128)(2,1)S(1)}, u32[]{:S(2)}, u32[]{:S(2)}) collective-permute-start(bf16[1,4,64,128]{3,2,1,0:T(8,128)(2,1)S(1)} %bitcast.79), channel_id=1, source_target_pairs={{32,0},{64,32},{96,64},{128,96},{160,128},{192,160},{224,192},{256... | collective-permute-start | bytes 196616 | tf_op jit(solution)/shard_map/ppermute | solution.py:19
  105.0 8.6 %collective-permute-start.17 = (bf16[1,4,64,128]{3,2,1,0:T(8,128)(2,1)S(1)}, bf16[1,4,64,128]{3,2,1,0:T(8,128)(2,1)S(1)}, u32[]{:S(2)}, u32[]{:S(2)}) collective-permute-start(bf16[1,4,64,128]{3,2,1,0:T(8,128)(2,1)S(1)} %bitcast.80), channel_id=1, source_target_pairs={{64,0},{96,32},{128,64},{160,96},{192,128},{224,160},{256,192},{28... | collective-permute-start | bytes 196616 | tf_op jit(solution)/shard_map/ppermute | solution.py:19
  106.3 20.4 %copy-start = (bf16[6,12,32,256]{3,2,1,0:T(8,128)(2,1)S(1)}, bf16[6,12,32,256]{3,2,1,0:T(8,128)(2,1)}, u32[]{:S(2)}) copy-start(bf16[6,12,32,256]{3,2,1,0:T(8,128)(2,1)} %select_maximum_fusion.refs_7_.refs_3_) | copy-start | bytes 3538948
  106.3 20.4 %copy-start.1 = (bf16[4,10,96,256]{3,2,1,0:T(8,128)(2,1)S(1)}, bf16[4,10,96,256]{3,2,1,0:T(8,128)(2,1)}, u32[]{:S(2)}) copy-start(bf16[4,10,96,256]{3,2,1,0:T(8,128)(2,1)} %get-tuple-element.22.refs_4_) | copy-start | bytes 5898244
  113.6 8.5 %collective-permute-start.18 = (bf16[5,2,64,128]{3,2,1,0:T(8,128)(2,1)S(1)}, bf16[5,2,64,128]{3,2,1,0:T(8,128)(2,1)S(1)}, u32[]{:S(2)}, u32[]{:S(2)}) collective-permute-start(bf16[5,2,64,128]{3,2,1,0:T(8,128)(2,1)S(1)} %get-tuple-element.79), channel_id=1, source_target_pairs={{0,4},{4,8},{8,12},{12,16},{16,20},{20,24},{24,28},{1,5},{5,9},{9,... | collective-permute-start | bytes 491528 | tf_op jit(solution)/shard_map/ppermute | solution.py:19
  119.9 6.6 %collective-permute-start.19 = (bf16[5,2,64,128]{3,2,1,0:T(8,128)(2,1)S(1)}, bf16[5,2,64,128]{3,2,1,0:T(8,128)(2,1)S(1)}, u32[]{:S(2)}, u32[]{:S(2)}) collective-permute-start(bf16[5,2,64,128]{3,2,1,0:T(8,128)(2,1)S(1)} %get-tuple-element.80), channel_id=1, source_target_pairs={{4,0},{8,4},{12,8},{16,12},{20,16},{24,20},{28,24},{5,1},{9,5},{13... | collective-permute-start | bytes 491528 | tf_op jit(solution)/shard_map/ppermute | solution.py:19
  136.0 7.5 %copy-start.5 = (bf16[32,3,3,3,32]{4,0,3,2,1:T(8,128)(2,1)S(1)}, bf16[32,3,3,3,32]{4,0,3,2,1:T(8,128)(2,1)}, u32[]{:S(2)}) copy-start(bf16[32,3,3,3,32]{4,0,3,2,1:T(8,128)(2,1)} %param.8) | copy-start | bytes 165892
  136.0 9.5 %copy-start.6 = (bf16[32,3,3,3,4]{0,4,3,2,1:T(4,128)(2,1)S(1)}, bf16[32,3,3,3,4]{0,4,3,2,1:T(4,128)(2,1)}, u32[]{:S(2)}) copy-start(bf16[32,3,3,3,4]{0,4,3,2,1:T(4,128)(2,1)} %param.7) | copy-start | bytes 20740
  136.1 9.6 %copy-start.3 = (f32[4,10,32,256]{3,2,1,0:T(8,128)S(1)}, f32[4,10,32,256]{3,2,1,0:T(8,128)}, u32[]{:S(2)}) copy-start(f32[4,10,32,256]{3,2,1,0:T(8,128)} %get-tuple-element.26.refs_2_) | copy-start | bytes 3932164
  137.0 21.6 %all-to-all-start.1 = ((bf16[32,56,128]{2,1,0:T(8,128)(2,1)}), bf16[32,56,128]{2,1,0:T(8,128)(2,1)S(1)}, u32[]{:S(2)}, u32[]{:S(2)}) async-start(bf16[32,56,128]{2,1,0:T(8,128)(2,1)} %pad_maximum_fusion.2), calls=%async_computation.1 | async-start | bytes 917504 | tf_op jit(solution)/shard_map/all_to_all | solution.py:261
  145.8 2.0 copy-start.2
  158.6 8.4 %collective-permute-start.20 = (bf16[56,128]{1,0:T(8,128)(2,1)S(1)}, bf16[56,128]{1,0:T(8,128)(2,1)S(1)}, u32[]{:S(2)}, u32[]{:S(2)}) collective-permute-start(bf16[56,128]{1,0:T(8,128)(2,1)S(1)} %get-tuple-element.101), channel_id=1, source_target_pairs={{0,32},{32,0},{64,96},{96,64},{128,160},{160,128},{192,224},{224,1... | collective-permute-start | bytes 43016 | tf_op jit(solution)/shard_map/ppermute | solution.py:294
  185.8 22.6 %all-to-all-start.3 = ((bf16[32,56,128]{2,1,0:T(8,128)(2,1)}), bf16[32,56,128]{2,1,0:T(8,128)(2,1)S(1)}, u32[]{:S(2)}, u32[]{:S(2)}) async-start(bf16[32,56,128]{2,1,0:T(8,128)(2,1)} %broadcast_in_dim.60), calls=%async_computation.3 | async-start | bytes 917504 | tf_op jit(solution)/shard_map/all_to_all | solution.py:261

commit v2 on v1

--- a/solution.py
+++ b/solution.py
@@ -91,7 +91,7 @@
 
 
 def forward_kernel(
-    sizes, offs, vol, w1, w2, w3, cot, pool, unread,
+    sizes, offs, vol, w1, w2, w3, cot, pool, unread_a, unread_b,
     skip_o, coarse_o, cgrad_o, craw_o, fpre_o, spre_o, t1_o, t2_o,
     t1, acc1, t2, acc2, fine, t3,
 ):
@@ -102,7 +102,9 @@
 
     def volume_taps(x, carry):
         for y in range(16):
-            store_taps(t1, (x, y), vol[x, y].astype(F32))
+            here = vol[x, y].astype(F32)
+            moved = [pltpu.roll(here, 1, 1), here, pltpu.roll(here, LANES - 1, 1)]
+            t1[x, y] = jnp.concatenate(moved + [jnp.zeros_like(here)], axis=0).astype(BF)
         return carry
 
     lax.fori_loop(0, 10, volume_taps, 0)
@@ -218,7 +220,7 @@
     lax.fori_loop(0, 4, one, 0)
 
 
-def first_kernel(sizes, offs, t5, fpre, t1, w2, w1, vgrad_o, fraw_o, acc5, t6, own6):
+def first_kernel(sizes, offs, t5, fpre, t1, w2, t6, thin_o, acc5, own6, fraw):
     nx, ny, nz = sizes
     ox, oy, oz = offs[0], offs[1], offs[2]
     fine_ok = lane_mask(LANES, oz - 8, 0, nz)
@@ -239,7 +241,19 @@
         for y in range(8):
             mine = t6[x + 1, y + 1, 32:64].astype(F32)
             own6[x + 2, y] = jnp.where(own_ok > 0.5, mine, 0.0).astype(BF)
-    weight_sums(fraw_o, own6, t1)
+    weight_sums(fraw, own6, t1)
+    place = lax.broadcasted_iota(jnp.int32, (48, 128), 0)
+    lane = lax.broadcasted_iota(jnp.int32, (48, 128), 1)
+    term = place & 15
+    column = jnp.where(term < 12, (place >> 4) * 12 + term, -200)
+    thin = jnp.zeros((32, 128), F32)
+    for i in range(3):
+        picked = jnp.where(lane == column + 36 * i, 1.0, 0.0).astype(BF)
+        thin = thin + dot(fraw[32 * i : 32 * i + 32].astype(BF), picked)
+    thin_o[...] = thin.astype(BF)
+
+
+def volume_kernel(t6, w1, vgrad_o):
     for x in range(2):
         for y in range(8):
             total = jnp.zeros((16, LANES), F32)
@@ -289,19 +303,6 @@
     return mine.reshape((count * blocks.shape[0],) + blocks.shape[1:])
 
 
-def total_over_line(part):
-    count = lax.axis_size("gx")
-    other = lax.ppermute(part, "gx", [(i, i ^ 1) for i in range(count)])
-    part = added(jnp.stack([part, other]))
-    groups = [list(range(n, count, 2)) for n in range(2)]
-    sent = jnp.broadcast_to(part, (count // 2,) + part.shape)
-    return added(
-        lax.all_to_all(
-            sent, "gx", split_axis=0, concat_axis=0, tiled=True, axis_index_groups=groups
-        )
-    )
-
-
 def weight_form(matrix, outputs, chans):
     return jnp.transpose(matrix.reshape(3, outputs, 3, 3, chans), (1, 0, 2, 3, 4))
 
@@ -317,11 +318,27 @@
     offs = jnp.stack([lax.axis_index(axis) * extent for axis, extent in zip(AXES, extents)])
     offs = offs.astype(jnp.int32)
 
-    line_volume = halo(volume, "gx", 1, 4)
-    wide_volume = halo(halo(line_volume, "gy", 2, 4), "gz", 3, 8)
-    wide_volume = jnp.pad(
-        jnp.transpose(wide_volume, (1, 2, 0, 3)), ((0, 0), (0, 0), (0, 12), (0, LANES - 144))
-    )
+    rows_volume = jnp.transpose(volume, (1, 2, 0, 3))
+    rows_cotangent = jnp.transpose(skip_cotangent, (1, 2, 0, 3))
+    both = jnp.concatenate([rows_cotangent, rows_volume], axis=2)
+    chans = skip_cotangent.shape[0]
+    near = (shifted(both, "gx", 1), shifted(both, "gx", -1))
+    far = (shifted(rows_volume, "gx", 2), shifted(rows_volume, "gx", -2))
+    wide_volume = jnp.concatenate(
+        [far[0], near[0][:, :, chans:], rows_volume, near[1][:, :, chans:], far[1]], axis=0
+    )
+    wide_volume = halo(halo(wide_volume, "gy", 1, 4), "gz", 3, 8)
+    wide_volume = jnp.pad(wide_volume, ((0, 0), (0, 0), (0, 0), (0, LANES - 144)))
+    tall_cotangent = jnp.concatenate(
+        [near[0][:, :, :chans], rows_cotangent, near[1][:, :, :chans]], axis=0
+    )
+    tall_cotangent = halo(tall_cotangent, "gy", 1, 2)
+    edges = (
+        shifted(tall_cotangent[..., -2:], "gz", 1),
+        shifted(tall_cotangent[..., :2], "gz", -1),
+    )
+    wide_cotangent = jnp.concatenate([edges[0], tall_cotangent, edges[1]], axis=3)
+    wide_cotangent = jnp.pad(wide_cotangent, ((0, 0), (0, 0), (0, 0), (6, LANES - 138)))
     sides = counts[2]
     depth = coarse_cotangent.shape[3] // sides
     guarded = jnp.pad(coarse_cotangent[:, 0], ((0, 0), (0, 0), (2, 2)))
@@ -329,17 +346,13 @@
     returned = swap(sent, "gz")
     returned = jnp.transpose(returned, (2, 0, 1, 3)).reshape(4, 64, depth + 4)
     returned = jnp.pad(returned, ((0, 0), (0, 0), (2, 128 - 70)))
-    later = line_volume[0, 0, 0, 0] * 0 + line_volume[0, 9, 0, 0] * 0
-    rows_cotangent = jnp.transpose(skip_cotangent, (1, 2, 0, 3)) + later
-    wide_cotangent = halo(halo(halo(rows_cotangent, "gx", 0, 2), "gy", 1, 2), "gz", 3, 2)
-    wide_cotangent = jnp.pad(wide_cotangent, ((0, 0), (0, 0), (0, 0), (6, LANES - 138)))
-
     fine_place = lax.broadcasted_iota(jnp.int32, (LANES, 128), 0)
     coarse_place = lax.broadcasted_iota(jnp.int32, (LANES, 128), 1)
     pool = jnp.where(fine_place // 2 == coarse_place, 1.0, 0.0).astype(BF)
     spread = jnp.transpose(pool) * 0.125
 
-    thin_first = jnp.pad(w_first, ((0, 0), (0, 0), (0, 0), (0, 0), (0, 12)))
+    thin_first = jnp.transpose(w_first, (1, 0, 2, 3, 4)).reshape(96, 3, 12)
+    thin_first = jnp.pad(thin_first, ((0, 0), (0, 0), (0, 4))).reshape(96, 48)
     smem = pl.BlockSpec(memory_space=pltpu.SMEM)
     vmem = pl.BlockSpec(memory_space=pltpu.VMEM)
     skip, coarse_local, coarse_grad, coarse_raw, first_pre, second_pre, taps1, taps2 = (
@@ -352,13 +365,13 @@
                 shape((192, 288), F32),
                 shape((4, 10, 32, LANES), F32),
                 shape((6, 12, 32, LANES), F32),
-                shape((4, 10, 48, LANES), BF),
+                shape((4, 10, 16, LANES), BF),
                 shape((4, 10, 96, LANES), BF),
             ),
-            in_specs=[smem] + [vmem] * 6 + [pl.BlockSpec(memory_space=pl.ANY)],
+            in_specs=[smem] + [vmem] * 6 + [pl.BlockSpec(memory_space=pl.ANY)] * 2,
             out_specs=(vmem,) * 8,
             scratch_shapes=[
-                pltpu.VMEM((10, 16, 48, LANES), BF),
+                pltpu.VMEM((10, 16, 16, LANES), BF),
                 pltpu.VMEM((12, 16, 32, LANES), F32),
                 pltpu.VMEM((10, 16, 96, LANES), BF),
                 pltpu.VMEM((12, 16, 32, LANES), F32),
@@ -373,12 +386,12 @@
         )(
             offs,
             wide_volume,
-            stacked(thin_first).reshape(96, 144),
+            thin_first,
             stacked(w_second).reshape(96, 288),
             stacked(w_coarse),
             returned,
             pool,
-            wide_cotangent,
+            *edges,
         )
     )
     wide_grad = halo(halo(coarse_grad[None], "gx", 0, 2), "gy", 1, 2)
@@ -420,30 +433,34 @@
         jnp.concatenate([rows.reshape(count, share, 128), plane_blocks(blocks)], axis=1), plane
     )
 
-    back_first = jnp.pad(flipped(w_first), ((0, 12),) + ((0, 0),) * 4)
-    volume_grad, first_raw = pl.pallas_call(
+    taps6, thin = pl.pallas_call(
         lambda *refs: first_kernel(sizes, *refs),
-        out_shape=(shape((2, 8, 16, 128), BF), shape((96, 144), F32)),
-        in_specs=[smem] + [vmem] * 5,
+        out_shape=(shape((4, 10, 96, LANES), BF), shape((32, 128), BF)),
+        in_specs=[smem] + [vmem] * 4,
         out_specs=(vmem,) * 2,
         scratch_shapes=[
             pltpu.VMEM((8, 12, 32, LANES), F32),
-            pltpu.VMEM((4, 10, 96, LANES), BF),
             pltpu.VMEM((6, 8, 32, LANES), BF),
+            pltpu.VMEM((96, 48), F32),
         ],
         compiler_params=pltpu.CompilerParams(vmem_limit_bytes=48 * 2**20),
         cost_estimate=pl.CostEstimate(
             flops=2 * 10**9, bytes_accessed=10 * 10**6, transcendentals=10**6
         ),
         name="first",
-    )(
-        offs,
-        taps5,
-        first_pre,
-        taps1,
-        stacked(flipped(w_second)).reshape(96, 288),
-        stacked(back_first),
-    )
+    )(offs, taps5, first_pre, taps1, stacked(flipped(w_second)).reshape(96, 288))
+    back_first = jnp.pad(flipped(w_first), ((0, 12),) + ((0, 0),) * 4)
+    volume_grad = pl.pallas_call(
+        volume_kernel,
+        out_shape=shape((2, 8, 16, 128), BF),
+        in_specs=[vmem] * 2,
+        out_specs=vmem,
+        compiler_params=pltpu.CompilerParams(vmem_limit_bytes=48 * 2**20),
+        cost_estimate=pl.CostEstimate(
+            flops=10**9, bytes_accessed=4 * 10**6, transcendentals=0
+        ),
+        name="volume",
+    )(taps6, stacked(back_first))
 
     part = added(arrived[:, :share])
     own_row = lax.axis_index("gy") * sides
@@ -452,9 +469,8 @@
     coarse = coarse.reshape(sides, 4, 64 // sides, depth)
     coarse = jnp.transpose(coarse, (2, 1, 0, 3)).reshape(64 // sides, 1, 4, sides * depth)
 
-    thin = first_raw.reshape(3, 32, 9, 16)[..., :4].reshape(3, 32, 36).astype(BF)
-    thin = jnp.pad(jnp.concatenate([thin[0], thin[1], thin[2]], axis=1), ((0, 0), (0, 20)))
-    part = total_over_line(jnp.concatenate([part, thin], axis=0))
+    part = jnp.concatenate([part, thin], axis=0)
+    part = added(swap(jnp.broadcast_to(part, (counts[0],) + part.shape), "gx"))
     whole = swap(jnp.broadcast_to(part, (count,) + part.shape), plane)
     second, wide = gathered_rows(whole[:, :share].reshape(count * share, 128).astype(F32))
     thin = jnp.sum(whole[:, share:].astype(F32), axis=0)

time: 213 us -> 193 us (0.906)
  starting transfers between devices: 94.8 us -> 72.2 us
  blocking collectives: 17.7 us -> 27.3 us
  local copies, waits for them, and re-layouts: 22.6 us -> 18.1 us
    ppermute x20 -> x18, starting transfers between devices: 71.7 us -> 58.9 us  [shifted(): return lax.ppermute(block, axis, pairs)]
    all_to_all x1, blocking collectives: 17.7 us -> 27.3 us  [swap(): return lax.all_to_all(blocks, axes, split_axis=0, concat_axis=0, tiled=True)]
    all_to_all x3, waiting for transfers between devices: 15.7 us -> 23 us  [swap(): return lax.all_to_all(blocks, axes, split_axis=0, concat_axis=0, tiled=True)]
    all_to_all x3, starting transfers between devices: 18.3 us -> 13.3 us  [swap(): return lax.all_to_all(blocks, axes, split_axis=0, concat_axis=0, tiled=True)]
    ppermute x1 -> x0, starting transfers between devices: 4.84 us -> none  [total_over_line(): other = lax.ppermute(part, 'gx', [(i, i ^ 1) for i in range(count)])]
    ppermute x1 -> x0, waiting for transfers between devices: 3.52 us -> none  [total_over_line(): other = lax.ppermute(part, 'gx', [(i, i ^ 1) for i in range(count)])]
    ppermute x20 -> x18, waiting for transfers between devices: 13.8 us -> 10.7 us  [shifted(): return lax.ppermute(block, axis, pairs)]
    concatenate x4, other arithmetic: 3.09 us -> 0.81 us  [halo(): return jnp.concatenate(before + [cells] + after, axis=dim)]
  transfers between devices with their start and end apart: 24 -> 21, of which waited for: 9 -> 8; matrix products, arithmetic and copies ran while one was open for 9% -> 8% of each run, Pallas kernels for 3% -> 4%
where the time goes in v2:
time: 193 us; the launch traced here: 192 us
  starting transfers between devices  72.2 us (37%)
  waiting for transfers between devices  33.7 us (17%)
  Pallas kernels  33.3 us (17%)
  blocking collectives  27.3 us (14%)
  local copies, waits for them, and re-layouts  18.1 us (9%)
  other arithmetic  5.76 us (3%)
    ppermute x18, starting transfers between devices, shifted(): return lax.ppermute(block, axis, pairs)  58.9 us
    all_to_all x1, blocking collectives, swap(): return lax.all_to_all(blocks, axes, split_axis=0, concat_axis=0, tiled=True)  27.3 us
    all_to_all x3, waiting for transfers between devices, swap(): return lax.all_to_all(blocks, axes, split_axis=0, concat_axis=0, tiled=True)  23 us
    pallas_call x1, Pallas kernels, local(): pl.pallas_call(lambda *refs: forward_kernel(sizes, *refs), out_shape=(sha...  15.6 us
    all_to_all x3, starting transfers between devices, swap(): return lax.all_to_all(blocks, axes, split_axis=0, concat_axis=0, tiled=True)  13.3 us
    ppermute x18, waiting for transfers between devices, shifted(): return lax.ppermute(block, axis, pairs)  10.7 us
    pallas_call x1, Pallas kernels, local(): pl.pallas_call(lambda *refs: second_kernel(sizes, *refs), out_shape=(shap...  9.28 us
    pallas_call x1, Pallas kernels, local(): pl.pallas_call(lambda *refs: first_kernel(sizes, *refs), out_shape=(shape...  6.96 us
  transfers between devices with their start and end apart: 21, of which 8 were waited for; matrix products, arithmetic and copies ran while one was open for 8% of the time, Pallas kernels for 4%

profile of v2, /device:TPU:1, one launch (start us, length us, event | category | flops | bytes accessed | tf_op | source)
XLA Modules:
  0.0 191.8 jit_solution(12050159535934162048)
XLA Ops:
  1.4 4.0 %collective-permute-start = (bf16[2,8,4,128]{3,2,1,0:T(4,128)(2,1)S(1)}, bf16[2,8,4,128]{3,2,1,0:T(4,128)(2,1)S(1)}, u32[]{:S(2)}, u32[]{:S(2)}) collective-permute-start(bf16[2,8,4,128]{3,2,1,0:T(4,128)(2,1)S(1)} %bitcast.94), channel_id=1, source_target_pairs={{0,64},{32,96},{64,128},{96,160},{128,192},{160,224},{192,256},{22... | collective-permute-start | bytes 49160 | tf_op jit(solution)/shard_map/ppermute | solution.py:19
  6.4 10.6 %collective-permute-start.1 = (bf16[2,8,36,128]{3,2,1,0:T(8,128)(2,1)S(1)}, bf16[2,8,36,128]{3,2,1,0:T(8,128)(2,1)S(1)}, u32[]{:S(2)}, u32[]{:S(2)}) collective-permute-start(bf16[2,8,36,128]{3,2,1,0:T(8,128)(2,1)S(1)} %pad_maximum_fusion.7), channel_id=1, source_target_pairs={{0,32},{32,64},{64,96},{96,128},{128,160},{160,192},{192,224},{224... | collective-permute-start | bytes 442376 | tf_op jit(solution)/shard_map/ppermute | solution.py:19
  17.1 1.3 collective-permute-start.2
  18.4 1.3 collective-permute-start.3
  21.4 4.3 %all-to-all-start = ((bf16[4,16,4,68]{3,2,1,0:T(4,128)(2,1)}), bf16[4,16,4,68]{3,2,1,0:T(4,128)(2,1)S(1)}, u32[]{:S(2)}, u32[]{:S(2)}) async-start(bf16[4,16,4,68]{3,2,1,0:T(4,128)(2,1)} %pad_maximum_fusion.12), calls=%async_computation | async-start | bytes 131072 | tf_op jit(solution)/shard_map/all_to_all | solution.py:275
  29.2 5.4 %all-to-all-done = bf16[4,16,4,68]{3,2,1,0:T(4,128)(2,1)S(1)} async-done(((bf16[4,16,4,68]{3,2,1,0:T(4,128)(2,1)}), bf16[4,16,4,68]{3,2,1,0:T(4,128)(2,1)S(1)}, u32[]{:S(2)}, u32[]{:S(2)}) %all-to-all-start) | async-done | bytes 34848 | tf_op jit(solution)/shard_map/all_to_all | solution.py:275
  34.9 3.5 %collective-permute-start.4 = (bf16[10,4,4,128]{3,2,1,0:T(4,128)(2,1)S(1)}, bf16[10,4,4,128]{3,2,1,0:T(4,128)(2,1)S(1)}, u32[]{:S(2)}, u32[]{:S(2)}) collective-permute-start(bf16[10,4,4,128]{3,2,1,0:T(4,128)(2,1)S(1)} %get-tuple-element.80), channel_id=1, source_target_pairs={{0,4},{4,8},{8,12},{12,16},{16,20},{20,24},{24,28},{1,5},{5,9},{9,... | collective-permute-start | bytes 122888 | tf_op jit(solution)/shard_map/ppermute | solution.py:19
  38.4 1.9 %collective-permute-start.5 = (bf16[10,4,4,128]{3,2,1,0:T(4,128)(2,1)S(1)}, bf16[10,4,4,128]{3,2,1,0:T(4,128)(2,1)S(1)}, u32[]{:S(2)}, u32[]{:S(2)}) collective-permute-start(bf16[10,4,4,128]{3,2,1,0:T(4,128)(2,1)S(1)} %get-tuple-element.81), channel_id=1, source_target_pairs={{4,0},{8,4},{12,8},{16,12},{20,16},{24,20},{28,24},{5,1},{9,5},{13... | collective-permute-start | bytes 122888 | tf_op jit(solution)/shard_map/ppermute | solution.py:19
  40.4 3.6 %collective-permute-start.8 = (bf16[6,2,32,128]{3,2,1,0:T(8,128)(2,1)S(1)}, bf16[6,2,32,128]{3,2,1,0:T(8,128)(2,1)S(1)}, u32[]{:S(2)}, u32[]{:S(2)}) collective-permute-start(bf16[6,2,32,128]{3,2,1,0:T(8,128)(2,1)S(1)} %get-tuple-element.68), channel_id=1, source_target_pairs={{0,4},{4,8},{8,12},{12,16},{16,20},{20,24},{24,28},{1,5},{5,9},{9,... | collective-permute-start | bytes 294920 | tf_op jit(solution)/shard_map/ppermute | solution.py:19
  44.1 1.9 %collective-permute-start.9 = (bf16[6,2,32,128]{3,2,1,0:T(8,128)(2,1)S(1)}, bf16[6,2,32,128]{3,2,1,0:T(8,128)(2,1)S(1)}, u32[]{:S(2)}, u32[]{:S(2)}) collective-permute-start(bf16[6,2,32,128]{3,2,1,0:T(8,128)(2,1)S(1)} %get-tuple-element.69), channel_id=1, source_target_pairs={{4,0},{8,4},{12,8},{16,12},{20,16},{24,20},{28,24},{5,1},{9,5},{13... | collective-permute-start | bytes 294920 | tf_op jit(solution)/shard_map/ppermute | solution.py:19
  46.3 1.9 %collective-permute-start.6 = (bf16[10,16,4,8]{3,2,1,0:T(4,128)(2,1)S(1)}, bf16[10,16,4,8]{3,2,1,0:T(4,128)(2,1)S(1)}, u32[]{:S(2)}, u32[]{:S(2)}) collective-permute-start(bf16[10,16,4,8]{3,2,1,0:T(4,128)(2,1)S(1)} %get-tuple-element.76), channel_id=1, source_target_pairs={{0,1},{1,2},{2,3},{4,5},{5,6},{6,7},{8,9},{9,10},{10,11},{12,13},{... | collective-permute-start | bytes 30728 | tf_op jit(solution)/shard_map/ppermute | solution.py:19
  50.9 3.6 %collective-permute-start.10 = (bf16[6,12,32,2]{2,3,1,0:T(2,128)(2,1)S(1)}, bf16[6,12,32,2]{2,3,1,0:T(2,128)(2,1)S(1)}, u32[]{:S(2)}, u32[]{:S(2)}) collective-permute-start(bf16[6,12,32,2]{2,3,1,0:T(2,128)(2,1)S(1)} %copy.93), channel_id=1, source_target_pairs={{0,1},{1,2},{2,3},{4,5},{5,6},{6,7},{8,9},{9,10},{10,11},{12,13},{... | collective-permute-start | bytes 27656 | tf_op jit(solution)/shard_map/ppermute | solution.py:19
  56.8 1.3 copy.97.refs_7_
  58.1 1.5 collective-permute-done.11
  59.6 1.3 copy.98.refs_8_
  60.9 15.6 %forward.1 = (bf16[2,8,32,128]{3,2,1,0:T(8,128)(2,1)S(1)}, bf16[4,64,128]{2,1,0:T(8,128)(2,1)S(1)}, bf16[4,64,128]{2,1,0:T(8,128)(2,1)S(1)}, f32[192,288]{1,0:T(...) custom-call(s32[3]{0:T(128)S(1)} %pad_add_fusion.refs_0_, ...), custom_call_target="tpu_custom_call" | custom-call | flops 4000000000 | bytes 12000000 | tf_op jit(solution)/shard_map/forward/pallas_call | solution.py:359
  76.6 4.4 %collective-permute-start.12 = (bf16[1,4,64,128]{3,2,1,0:T(8,128)(2,1)S(1)}, bf16[1,4,64,128]{3,2,1,0:T(8,128)(2,1)S(1)}, u32[]{:S(2)}, u32[]{:S(2)}) collective-permute-start(bf16[1,4,64,128]{3,2,1,0:T(8,128)(2,1)S(1)} %bitcast.69), channel_id=1, source_target_pairs={{0,64},{32,96},{64,128},{96,160},{128,192},{160,224},{192,256},{22... | collective-permute-start | bytes 196616 | tf_op jit(solution)/shard_map/ppermute | solution.py:19
  81.0 6.4 %collective-permute-start.13 = (bf16[1,4,64,128]{3,2,1,0:T(8,128)(2,1)S(1)}, bf16[1,4,64,128]{3,2,1,0:T(8,128)(2,1)S(1)}, u32[]{:S(2)}, u32[]{:S(2)}) collective-permute-start(bf16[1,4,64,128]{3,2,1,0:T(8,128)(2,1)S(1)} %bitcast.70), channel_id=1, source_target_pairs={{0,32},{32,64},{64,96},{96,128},{128,160},{160,192},{192,224},{224... | collective-permute-start | bytes 196616 | tf_op jit(solution)/shard_map/ppermute | solution.py:19
  90.2 1.9 select_maximum_fusion.refs_3_
  92.4 4.0 %collective-permute-done.14 = bf16[1,4,64,128]{3,2,1,0:T(8,128)(2,1)S(1)} collective-permute-done((bf16[1,4,64,128]{3,2,1,0:T(8,128)(2,1)S(1)}, bf16[1,4,64,128]{3,2,1,0:T(8,128)(2,1)S(1)}, u32[]{:S(2)}, u32[]{:S(2)}) %collective-permute-start.14) | collective-permute-done | bytes 65568 | tf_op jit(solution)/shard_map/ppermute | solution.py:19
  96.4 7.3 %collective-permute-start.16 = (bf16[5,2,64,128]{3,2,1,0:T(8,128)(2,1)S(1)}, bf16[5,2,64,128]{3,2,1,0:T(8,128)(2,1)S(1)}, u32[]{:S(2)}, u32[]{:S(2)}) collective-permute-start(bf16[5,2,64,128]{3,2,1,0:T(8,128)(2,1)S(1)} %get-tuple-element.70), channel_id=1, source_target_pairs={{0,4},{4,8},{8,12},{12,16},{16,20},{20,24},{24,28},{1,5},{5,9},{9,... | collective-permute-start | bytes 491528 | tf_op jit(solution)/shard_map/ppermute | solution.py:19
  103.7 1.9 %collective-permute-start.17 = (bf16[5,2,64,128]{3,2,1,0:T(8,128)(2,1)S(1)}, bf16[5,2,64,128]{3,2,1,0:T(8,128)(2,1)S(1)}, u32[]{:S(2)}, u32[]{:S(2)}) collective-permute-start(bf16[5,2,64,128]{3,2,1,0:T(8,128)(2,1)S(1)} %get-tuple-element.71), channel_id=1, source_target_pairs={{4,0},{8,4},{12,8},{16,12},{20,16},{24,20},{28,24},{5,1},{9,5},{13... | collective-permute-start | bytes 491528 | tf_op jit(solution)/shard_map/ppermute | solution.py:19
  106.0 4.4 %collective-permute-done.17 = bf16[5,2,64,128]{3,2,1,0:T(8,128)(2,1)S(1)} collective-permute-done((bf16[5,2,64,128]{3,2,1,0:T(8,128)(2,1)S(1)}, bf16[5,2,64,128]{3,2,1,0:T(8,128)(2,1)S(1)}, u32[]{:S(2)}, u32[]{:S(2)}) %collective-permute-start.17) | collective-permute-done | bytes 163872 | tf_op jit(solution)/shard_map/ppermute | solution.py:19
  110.5 9.3 %second.1 = (bf16[6,12,96,256]{3,2,1,0:T(8,128)(2,1)}, f32[96,288]{1,0:T(8,128)S(1)}) custom-call(s32[3]{0:T(128)S(1)} %pad_add_fusion.refs_0_, bf16[5,8,64,128]{3,2,1,0:T(8,128)(2,1)S(1)} %pad_maximum_fusion.refs_1_, f32[6,12,32,256]{3,2,1,0:T(8,128)} %get-tuple-element.21.refs_2_, bf16[6,12,32,256]{3,2,1,0:T(8,128)(2,1)S(1)} %select_maximum_fusion.refs_3_, ...), custom_call_target="tpu_custom_call" | custom-call | flops 1000000000 | bytes 10000000 | tf_op jit(solution)/shard_map/second/pallas_call | solution.py:398
  120.7 5.1 %all-to-all-start.1 = ((bf16[32,56,128]{2,1,0:T(8,128)(2,1)}), bf16[32,56,128]{2,1,0:T(8,128)(2,1)S(1)}, u32[]{:S(2)}, u32[]{:S(2)}) async-start(bf16[32,56,128]{2,1,0:T(8,128)(2,1)} %pad_maximum_fusion.2), calls=%async_computation.1 | async-start | bytes 917504 | tf_op jit(solution)/shard_map/all_to_all | solution.py:275
  126.2 1.3 copy-done.1
  127.5 7.0 %first.1 = (bf16[4,10,96,256]{3,2,1,0:T(8,128)(2,1)S(1)}, bf16[32,128]{1,0:T(8,128)(2,1)S(1)}) custom-call(s32[3]{0:T(128)S(1)} %pad_add_fusion.refs_0_, bf16[6,12,96,256]{3,2,1,0:T(8,128)(2,1)} %get-tuple-element.25.refs_1_, f32[4,10,32,256]{3,2,1,0:T(8,128)S(1)} %copy-done.1, bf16[4,10,16,256]{3,2,1,0:T(8,128)(2,1)S(1)} %get-tuple-element.27.refs_3_, ...), custom_call_target="tpu_custom_call" | custom-call | flops 2000000000 | bytes 10000000 | tf_op jit(solution)/shard_map/first/pallas_call | solution.py:436
  134.5 6.4 %all-to-all-done.1 = bf16[32,56,128]{2,1,0:T(8,128)(2,1)S(1)} async-done(((bf16[32,56,128]{2,1,0:T(8,128)(2,1)}), bf16[32,56,128]{2,1,0:T(8,128)(2,1)S(1)}, u32[]{:S(2)}, u32[]{:S(2)}) %all-to-all-start.1) | async-done | bytes 458784 | tf_op jit(solution)/shard_map/all_to_all | solution.py:275
  141.0 27.3 %all_to_all.20 = bf16[16,56,128]{2,1,0:T(8,128)(2,1)S(1)} all-to-all(bf16[16,56,128]{2,1,0:T(8,128)(2,1)S(1)} %broadcast_in_dim.59), channel_id=1, replica_groups=mesh['gx'=16,'gy'=8,'gz'=4] {'gx'}, dimensions={0} | all-to-all | bytes 458752 | tf_op jit(solution)/shard_map/all_to_all | solution.py:275
  169.2 4.0 %all-to-all-start.3 = ((bf16[32,56,128]{2,1,0:T(8,128)(2,1)}), bf16[32,56,128]{2,1,0:T(8,128)(2,1)S(1)}, u32[]{:S(2)}, u32[]{:S(2)}) async-start(bf16[32,56,128]{2,1,0:T(8,128)(2,1)} %broadcast_in_dim.60), calls=%async_computation.3 | async-start | bytes 917504 | tf_op jit(solution)/shard_map/all_to_all | solution.py:275
  174.1 1.4 volume.1
  177.1 11.2 %all-to-all-done.3 = bf16[32,56,128]{2,1,0:T(8,128)(2,1)S(1)} async-done(((bf16[32,56,128]{2,1,0:T(8,128)(2,1)}), bf16[32,56,128]{2,1,0:T(8,128)(2,1)S(1)}, u32[]{:S(2)}, u32[]{:S(2)}) %all-to-all-start.3) | async-done | bytes 458784 | tf_op jit(solution)/shard_map/all_to_all | solution.py:275
  (135 shorter events, 23.9 us)
Async XLA Ops:
  0.6 27.6 %copy-start.4 = (bf16[64,3,3,3,32]{0,4,3,2,1:T(8,128)(2,1)S(1)}, bf16[64,3,3,3,32]{0,4,3,2,1:T(8,128)(2,1)}, u32[]{:S(2)}) copy-start(bf16[64,3,3,3,32]{0,4,3,2,1:T(8,128)(2,1)} %param.9) | copy-start | bytes 331780
  0.6 27.8 %copy-start.6 = (bf16[32,3,3,3,4]{0,4,3,2,1:T(4,128)(2,1)S(1)}, bf16[32,3,3,3,4]{0,4,3,2,1:T(4,128)(2,1)}, u32[]{:S(2)}) copy-start(bf16[32,3,3,3,4]{0,4,3,2,1:T(4,128)(2,1)} %param.7) | copy-start | bytes 20740
  1.4 27.8 %collective-permute-start = (bf16[2,8,4,128]{3,2,1,0:T(4,128)(2,1)S(1)}, bf16[2,8,4,128]{3,2,1,0:T(4,128)(2,1)S(1)}, u32[]{:S(2)}, u32[]{:S(2)}) collective-permute-start(bf16[2,8,4,128]{3,2,1,0:T(4,128)(2,1)S(1)} %bitcast.94), channel_id=1, source_target_pairs={{0,64},{32,96},{64,128},{96,160},{128,192},{160,224},{192,256},{22... | collective-permute-start | bytes 49160 | tf_op jit(solution)/shard_map/ppermute | solution.py:19
  6.4 28.4 %copy-start.7 = (bf16[4,2,8,128]{3,2,1,0:T(8,128)(2,1)S(1)}, bf16[4,2,8,128]{3,2,1,0:T(8,128)(2,1)}, u32[]{:S(2)}) copy-start(bf16[4,2,8,128]{3,2,1,0:T(8,128)(2,1)} %param.6) | copy-start | bytes 49156
  6.4 28.3 %collective-permute-start.1 = (bf16[2,8,36,128]{3,2,1,0:T(8,128)(2,1)S(1)}, bf16[2,8,36,128]{3,2,1,0:T(8,128)(2,1)S(1)}, u32[]{:S(2)}, u32[]{:S(2)}) collective-permute-start(bf16[2,8,36,128]{3,2,1,0:T(8,128)(2,1)S(1)} %pad_maximum_fusion.7), channel_id=1, source_target_pairs={{0,32},{32,64},{64,96},{96,128},{128,160},{160,192},{192,224},{224... | collective-permute-start | bytes 442376 | tf_op jit(solution)/shard_map/ppermute | solution.py:19
  17.1 17.7 %collective-permute-start.2 = (bf16[2,8,36,128]{3,2,1,0:T(8,128)(2,1)S(1)}, bf16[2,8,36,128]{3,2,1,0:T(8,128)(2,1)S(1)}, u32[]{:S(2)}, u32[]{:S(2)}) collective-permute-start(bf16[2,8,36,128]{3,2,1,0:T(8,128)(2,1)S(1)} %pad_maximum_fusion.7), channel_id=1, source_target_pairs={{32,0},{64,32},{96,64},{128,96},{160,128},{192,160},{224,192},{256... | collective-permute-start | bytes 442376 | tf_op jit(solution)/shard_map/ppermute | solution.py:19
  18.4 16.5 %collective-permute-start.3 = (bf16[2,8,4,128]{3,2,1,0:T(4,128)(2,1)S(1)}, bf16[2,8,4,128]{3,2,1,0:T(4,128)(2,1)S(1)}, u32[]{:S(2)}, u32[]{:S(2)}) collective-permute-start(bf16[2,8,4,128]{3,2,1,0:T(4,128)(2,1)S(1)} %bitcast.96), channel_id=1, source_target_pairs={{64,0},{96,32},{128,64},{160,96},{192,128},{224,160},{256,192},{28... | collective-permute-start | bytes 49160 | tf_op jit(solution)/shard_map/ppermute | solution.py:19
  21.4 13.3 %all-to-all-start = ((bf16[4,16,4,68]{3,2,1,0:T(4,128)(2,1)}), bf16[4,16,4,68]{3,2,1,0:T(4,128)(2,1)S(1)}, u32[]{:S(2)}, u32[]{:S(2)}) async-start(bf16[4,16,4,68]{3,2,1,0:T(4,128)(2,1)} %pad_maximum_fusion.12), calls=%async_computation | async-start | bytes 131072 | tf_op jit(solution)/shard_map/all_to_all | solution.py:275
  34.9 11.1 %collective-permute-start.4 = (bf16[10,4,4,128]{3,2,1,0:T(4,128)(2,1)S(1)}, bf16[10,4,4,128]{3,2,1,0:T(4,128)(2,1)S(1)}, u32[]{:S(2)}, u32[]{:S(2)}) collective-permute-start(bf16[10,4,4,128]{3,2,1,0:T(4,128)(2,1)S(1)} %get-tuple-element.80), channel_id=1, source_target_pairs={{0,4},{4,8},{8,12},{12,16},{16,20},{20,24},{24,28},{1,5},{5,9},{9,... | collective-permute-start | bytes 122888 | tf_op jit(solution)/shard_map/ppermute | solution.py:19
  38.4 7.6 %collective-permute-start.5 = (bf16[10,4,4,128]{3,2,1,0:T(4,128)(2,1)S(1)}, bf16[10,4,4,128]{3,2,1,0:T(4,128)(2,1)S(1)}, u32[]{:S(2)}, u32[]{:S(2)}) collective-permute-start(bf16[10,4,4,128]{3,2,1,0:T(4,128)(2,1)S(1)} %get-tuple-element.81), channel_id=1, source_target_pairs={{4,0},{8,4},{12,8},{16,12},{20,16},{24,20},{28,24},{5,1},{9,5},{13... | collective-permute-start | bytes 122888 | tf_op jit(solution)/shard_map/ppermute | solution.py:19
  40.4 9.1 %collective-permute-start.8 = (bf16[6,2,32,128]{3,2,1,0:T(8,128)(2,1)S(1)}, bf16[6,2,32,128]{3,2,1,0:T(8,128)(2,1)S(1)}, u32[]{:S(2)}, u32[]{:S(2)}) collective-permute-start(bf16[6,2,32,128]{3,2,1,0:T(8,128)(2,1)S(1)} %get-tuple-element.68), channel_id=1, source_target_pairs={{0,4},{4,8},{8,12},{12,16},{16,20},{20,24},{24,28},{1,5},{5,9},{9,... | collective-permute-start | bytes 294920 | tf_op jit(solution)/shard_map/ppermute | solution.py:19
  44.1 5.9 %collective-permute-start.9 = (bf16[6,2,32,128]{3,2,1,0:T(8,128)(2,1)S(1)}, bf16[6,2,32,128]{3,2,1,0:T(8,128)(2,1)S(1)}, u32[]{:S(2)}, u32[]{:S(2)}) collective-permute-start(bf16[6,2,32,128]{3,2,1,0:T(8,128)(2,1)S(1)} %get-tuple-element.69), channel_id=1, source_target_pairs={{4,0},{8,4},{12,8},{16,12},{20,16},{24,20},{28,24},{5,1},{9,5},{13... | collective-permute-start | bytes 294920 | tf_op jit(solution)/shard_map/ppermute | solution.py:19
  46.3 9.9 %collective-permute-start.6 = (bf16[10,16,4,8]{3,2,1,0:T(4,128)(2,1)S(1)}, bf16[10,16,4,8]{3,2,1,0:T(4,128)(2,1)S(1)}, u32[]{:S(2)}, u32[]{:S(2)}) collective-permute-start(bf16[10,16,4,8]{3,2,1,0:T(4,128)(2,1)S(1)} %get-tuple-element.76), channel_id=1, source_target_pairs={{0,1},{1,2},{2,3},{4,5},{5,6},{6,7},{8,9},{9,10},{10,11},{12,13},{... | collective-permute-start | bytes 30728 | tf_op jit(solution)/shard_map/ppermute | solution.py:19
  48.3 8.0 %collective-permute-start.7 = (bf16[10,16,4,8]{3,2,1,0:T(4,128)(2,1)S(1)}, bf16[10,16,4,8]{3,2,1,0:T(4,128)(2,1)S(1)}, u32[]{:S(2)}, u32[]{:S(2)}) collective-permute-start(bf16[10,16,4,8]{3,2,1,0:T(4,128)(2,1)S(1)} %get-tuple-element.77), channel_id=1, source_target_pairs={{1,0},{2,1},{3,2},{5,4},{6,5},{7,6},{9,8},{10,9},{11,10},{13,12},{... | collective-permute-start | bytes 30728 | tf_op jit(solution)/shard_map/ppermute | solution.py:19
  50.9 5.9 %collective-permute-start.10 = (bf16[6,12,32,2]{2,3,1,0:T(2,128)(2,1)S(1)}, bf16[6,12,32,2]{2,3,1,0:T(2,128)(2,1)S(1)}, u32[]{:S(2)}, u32[]{:S(2)}) collective-permute-start(bf16[6,12,32,2]{2,3,1,0:T(2,128)(2,1)S(1)} %copy.93), channel_id=1, source_target_pairs={{0,1},{1,2},{2,3},{4,5},{5,6},{6,7},{8,9},{9,10},{10,11},{12,13},{... | collective-permute-start | bytes 27656 | tf_op jit(solution)/shard_map/ppermute | solution.py:19
  54.9 4.7 %collective-permute-start.11 = (bf16[6,12,32,2]{2,3,1,0:T(2,128)(2,1)S(1)}, bf16[6,12,32,2]{2,3,1,0:T(2,128)(2,1)S(1)}, u32[]{:S(2)}, u32[]{:S(2)}) collective-permute-start(bf16[6,12,32,2]{2,3,1,0:T(2,128)(2,1)S(1)} %copy.94), channel_id=1, source_target_pairs={{1,0},{2,1},{3,2},{5,4},{6,5},{7,6},{9,8},{10,9},{11,10},{13,12},{... | collective-permute-start | bytes 27656 | tf_op jit(solution)/shard_map/ppermute | solution.py:19
  60.9 29.2 %copy-start.2 = (bf16[6,12,32,2]{3,2,1,0:T(8,128)(2,1)S(1)}, bf16[6,12,32,2]{3,2,1,0:T(8,128)(2,1)}, u32[]{:S(2)}) copy-start(bf16[6,12,32,2]{3,2,1,0:T(8,128)(2,1)} %copy.97.refs_7_) | copy-start | bytes 27652
  60.9 29.2 %copy-start.3 = (bf16[6,12,32,2]{3,2,1,0:T(8,128)(2,1)S(1)}, bf16[6,12,32,2]{3,2,1,0:T(8,128)(2,1)}, u32[]{:S(2)}) copy-start(bf16[6,12,32,2]{3,2,1,0:T(8,128)(2,1)} %copy.98.refs_8_) | copy-start | bytes 27652
  76.6 15.7 %collective-permute-start.12 = (bf16[1,4,64,128]{3,2,1,0:T(8,128)(2,1)S(1)}, bf16[1,4,64,128]{3,2,1,0:T(8,128)(2,1)S(1)}, u32[]{:S(2)}, u32[]{:S(2)}) collective-permute-start(bf16[1,4,64,128]{3,2,1,0:T(8,128)(2,1)S(1)} %bitcast.69), channel_id=1, source_target_pairs={{0,64},{32,96},{64,128},{96,160},{128,192},{160,224},{192,256},{22... | collective-permute-start | bytes 196616 | tf_op jit(solution)/shard_map/ppermute | solution.py:19
  81.0 11.3 %collective-permute-start.13 = (bf16[1,4,64,128]{3,2,1,0:T(8,128)(2,1)S(1)}, bf16[1,4,64,128]{3,2,1,0:T(8,128)(2,1)S(1)}, u32[]{:S(2)}, u32[]{:S(2)}) collective-permute-start(bf16[1,4,64,128]{3,2,1,0:T(8,128)(2,1)S(1)} %bitcast.70), channel_id=1, source_target_pairs={{0,32},{32,64},{64,96},{96,128},{128,160},{160,192},{192,224},{224... | collective-permute-start | bytes 196616 | tf_op jit(solution)/shard_map/ppermute | solution.py:19
  87.4 9.0 %collective-permute-start.14 = (bf16[1,4,64,128]{3,2,1,0:T(8,128)(2,1)S(1)}, bf16[1,4,64,128]{3,2,1,0:T(8,128)(2,1)S(1)}, u32[]{:S(2)}, u32[]{:S(2)}) collective-permute-start(bf16[1,4,64,128]{3,2,1,0:T(8,128)(2,1)S(1)} %bitcast.71), channel_id=1, source_target_pairs={{32,0},{64,32},{96,64},{128,96},{160,128},{192,160},{224,192},{256... | collective-permute-start | bytes 196616 | tf_op jit(solution)/shard_map/ppermute | solution.py:19
  88.7 7.7 %collective-permute-start.15 = (bf16[1,4,64,128]{3,2,1,0:T(8,128)(2,1)S(1)}, bf16[1,4,64,128]{3,2,1,0:T(8,128)(2,1)S(1)}, u32[]{:S(2)}, u32[]{:S(2)}) collective-permute-start(bf16[1,4,64,128]{3,2,1,0:T(8,128)(2,1)S(1)} %bitcast.72), channel_id=1, source_target_pairs={{64,0},{96,32},{128,64},{160,96},{192,128},{224,160},{256,192},{28... | collective-permute-start | bytes 196616 | tf_op jit(solution)/shard_map/ppermute | solution.py:19
  92.1 18.4 %copy-start = (bf16[4,10,96,256]{3,2,1,0:T(8,128)(2,1)S(1)}, bf16[4,10,96,256]{3,2,1,0:T(8,128)(2,1)}, u32[]{:S(2)}) copy-start(bf16[4,10,96,256]{3,2,1,0:T(8,128)(2,1)} %get-tuple-element.22.refs_4_) | copy-start | bytes 5898244
  96.4 9.5 %collective-permute-start.16 = (bf16[5,2,64,128]{3,2,1,0:T(8,128)(2,1)S(1)}, bf16[5,2,64,128]{3,2,1,0:T(8,128)(2,1)S(1)}, u32[]{:S(2)}, u32[]{:S(2)}) collective-permute-start(bf16[5,2,64,128]{3,2,1,0:T(8,128)(2,1)S(1)} %get-tuple-element.70), channel_id=1, source_target_pairs={{0,4},{4,8},{8,12},{12,16},{16,20},{20,24},{24,28},{1,5},{5,9},{9,... | collective-permute-start | bytes 491528 | tf_op jit(solution)/shard_map/ppermute | solution.py:19
  103.7 6.6 %collective-permute-start.17 = (bf16[5,2,64,128]{3,2,1,0:T(8,128)(2,1)S(1)}, bf16[5,2,64,128]{3,2,1,0:T(8,128)(2,1)S(1)}, u32[]{:S(2)}, u32[]{:S(2)}) collective-permute-start(bf16[5,2,64,128]{3,2,1,0:T(8,128)(2,1)S(1)} %get-tuple-element.71), channel_id=1, source_target_pairs={{4,0},{8,4},{12,8},{16,12},{20,16},{24,20},{28,24},{5,1},{9,5},{13... | collective-permute-start | bytes 491528 | tf_op jit(solution)/shard_map/ppermute | solution.py:19
  119.7 6.0 %copy-start.5 = (bf16[32,3,3,3,32]{4,0,3,2,1:T(8,128)(2,1)S(1)}, bf16[32,3,3,3,32]{4,0,3,2,1:T(8,128)(2,1)}, u32[]{:S(2)}) copy-start(bf16[32,3,3,3,32]{4,0,3,2,1:T(8,128)(2,1)} %param.8) | copy-start | bytes 165892
  120.7 20.2 %all-to-all-start.1 = ((bf16[32,56,128]{2,1,0:T(8,128)(2,1)}), bf16[32,56,128]{2,1,0:T(8,128)(2,1)S(1)}, u32[]{:S(2)}, u32[]{:S(2)}) async-start(bf16[32,56,128]{2,1,0:T(8,128)(2,1)} %pad_maximum_fusion.2), calls=%async_computation.1 | async-start | bytes 917504 | tf_op jit(solution)/shard_map/all_to_all | solution.py:275
  126.2 1.3 copy-start.1
  169.2 19.1 %all-to-all-start.3 = ((bf16[32,56,128]{2,1,0:T(8,128)(2,1)}), bf16[32,56,128]{2,1,0:T(8,128)(2,1)S(1)}, u32[]{:S(2)}, u32[]{:S(2)}) async-start(bf16[32,56,128]{2,1,0:T(8,128)(2,1)} %broadcast_in_dim.60), calls=%async_computation.3 | async-start | bytes 917504 | tf_op jit(solution)/shard_map/all_to_all | solution.py:275

commit v3 on v2

--- a/solution.py
+++ b/solution.py
@@ -92,8 +92,8 @@
 
 def forward_kernel(
     sizes, offs, vol, w1, w2, w3, cot, pool, unread_a, unread_b,
-    skip_o, coarse_o, cgrad_o, craw_o, fpre_o, spre_o, t1_o, t2_o,
-    t1, acc1, t2, acc2, fine, t3,
+    skip_o, coarse_o, cgrad_o, t3, fpre_o, spre_o, t1_o, t2_o,
+    t1, acc1, t2, acc2, fine,
 ):
     nx, ny, nz = sizes
     ox, oy, oz = offs[0], offs[1], offs[2]
@@ -152,16 +152,19 @@
             mean = keep(mean, coarse_ok, (ox // 2 + x - 1, nx // 2), (oy // 2 + y - 1, ny // 2))
             store_taps(t3, (x, y), mean.astype(BF).astype(F32))
 
-    own = lane_mask(128, 0, 4, 68)
-    raw = [jnp.zeros((64, 288), F32) for _ in range(3)]
     for y in range(4):
         pre = jnp.zeros((64, 128), F32)
         for i in range(3):
             pre = pre + dot(w3[i], rows_at(t3, i, y + 1))
         coarse_o[y] = silu(pre).astype(BF)
-        grad = cot[y].astype(F32) * slope(pre)
-        cgrad_o[y] = grad.astype(BF)
-        mine = jnp.where(own > 0.5, grad, 0.0).astype(BF)
+        cgrad_o[y] = (cot[y].astype(F32) * slope(pre)).astype(BF)
+
+
+def middle_kernel(cgrad, t3, craw_o):
+    own = lane_mask(128, 0, 4, 68)
+    raw = [jnp.zeros((64, 288), F32) for _ in range(3)]
+    for y in range(4):
+        mine = jnp.where(own > 0.5, cgrad[y].astype(F32), 0.0).astype(BF)
         for i in range(3):
             raw[i] = raw[i] + dot_lanes(mine, rows_at(t3, i, y + 1))
     for i in range(3):
@@ -327,16 +330,19 @@
     wide_volume = jnp.concatenate(
         [far[0], near[0][:, :, chans:], rows_volume, near[1][:, :, chans:], far[1]], axis=0
     )
-    wide_volume = halo(halo(wide_volume, "gy", 1, 4), "gz", 3, 8)
+    wide_volume = halo(wide_volume, "gy", 1, 4)
+    later = wide_volume[0, 0, 0, 0] * 0
+    wide_volume = halo(wide_volume, "gz", 3, 8)
     wide_volume = jnp.pad(wide_volume, ((0, 0), (0, 0), (0, 0), (0, LANES - 144)))
     tall_cotangent = jnp.concatenate(
         [near[0][:, :, :chans], rows_cotangent, near[1][:, :, :chans]], axis=0
     )
     tall_cotangent = halo(tall_cotangent, "gy", 1, 2)
-    edges = (
-        shifted(tall_cotangent[..., -2:], "gz", 1),
-        shifted(tall_cotangent[..., :2], "gz", -1),
-    )
+    turned = (
+        shifted(jnp.transpose(tall_cotangent[..., -2:], (0, 1, 3, 2)), "gz", 1),
+        shifted(jnp.transpose(tall_cotangent[..., :2], (0, 1, 3, 2)), "gz", -1),
+    )
+    edges = [jnp.transpose(edge, (0, 1, 3, 2)) for edge in turned]
     wide_cotangent = jnp.concatenate([edges[0], tall_cotangent, edges[1]], axis=3)
     wide_cotangent = jnp.pad(wide_cotangent, ((0, 0), (0, 0), (0, 0), (6, LANES - 138)))
     sides = counts[2]
@@ -346,6 +352,7 @@
     returned = swap(sent, "gz")
     returned = jnp.transpose(returned, (2, 0, 1, 3)).reshape(4, 64, depth + 4)
     returned = jnp.pad(returned, ((0, 0), (0, 0), (2, 128 - 70)))
+    returned = returned + later
     fine_place = lax.broadcasted_iota(jnp.int32, (LANES, 128), 0)
     coarse_place = lax.broadcasted_iota(jnp.int32, (LANES, 128), 1)
     pool = jnp.where(fine_place // 2 == coarse_place, 1.0, 0.0).astype(BF)
@@ -355,14 +362,14 @@
     thin_first = jnp.pad(thin_first, ((0, 0), (0, 0), (0, 4))).reshape(96, 48)
     smem = pl.BlockSpec(memory_space=pltpu.SMEM)
     vmem = pl.BlockSpec(memory_space=pltpu.VMEM)
-    skip, coarse_local, coarse_grad, coarse_raw, first_pre, second_pre, taps1, taps2 = (
+    skip, coarse_local, coarse_grad, taps3, first_pre, second_pre, taps1, taps2 = (
         pl.pallas_call(
             lambda *refs: forward_kernel(sizes, *refs),
             out_shape=(
                 shape((2, 8, 32, 128), BF),
                 shape((4, 64, 128), BF),
                 shape((4, 64, 128), BF),
-                shape((192, 288), F32),
+                shape((3, 6, 96, 128), BF),
                 shape((4, 10, 32, LANES), F32),
                 shape((6, 12, 32, LANES), F32),
                 shape((4, 10, 16, LANES), BF),
@@ -376,7 +383,6 @@
                 pltpu.VMEM((10, 16, 96, LANES), BF),
                 pltpu.VMEM((12, 16, 32, LANES), F32),
                 pltpu.VMEM((6, 12, 32, LANES), BF),
-                pltpu.VMEM((3, 6, 96, 128), BF),
             ],
             compiler_params=pltpu.CompilerParams(vmem_limit_bytes=52 * 2**20),
             cost_estimate=pl.CostEstimate(
@@ -391,9 +397,20 @@
             stacked(w_coarse),
             returned,
             pool,
-            *edges,
+            *turned,
         )
     )
+    coarse_raw = pl.pallas_call(
+        middle_kernel,
+        out_shape=shape((192, 288), F32),
+        in_specs=[vmem] * 2,
+        out_specs=vmem,
+        compiler_params=pltpu.CompilerParams(vmem_limit_bytes=48 * 2**20),
+        cost_estimate=pl.CostEstimate(
+            flops=2 * 10**8, bytes_accessed=10**6, transcendentals=0
+        ),
+        name="middle",
+    )(coarse_grad, taps3)
     wide_grad = halo(halo(coarse_grad[None], "gx", 0, 2), "gy", 1, 2)
     taps5, second_raw = pl.pallas_call(
         lambda *refs: second_kernel(sizes, *refs),

time: 193 us -> 197 us (1.021)
  starting transfers between devices: 72.2 us -> 77.7 us
  waiting for transfers between devices: 33.7 us -> 30.6 us
    ppermute x18, waiting for transfers between devices: 10.7 us -> 7 us  [shifted(): return lax.ppermute(block, axis, pairs)]
    ppermute x18, starting transfers between devices: 58.9 us -> 61.8 us  [shifted(): return lax.ppermute(block, axis, pairs)]
    all_to_all x3, starting transfers between devices: 13.3 us -> 15.9 us  [swap(): return lax.all_to_all(blocks, axes, split_axis=0, concat_axis=0, tiled=True)]
    unnamed x32 -> x28, local copies, waits for them, and re-layouts: 6.89 us -> 6.89 us
  transfers between devices with their start and end apart: 21 -> 21, of which waited for: 8 -> 6; matrix products, arithmetic and copies ran while one was open for 8% -> 9% of each run, Pallas kernels for 4% -> 5%
where the time goes in v3:
time: 197 us; the launch traced here: 196 us
  starting transfers between devices  77.7 us (39%)
  Pallas kernels  32.8 us (17%)
  waiting for transfers between devices  30.6 us (16%)
  blocking collectives  26.9 us (14%)
  local copies, waits for them, and re-layouts  17.7 us (9%)
  other arithmetic  7.68 us (4%)
  between operations  2.15 us (1%)
    ppermute x18, starting transfers between devices, shifted(): return lax.ppermute(block, axis, pairs)  61.8 us
    all_to_all x1, blocking collectives, swap(): return lax.all_to_all(blocks, axes, split_axis=0, concat_axis=0, tiled=True)  26.9 us
    all_to_all x3, waiting for transfers between devices, swap(): return lax.all_to_all(blocks, axes, split_axis=0, concat_axis=0, tiled=True)  23.6 us
    all_to_all x3, starting transfers between devices, swap(): return lax.all_to_all(blocks, axes, split_axis=0, concat_axis=0, tiled=True)  15.9 us
    pallas_call x1, Pallas kernels, local(): pl.pallas_call(lambda *refs: forward_kernel(sizes, *refs), out_shape=(sha...  14.6 us
    pallas_call x1, Pallas kernels, local(): pl.pallas_call(lambda *refs: second_kernel(sizes, *refs), out_shape=(shap...  9.28 us
    pallas_call x1, Pallas kernels, local(): pl.pallas_call(lambda *refs: first_kernel(sizes, *refs), out_shape=(shape...  7.03 us
    ppermute x18, waiting for transfers between devices, shifted(): return lax.ppermute(block, axis, pairs)  7 us
  transfers between devices with their start and end apart: 21, of which 6 were waited for; matrix products, arithmetic and copies ran while one was open for 9% of the time, Pallas kernels for 5%

profile of v3, /device:TPU:1, one launch (start us, length us, event | category | flops | bytes accessed | tf_op | source)
XLA Modules:
  0.0 195.5 jit_solution(8653930520166491171)
XLA Ops:
  2.7 4.7 %collective-permute-start = (bf16[2,8,4,128]{3,2,1,0:T(4,128)(2,1)S(1)}, bf16[2,8,4,128]{3,2,1,0:T(4,128)(2,1)S(1)}, u32[]{:S(2)}, u32[]{:S(2)}) collective-permute-start(bf16[2,8,4,128]{3,2,1,0:T(4,128)(2,1)S(1)} %bitcast.104), channel_id=1, source_target_pairs={{0,64},{32,96},{64,128},{96,160},{128,192},{160,224},{192,256},{22... | collective-permute-start | bytes 49160 | tf_op jit(solution)/shard_map/ppermute | solution.py:19
  8.4 1.3 collective-permute-start.2
  9.7 11.4 %collective-permute-start.1 = (bf16[2,8,36,128]{3,2,1,0:T(8,128)(2,1)S(1)}, bf16[2,8,36,128]{3,2,1,0:T(8,128)(2,1)S(1)}, u32[]{:S(2)}, u32[]{:S(2)}) collective-permute-start(bf16[2,8,36,128]{3,2,1,0:T(8,128)(2,1)S(1)} %pad_maximum_fusion.7), channel_id=1, source_target_pairs={{0,32},{32,64},{64,96},{96,128},{128,160},{160,192},{192,224},{224... | collective-permute-start | bytes 442376 | tf_op jit(solution)/shard_map/ppermute | solution.py:19
  22.8 4.3 %all-to-all-start = ((bf16[4,16,4,68]{3,2,1,0:T(4,128)(2,1)}), bf16[4,16,4,68]{3,2,1,0:T(4,128)(2,1)S(1)}, u32[]{:S(2)}, u32[]{:S(2)}) async-start(bf16[4,16,4,68]{3,2,1,0:T(4,128)(2,1)} %pad_maximum_fusion.12), calls=%async_computation | async-start | bytes 131072 | tf_op jit(solution)/shard_map/all_to_all | solution.py:278
  30.5 7.0 %all-to-all-done = bf16[4,16,4,68]{3,2,1,0:T(4,128)(2,1)S(1)} async-done(((bf16[4,16,4,68]{3,2,1,0:T(4,128)(2,1)}), bf16[4,16,4,68]{3,2,1,0:T(4,128)(2,1)S(1)}, u32[]{:S(2)}, u32[]{:S(2)}) %all-to-all-start) | async-done | bytes 34848 | tf_op jit(solution)/shard_map/all_to_all | solution.py:278
  37.7 3.5 %collective-permute-start.4 = (bf16[10,4,4,128]{3,2,1,0:T(4,128)(2,1)S(1)}, bf16[10,4,4,128]{3,2,1,0:T(4,128)(2,1)S(1)}, u32[]{:S(2)}, u32[]{:S(2)}) collective-permute-start(bf16[10,4,4,128]{3,2,1,0:T(4,128)(2,1)S(1)} %get-tuple-element.80), channel_id=1, source_target_pairs={{0,4},{4,8},{8,12},{12,16},{16,20},{20,24},{24,28},{1,5},{5,9},{9,... | collective-permute-start | bytes 122888 | tf_op jit(solution)/shard_map/ppermute | solution.py:19
  41.2 1.9 collective-permute-start.5
  43.2 3.6 %collective-permute-start.8 = (bf16[6,2,32,128]{3,2,1,0:T(8,128)(2,1)S(1)}, bf16[6,2,32,128]{3,2,1,0:T(8,128)(2,1)S(1)}, u32[]{:S(2)}, u32[]{:S(2)}) collective-permute-start(bf16[6,2,32,128]{3,2,1,0:T(8,128)(2,1)S(1)} %get-tuple-element.68), channel_id=1, source_target_pairs={{0,4},{4,8},{8,12},{12,16},{16,20},{20,24},{24,28},{1,5},{5,9},{9,... | collective-permute-start | bytes 294920 | tf_op jit(solution)/shard_map/ppermute | solution.py:19
  46.8 1.9 collective-permute-start.9
  49.1 1.3 collective-permute-start.6
  50.4 1.3 collective-permute-start.7
  54.3 4.0 %collective-permute-start.10 = (bf16[6,12,2,32]{3,2,1,0:T(2,128)(2,1)S(1)}, bf16[6,12,2,32]{3,2,1,0:T(2,128)(2,1)S(1)}, u32[]{:S(2)}, u32[]{:S(2)}) collective-permute-start(bf16[6,12,2,32]{3,2,1,0:T(2,128)(2,1)S(1)} %copy.97), channel_id=1, source_target_pairs={{0,1},{1,2},{2,3},{4,5},{5,6},{6,7},{8,9},{9,10},{10,11},{12,13},{... | collective-permute-start | bytes 27656 | tf_op jit(solution)/shard_map/ppermute | solution.py:19
  58.3 1.3 collective-permute-start.11
  59.6 1.4 fusion.20.refs_1_
  61.1 2.3 %collective-permute-done.11.refs_8_ = bf16[6,12,2,32]{3,2,1,0:T(2,128)(2,1)S(1)} collective-permute-done((bf16[6,12,2,32]{3,2,1,0:T(2,128)(2,1)S(1)}, bf16[6,12,2,32]{3,2,1,0:T(2,128)(2,1)S(1)}, u32[]{:S(2)}, u32[]{:S(2)}) %collective-permute-start.11) | collective-permute-done | bytes 9248 | tf_op jit(solution)/shard_map/ppermute | solution.py:19
  63.4 14.6 %forward.1 = (bf16[2,8,32,128]{3,2,1,0:T(8,128)(2,1)S(1)}, bf16[4,64,128]{2,1,0:T(8,128)(2,1)S(1)}, bf16[4,64,128]{2,1,0:T(8,128)(2,1)S(1)}, bf16[3,6,96,128]{3,...) custom-call(s32[3]{0:T(128)S(1)} %pad_add_fusion.1.refs_0_, ...), custom_call_target="tpu_custom_call" | custom-call | flops 4000000000 | bytes 12000000 | tf_op jit(solution)/shard_map/forward/pallas_call | solution.py:366
  79.3 1.3 collective-permute-start.14
  80.6 8.4 %collective-permute-start.13 = (bf16[1,4,64,128]{3,2,1,0:T(8,128)(2,1)S(1)}, bf16[1,4,64,128]{3,2,1,0:T(8,128)(2,1)S(1)}, u32[]{:S(2)}, u32[]{:S(2)}) collective-permute-start(bf16[1,4,64,128]{3,2,1,0:T(8,128)(2,1)S(1)} %bitcast.77), channel_id=1, source_target_pairs={{0,32},{32,64},{64,96},{96,128},{128,160},{160,192},{192,224},{224... | collective-permute-start | bytes 196616 | tf_op jit(solution)/shard_map/ppermute | solution.py:19
  88.9 5.1 %collective-permute-start.12 = (bf16[1,4,64,128]{3,2,1,0:T(8,128)(2,1)S(1)}, bf16[1,4,64,128]{3,2,1,0:T(8,128)(2,1)S(1)}, u32[]{:S(2)}, u32[]{:S(2)}) collective-permute-start(bf16[1,4,64,128]{3,2,1,0:T(8,128)(2,1)S(1)} %bitcast.78), channel_id=1, source_target_pairs={{0,64},{32,96},{64,128},{96,160},{128,192},{160,224},{192,256},{22... | collective-permute-start | bytes 196616 | tf_op jit(solution)/shard_map/ppermute | solution.py:19
  95.7 1.9 select_maximum_fusion.refs_3_
  98.0 6.3 %collective-permute-start.16 = (bf16[5,2,64,128]{3,2,1,0:T(8,128)(2,1)S(1)}, bf16[5,2,64,128]{3,2,1,0:T(8,128)(2,1)S(1)}, u32[]{:S(2)}, u32[]{:S(2)}) collective-permute-start(bf16[5,2,64,128]{3,2,1,0:T(8,128)(2,1)S(1)} %get-tuple-element.70), channel_id=1, source_target_pairs={{0,4},{4,8},{8,12},{12,16},{16,20},{20,24},{24,28},{1,5},{5,9},{9,... | collective-permute-start | bytes 491528 | tf_op jit(solution)/shard_map/ppermute | solution.py:19
  104.3 1.9 collective-permute-start.17
  106.6 4.4 %collective-permute-done.17 = bf16[5,2,64,128]{3,2,1,0:T(8,128)(2,1)S(1)} collective-permute-done((bf16[5,2,64,128]{3,2,1,0:T(8,128)(2,1)S(1)}, bf16[5,2,64,128]{3,2,1,0:T(8,128)(2,1)S(1)}, u32[]{:S(2)}, u32[]{:S(2)}) %collective-permute-start.17) | collective-permute-done | bytes 163872 | tf_op jit(solution)/shard_map/ppermute | solution.py:19
  111.1 9.3 %second.1 = (bf16[6,12,96,256]{3,2,1,0:T(8,128)(2,1)}, f32[96,288]{1,0:T(8,128)S(1)}) custom-call(s32[3]{0:T(128)S(1)} %pad_add_fusion.1.refs_0_, bf16[5,8,64,128]{3,2,1,0:T(8,128)(2,1)S(1)} %pad_maximum_fusion.refs_1_, f32[6,12,32,256]{3,2,1,0:T(8,128)} %get-tuple-element.21.refs_2_, bf16[6,12,32,256]{3,2,1,0:T(8,128)(2,1)S(1)} %select_maximum_fusion.refs_3_, ...), custom_call_target="tpu_custom_call" | custom-call | flops 1000000000 | bytes 10000000 | tf_op jit(solution)/shard_map/second/pallas_call | solution.py:415
  121.3 7.6 %all-to-all-start.1 = ((bf16[32,56,128]{2,1,0:T(8,128)(2,1)}), bf16[32,56,128]{2,1,0:T(8,128)(2,1)}, u32[]{:S(2)}, u32[]{:S(2)}) async-start(bf16[32,56,128]{2,1,0:T(8,128)(2,1)} %pad_maximum_fusion.2), calls=%async_computation.1 | async-start | bytes 917504 | tf_op jit(solution)/shard_map/all_to_all | solution.py:278
  129.3 1.3 copy-done.1
  130.7 7.0 %first.1 = (bf16[4,10,96,256]{3,2,1,0:T(8,128)(2,1)S(1)}, bf16[32,128]{1,0:T(8,128)(2,1)S(1)}) custom-call(s32[3]{0:T(128)S(1)} %pad_add_fusion.1.refs_0_, bf16[6,12,96,256]{3,2,1,0:T(8,128)(2,1)} %get-tuple-element.25.refs_1_, f32[4,10,32,256]{3,2,1,0:T(8,128)S(1)} %copy-done.1, bf16[4,10,16,256]{3,2,1,0:T(8,128)(2,1)S(1)} %get-tuple-element.27.refs_3_, ...), custom_call_target="tpu_custom_call" | custom-call | flops 2000000000 | bytes 10000000 | tf_op jit(solution)/shard_map/first/pallas_call | solution.py:453
  137.7 6.4 %all-to-all-done.1 = bf16[32,56,128]{2,1,0:T(8,128)(2,1)} async-done(((bf16[32,56,128]{2,1,0:T(8,128)(2,1)}), bf16[32,56,128]{2,1,0:T(8,128)(2,1)}, u32[]{:S(2)}, u32[]{:S(2)}) %all-to-all-start.1) | async-done | bytes 458784 | tf_op jit(solution)/shard_map/all_to_all | solution.py:278
  145.1 26.9 %all_to_all.20 = bf16[16,56,128]{2,1,0:T(8,128)(2,1)S(1)} all-to-all(bf16[16,56,128]{2,1,0:T(8,128)(2,1)S(1)} %broadcast_in_dim.59), channel_id=1, replica_groups=mesh['gx'=16,'gy'=8,'gz'=4] {'gx'}, dimensions={0} | all-to-all | bytes 458752 | tf_op jit(solution)/shard_map/all_to_all | solution.py:278
  172.9 4.0 %all-to-all-start.3 = ((bf16[32,56,128]{2,1,0:T(8,128)(2,1)}), bf16[32,56,128]{2,1,0:T(8,128)(2,1)S(1)}, u32[]{:S(2)}, u32[]{:S(2)}) async-start(bf16[32,56,128]{2,1,0:T(8,128)(2,1)} %broadcast_in_dim.60), calls=%async_computation.3 | async-start | bytes 917504 | tf_op jit(solution)/shard_map/all_to_all | solution.py:278
  177.8 1.4 volume.1
  181.7 10.2 %all-to-all-done.3 = bf16[32,56,128]{2,1,0:T(8,128)(2,1)S(1)} async-done(((bf16[32,56,128]{2,1,0:T(8,128)(2,1)}), bf16[32,56,128]{2,1,0:T(8,128)(2,1)S(1)}, u32[]{:S(2)}, u32[]{:S(2)}) %all-to-all-start.3) | async-done | bytes 458784 | tf_op jit(solution)/shard_map/all_to_all | solution.py:278
  (133 shorter events, 24.1 us)
Async XLA Ops:
  0.6 28.9 %copy-start.2 = (bf16[64,3,3,3,32]{0,4,3,2,1:T(8,128)(2,1)S(1)}, bf16[64,3,3,3,32]{0,4,3,2,1:T(8,128)(2,1)}, u32[]{:S(2)}) copy-start(bf16[64,3,3,3,32]{0,4,3,2,1:T(8,128)(2,1)} %param.9) | copy-start | bytes 331780
  0.6 29.5 %copy-start.3 = (bf16[32,3,3,3,32]{4,0,3,2,1:T(8,128)(2,1)S(1)}, bf16[32,3,3,3,32]{4,0,3,2,1:T(8,128)(2,1)}, u32[]{:S(2)}) copy-start(bf16[32,3,3,3,32]{4,0,3,2,1:T(8,128)(2,1)} %param.8) | copy-start | bytes 165892
  1.4 36.2 %collective-permute-start.3 = (bf16[2,8,4,128]{3,2,1,0:T(4,128)(2,1)S(1)}, bf16[2,8,4,128]{3,2,1,0:T(4,128)(2,1)S(1)}, u32[]{:S(2)}, u32[]{:S(2)}) collective-permute-start(bf16[2,8,4,128]{3,2,1,0:T(4,128)(2,1)S(1)} %bitcast.103), channel_id=1, source_target_pairs={{64,0},{96,32},{128,64},{160,96},{192,128},{224,160},{256,192},{28... | collective-permute-start | bytes 49160 | tf_op jit(solution)/shard_map/ppermute | solution.py:19
  2.7 27.7 %collective-permute-start = (bf16[2,8,4,128]{3,2,1,0:T(4,128)(2,1)S(1)}, bf16[2,8,4,128]{3,2,1,0:T(4,128)(2,1)S(1)}, u32[]{:S(2)}, u32[]{:S(2)}) collective-permute-start(bf16[2,8,4,128]{3,2,1,0:T(4,128)(2,1)S(1)} %bitcast.104), channel_id=1, source_target_pairs={{0,64},{32,96},{64,128},{96,160},{128,192},{160,224},{192,256},{22... | collective-permute-start | bytes 49160 | tf_op jit(solution)/shard_map/ppermute | solution.py:19
  8.3 29.2 %copy-start.5 = (bf16[4,2,8,128]{3,2,1,0:T(8,128)(2,1)S(1)}, bf16[4,2,8,128]{3,2,1,0:T(8,128)(2,1)}, u32[]{:S(2)}) copy-start(bf16[4,2,8,128]{3,2,1,0:T(8,128)(2,1)} %param.6) | copy-start | bytes 49156
  8.4 29.2 %collective-permute-start.2 = (bf16[2,8,36,128]{3,2,1,0:T(8,128)(2,1)S(1)}, bf16[2,8,36,128]{3,2,1,0:T(8,128)(2,1)S(1)}, u32[]{:S(2)}, u32[]{:S(2)}) collective-permute-start(bf16[2,8,36,128]{3,2,1,0:T(8,128)(2,1)S(1)} %pad_maximum_fusion.7), channel_id=1, source_target_pairs={{32,0},{64,32},{96,64},{128,96},{160,128},{192,160},{224,192},{256... | collective-permute-start | bytes 442376 | tf_op jit(solution)/shard_map/ppermute | solution.py:19
  9.7 27.8 %collective-permute-start.1 = (bf16[2,8,36,128]{3,2,1,0:T(8,128)(2,1)S(1)}, bf16[2,8,36,128]{3,2,1,0:T(8,128)(2,1)S(1)}, u32[]{:S(2)}, u32[]{:S(2)}) collective-permute-start(bf16[2,8,36,128]{3,2,1,0:T(8,128)(2,1)S(1)} %pad_maximum_fusion.7), channel_id=1, source_target_pairs={{0,32},{32,64},{64,96},{96,128},{128,160},{160,192},{192,224},{224... | collective-permute-start | bytes 442376 | tf_op jit(solution)/shard_map/ppermute | solution.py:19
  22.8 14.7 %all-to-all-start = ((bf16[4,16,4,68]{3,2,1,0:T(4,128)(2,1)}), bf16[4,16,4,68]{3,2,1,0:T(4,128)(2,1)S(1)}, u32[]{:S(2)}, u32[]{:S(2)}) async-start(bf16[4,16,4,68]{3,2,1,0:T(4,128)(2,1)} %pad_maximum_fusion.12), calls=%async_computation | async-start | bytes 131072 | tf_op jit(solution)/shard_map/all_to_all | solution.py:278
  37.7 11.1 %collective-permute-start.4 = (bf16[10,4,4,128]{3,2,1,0:T(4,128)(2,1)S(1)}, bf16[10,4,4,128]{3,2,1,0:T(4,128)(2,1)S(1)}, u32[]{:S(2)}, u32[]{:S(2)}) collective-permute-start(bf16[10,4,4,128]{3,2,1,0:T(4,128)(2,1)S(1)} %get-tuple-element.80), channel_id=1, source_target_pairs={{0,4},{4,8},{8,12},{12,16},{16,20},{20,24},{24,28},{1,5},{5,9},{9,... | collective-permute-start | bytes 122888 | tf_op jit(solution)/shard_map/ppermute | solution.py:19
  41.2 7.6 %collective-permute-start.5 = (bf16[10,4,4,128]{3,2,1,0:T(4,128)(2,1)S(1)}, bf16[10,4,4,128]{3,2,1,0:T(4,128)(2,1)S(1)}, u32[]{:S(2)}, u32[]{:S(2)}) collective-permute-start(bf16[10,4,4,128]{3,2,1,0:T(4,128)(2,1)S(1)} %get-tuple-element.81), channel_id=1, source_target_pairs={{4,0},{8,4},{12,8},{16,12},{20,16},{24,20},{28,24},{5,1},{9,5},{13... | collective-permute-start | bytes 122888 | tf_op jit(solution)/shard_map/ppermute | solution.py:19
  43.2 9.8 %collective-permute-start.8 = (bf16[6,2,32,128]{3,2,1,0:T(8,128)(2,1)S(1)}, bf16[6,2,32,128]{3,2,1,0:T(8,128)(2,1)S(1)}, u32[]{:S(2)}, u32[]{:S(2)}) collective-permute-start(bf16[6,2,32,128]{3,2,1,0:T(8,128)(2,1)S(1)} %get-tuple-element.68), channel_id=1, source_target_pairs={{0,4},{4,8},{8,12},{12,16},{16,20},{20,24},{24,28},{1,5},{5,9},{9,... | collective-permute-start | bytes 294920 | tf_op jit(solution)/shard_map/ppermute | solution.py:19
  46.8 6.1 %collective-permute-start.9 = (bf16[6,2,32,128]{3,2,1,0:T(8,128)(2,1)S(1)}, bf16[6,2,32,128]{3,2,1,0:T(8,128)(2,1)S(1)}, u32[]{:S(2)}, u32[]{:S(2)}) collective-permute-start(bf16[6,2,32,128]{3,2,1,0:T(8,128)(2,1)S(1)} %get-tuple-element.69), channel_id=1, source_target_pairs={{4,0},{8,4},{12,8},{16,12},{20,16},{24,20},{28,24},{5,1},{9,5},{13... | collective-permute-start | bytes 294920 | tf_op jit(solution)/shard_map/ppermute | solution.py:19
  49.1 10.6 %collective-permute-start.6 = (bf16[10,16,4,8]{3,2,1,0:T(4,128)(2,1)S(1)}, bf16[10,16,4,8]{3,2,1,0:T(4,128)(2,1)S(1)}, u32[]{:S(2)}, u32[]{:S(2)}) collective-permute-start(bf16[10,16,4,8]{3,2,1,0:T(4,128)(2,1)S(1)} %get-tuple-element.76), channel_id=1, source_target_pairs={{0,1},{1,2},{2,3},{4,5},{5,6},{6,7},{8,9},{9,10},{10,11},{12,13},{... | collective-permute-start | bytes 30728 | tf_op jit(solution)/shard_map/ppermute | solution.py:19
  50.4 9.3 %collective-permute-start.7 = (bf16[10,16,4,8]{3,2,1,0:T(4,128)(2,1)S(1)}, bf16[10,16,4,8]{3,2,1,0:T(4,128)(2,1)}, u32[]{:S(2)}, u32[]{:S(2)}) collective-permute-start(bf16[10,16,4,8]{3,2,1,0:T(4,128)(2,1)S(1)} %get-tuple-element.77), channel_id=1, source_target_pairs={{1,0},{2,1},{3,2},{5,4},{6,5},{7,6},{9,8},{10,9},{11,10},{13,12},{... | collective-permute-start | bytes 30728 | tf_op jit(solution)/shard_map/ppermute | solution.py:19
  54.3 6.8 %collective-permute-start.10 = (bf16[6,12,2,32]{3,2,1,0:T(2,128)(2,1)S(1)}, bf16[6,12,2,32]{3,2,1,0:T(2,128)(2,1)S(1)}, u32[]{:S(2)}, u32[]{:S(2)}) collective-permute-start(bf16[6,12,2,32]{3,2,1,0:T(2,128)(2,1)S(1)} %copy.97), channel_id=1, source_target_pairs={{0,1},{1,2},{2,3},{4,5},{5,6},{6,7},{8,9},{9,10},{10,11},{12,13},{... | collective-permute-start | bytes 27656 | tf_op jit(solution)/shard_map/ppermute | solution.py:19
  58.3 5.0 %collective-permute-start.11 = (bf16[6,12,2,32]{3,2,1,0:T(2,128)(2,1)S(1)}, bf16[6,12,2,32]{3,2,1,0:T(2,128)(2,1)S(1)}, u32[]{:S(2)}, u32[]{:S(2)}) collective-permute-start(bf16[6,12,2,32]{3,2,1,0:T(2,128)(2,1)S(1)} %copy.98), channel_id=1, source_target_pairs={{1,0},{2,1},{3,2},{5,4},{6,5},{7,6},{9,8},{10,9},{11,10},{13,12},{... | collective-permute-start | bytes 27656 | tf_op jit(solution)/shard_map/ppermute | solution.py:19
  78.0 20.0 %collective-permute-start.15 = (bf16[1,4,64,128]{3,2,1,0:T(8,128)(2,1)S(1)}, bf16[1,4,64,128]{3,2,1,0:T(8,128)(2,1)S(1)}, u32[]{:S(2)}, u32[]{:S(2)}) collective-permute-start(bf16[1,4,64,128]{3,2,1,0:T(8,128)(2,1)S(1)} %bitcast.75), channel_id=1, source_target_pairs={{64,0},{96,32},{128,64},{160,96},{192,128},{224,160},{256,192},{28... | collective-permute-start | bytes 196616 | tf_op jit(solution)/shard_map/ppermute | solution.py:19
  79.3 18.7 %collective-permute-start.14 = (bf16[1,4,64,128]{3,2,1,0:T(8,128)(2,1)S(1)}, bf16[1,4,64,128]{3,2,1,0:T(8,128)(2,1)S(1)}, u32[]{:S(2)}, u32[]{:S(2)}) collective-permute-start(bf16[1,4,64,128]{3,2,1,0:T(8,128)(2,1)S(1)} %bitcast.76), channel_id=1, source_target_pairs={{32,0},{64,32},{96,64},{128,96},{160,128},{192,160},{224,192},{256... | collective-permute-start | bytes 196616 | tf_op jit(solution)/shard_map/ppermute | solution.py:19
  80.6 17.3 %collective-permute-start.13 = (bf16[1,4,64,128]{3,2,1,0:T(8,128)(2,1)S(1)}, bf16[1,4,64,128]{3,2,1,0:T(8,128)(2,1)S(1)}, u32[]{:S(2)}, u32[]{:S(2)}) collective-permute-start(bf16[1,4,64,128]{3,2,1,0:T(8,128)(2,1)S(1)} %bitcast.77), channel_id=1, source_target_pairs={{0,32},{32,64},{64,96},{96,128},{128,160},{160,192},{192,224},{224... | collective-permute-start | bytes 196616 | tf_op jit(solution)/shard_map/ppermute | solution.py:19
  88.9 8.9 %collective-permute-start.12 = (bf16[1,4,64,128]{3,2,1,0:T(8,128)(2,1)S(1)}, bf16[1,4,64,128]{3,2,1,0:T(8,128)(2,1)S(1)}, u32[]{:S(2)}, u32[]{:S(2)}) collective-permute-start(bf16[1,4,64,128]{3,2,1,0:T(8,128)(2,1)S(1)} %bitcast.78), channel_id=1, source_target_pairs={{0,64},{32,96},{64,128},{96,160},{128,192},{160,224},{192,256},{22... | collective-permute-start | bytes 196616 | tf_op jit(solution)/shard_map/ppermute | solution.py:19
  97.6 13.4 %copy-start = (bf16[4,10,96,256]{3,2,1,0:T(8,128)(2,1)S(1)}, bf16[4,10,96,256]{3,2,1,0:T(8,128)(2,1)}, u32[]{:S(2)}) copy-start(bf16[4,10,96,256]{3,2,1,0:T(8,128)(2,1)} %get-tuple-element.22.refs_4_) | copy-start | bytes 5898244
  98.0 8.6 %collective-permute-start.16 = (bf16[5,2,64,128]{3,2,1,0:T(8,128)(2,1)S(1)}, bf16[5,2,64,128]{3,2,1,0:T(8,128)(2,1)S(1)}, u32[]{:S(2)}, u32[]{:S(2)}) collective-permute-start(bf16[5,2,64,128]{3,2,1,0:T(8,128)(2,1)S(1)} %get-tuple-element.70), channel_id=1, source_target_pairs={{0,4},{4,8},{8,12},{12,16},{16,20},{20,24},{24,28},{1,5},{5,9},{9,... | collective-permute-start | bytes 491528 | tf_op jit(solution)/shard_map/ppermute | solution.py:19
  104.3 6.6 %collective-permute-start.17 = (bf16[5,2,64,128]{3,2,1,0:T(8,128)(2,1)S(1)}, bf16[5,2,64,128]{3,2,1,0:T(8,128)(2,1)S(1)}, u32[]{:S(2)}, u32[]{:S(2)}) collective-permute-start(bf16[5,2,64,128]{3,2,1,0:T(8,128)(2,1)S(1)} %get-tuple-element.71), channel_id=1, source_target_pairs={{4,0},{8,4},{12,8},{16,12},{20,16},{24,20},{28,24},{5,1},{9,5},{13... | collective-permute-start | bytes 491528 | tf_op jit(solution)/shard_map/ppermute | solution.py:19
  121.3 22.8 %all-to-all-start.1 = ((bf16[32,56,128]{2,1,0:T(8,128)(2,1)}), bf16[32,56,128]{2,1,0:T(8,128)(2,1)}, u32[]{:S(2)}, u32[]{:S(2)}) async-start(bf16[32,56,128]{2,1,0:T(8,128)(2,1)} %pad_maximum_fusion.2), calls=%async_computation.1 | async-start | bytes 917504 | tf_op jit(solution)/shard_map/all_to_all | solution.py:278
  129.3 1.3 copy-start.1
  137.7 39.2 %copy-start.4 = (bf16[32,3,3,3,4]{0,4,3,2,1:T(4,128)(2,1)S(1)}, bf16[32,3,3,3,4]{0,4,3,2,1:T(4,128)(2,1)}, u32[]{:S(2)}) copy-start(bf16[32,3,3,3,4]{0,4,3,2,1:T(4,128)(2,1)} %param.7) | copy-start | bytes 20740
  172.9 19.1 %all-to-all-start.3 = ((bf16[32,56,128]{2,1,0:T(8,128)(2,1)}), bf16[32,56,128]{2,1,0:T(8,128)(2,1)S(1)}, u32[]{:S(2)}, u32[]{:S(2)}) async-start(bf16[32,56,128]{2,1,0:T(8,128)(2,1)} %broadcast_in_dim.60), calls=%async_computation.3 | async-start | bytes 917504 | tf_op jit(solution)/shard_map/all_to_all | solution.py:278

commit v4 on v2

--- a/solution.py
+++ b/solution.py
@@ -327,23 +327,26 @@
     wide_volume = jnp.concatenate(
         [far[0], near[0][:, :, chans:], rows_volume, near[1][:, :, chans:], far[1]], axis=0
     )
-    wide_volume = halo(halo(wide_volume, "gy", 1, 4), "gz", 3, 8)
+    wide_volume = halo(wide_volume, "gy", 1, 4)
+    later = wide_volume[0, 0, 0, 0] * 0
+    wide_volume = halo(wide_volume, "gz", 3, 8)
     wide_volume = jnp.pad(wide_volume, ((0, 0), (0, 0), (0, 0), (0, LANES - 144)))
     tall_cotangent = jnp.concatenate(
         [near[0][:, :, :chans], rows_cotangent, near[1][:, :, :chans]], axis=0
     )
     tall_cotangent = halo(tall_cotangent, "gy", 1, 2)
-    edges = (
-        shifted(tall_cotangent[..., -2:], "gz", 1),
-        shifted(tall_cotangent[..., :2], "gz", -1),
-    )
+    turned = (
+        shifted(jnp.transpose(tall_cotangent[..., -2:], (0, 1, 3, 2)), "gz", 1),
+        shifted(jnp.transpose(tall_cotangent[..., :2], (0, 1, 3, 2)), "gz", -1),
+    )
+    edges = [jnp.transpose(edge, (0, 1, 3, 2)) for edge in turned]
     wide_cotangent = jnp.concatenate([edges[0], tall_cotangent, edges[1]], axis=3)
     wide_cotangent = jnp.pad(wide_cotangent, ((0, 0), (0, 0), (0, 0), (6, LANES - 138)))
     sides = counts[2]
     depth = coarse_cotangent.shape[3] // sides
     guarded = jnp.pad(coarse_cotangent[:, 0], ((0, 0), (0, 0), (2, 2)))
     sent = jnp.stack([guarded[..., n * depth : n * depth + depth + 4] for n in range(sides)])
-    returned = swap(sent, "gz")
+    returned = swap(sent, "gz") + later
     returned = jnp.transpose(returned, (2, 0, 1, 3)).reshape(4, 64, depth + 4)
     returned = jnp.pad(returned, ((0, 0), (0, 0), (2, 128 - 70)))
     fine_place = lax.broadcasted_iota(jnp.int32, (LANES, 128), 0)
@@ -391,7 +394,7 @@
             stacked(w_coarse),
             returned,
             pool,
-            *edges,
+            *turned,
         )
     )
     wide_grad = halo(halo(coarse_grad[None], "gx", 0, 2), "gy", 1, 2)

time: 193 us -> 195 us (1.010)
  starting transfers between devices: 72.2 us -> 77.9 us
  waiting for transfers between devices: 33.7 us -> 28.2 us
    all_to_all x3, waiting for transfers between devices: 23 us -> 16.7 us  [swap(): return lax.all_to_all(blocks, axes, split_axis=0, concat_axis=0, tiled=True)]
    ppermute x18, starting transfers between devices: 58.9 us -> 63.2 us  [shifted(): return lax.ppermute(block, axis, pairs)]
    unnamed x32 -> x28, local copies, waits for them, and re-layouts: 6.89 us -> 6.88 us
  transfers between devices with their start and end apart: 21 -> 21, of which waited for: 8 -> 6; matrix products, arithmetic and copies ran while one was open for 8% -> 8% of each run, Pallas kernels for 4% -> 4%
where the time goes in v4:
time: 195 us; the launch traced here: 194 us
  starting transfers between devices  77.9 us (40%)
  Pallas kernels  33.3 us (17%)
  waiting for transfers between devices  28.2 us (14%)
  blocking collectives  27.4 us (14%)
  local copies, waits for them, and re-layouts  18 us (9%)
  other arithmetic  6.72 us (3%)
  between operations  2.13 us (1%)
    ppermute x18, starting transfers between devices, shifted(): return lax.ppermute(block, axis, pairs)  63.2 us
    all_to_all x1, blocking collectives, swap(): return lax.all_to_all(blocks, axes, split_axis=0, concat_axis=0, tiled=True)  27.4 us
    all_to_all x3, waiting for transfers between devices, swap(): return lax.all_to_all(blocks, axes, split_axis=0, concat_axis=0, tiled=True)  16.7 us
    pallas_call x1, Pallas kernels, local(): pl.pallas_call(lambda *refs: forward_kernel(sizes, *refs), out_shape=(sha...  15.6 us
    all_to_all x3, starting transfers between devices, swap(): return lax.all_to_all(blocks, axes, split_axis=0, concat_axis=0, tiled=True)  14.7 us
    ppermute x18, waiting for transfers between devices, shifted(): return lax.ppermute(block, axis, pairs)  11.5 us
    pallas_call x1, Pallas kernels, local(): pl.pallas_call(lambda *refs: second_kernel(sizes, *refs), out_shape=(shap...  9.29 us
    pallas_call x1, Pallas kernels, local(): pl.pallas_call(lambda *refs: first_kernel(sizes, *refs), out_shape=(shape...  6.97 us
  transfers between devices with their start and end apart: 21, of which 6 were waited for; matrix products, arithmetic and copies ran while one was open for 8% of the time, Pallas kernels for 4%

profile of v4, /device:TPU:1, one launch (start us, length us, event | category | flops | bytes accessed | tf_op | source)
XLA Modules:
  0.0 193.6 jit_solution(12862016323316279425)
XLA Ops:
  1.4 4.0 %collective-permute-start = (bf16[2,8,4,128]{3,2,1,0:T(4,128)(2,1)S(1)}, bf16[2,8,4,128]{3,2,1,0:T(4,128)(2,1)S(1)}, u32[]{:S(2)}, u32[]{:S(2)}) collective-permute-start(bf16[2,8,4,128]{3,2,1,0:T(4,128)(2,1)S(1)} %bitcast.103), channel_id=1, source_target_pairs={{0,64},{32,96},{64,128},{96,160},{128,192},{160,224},{192,256},{22... | collective-permute-start | bytes 49160 | tf_op jit(solution)/shard_map/ppermute | solution.py:19
  6.4 10.6 %collective-permute-start.1 = (bf16[2,8,36,128]{3,2,1,0:T(8,128)(2,1)S(1)}, bf16[2,8,36,128]{3,2,1,0:T(8,128)(2,1)S(1)}, u32[]{:S(2)}, u32[]{:S(2)}) collective-permute-start(bf16[2,8,36,128]{3,2,1,0:T(8,128)(2,1)S(1)} %pad_maximum_fusion.7), channel_id=1, source_target_pairs={{0,32},{32,64},{64,96},{96,128},{128,160},{160,192},{192,224},{224... | collective-permute-start | bytes 442376 | tf_op jit(solution)/shard_map/ppermute | solution.py:19
  17.1 1.3 collective-permute-start.2
  18.4 1.3 collective-permute-start.3
  21.4 4.3 %all-to-all-start = ((bf16[4,16,4,68]{3,2,1,0:T(4,128)(2,1)}), bf16[4,16,4,68]{3,2,1,0:T(4,128)(2,1)S(1)}, u32[]{:S(2)}, u32[]{:S(2)}) async-start(bf16[4,16,4,68]{3,2,1,0:T(4,128)(2,1)} %pad_maximum_fusion.12), calls=%async_computation | async-start | bytes 131072 | tf_op jit(solution)/shard_map/all_to_all | solution.py:275
  29.4 5.3 %collective-permute-start.4 = (bf16[10,4,4,128]{3,2,1,0:T(4,128)(2,1)S(1)}, bf16[10,4,4,128]{3,2,1,0:T(4,128)(2,1)S(1)}, u32[]{:S(2)}, u32[]{:S(2)}) collective-permute-start(bf16[10,4,4,128]{3,2,1,0:T(4,128)(2,1)S(1)} %get-tuple-element.80), channel_id=1, source_target_pairs={{0,4},{4,8},{8,12},{12,16},{16,20},{20,24},{24,28},{1,5},{5,9},{9,... | collective-permute-start | bytes 122888 | tf_op jit(solution)/shard_map/ppermute | solution.py:19
  34.7 1.9 collective-permute-start.5
  36.7 3.6 %collective-permute-start.8 = (bf16[6,2,32,128]{3,2,1,0:T(8,128)(2,1)S(1)}, bf16[6,2,32,128]{3,2,1,0:T(8,128)(2,1)S(1)}, u32[]{:S(2)}, u32[]{:S(2)}) collective-permute-start(bf16[6,2,32,128]{3,2,1,0:T(8,128)(2,1)S(1)} %get-tuple-element.68), channel_id=1, source_target_pairs={{0,4},{4,8},{8,12},{12,16},{16,20},{20,24},{24,28},{1,5},{5,9},{9,... | collective-permute-start | bytes 294920 | tf_op jit(solution)/shard_map/ppermute | solution.py:19
  40.4 1.9 collective-permute-start.9
  42.6 4.1 %collective-permute-start.6 = (bf16[10,16,4,8]{3,2,1,0:T(4,128)(2,1)S(1)}, bf16[10,16,4,8]{3,2,1,0:T(4,128)(2,1)S(1)}, u32[]{:S(2)}, u32[]{:S(2)}) collective-permute-start(bf16[10,16,4,8]{3,2,1,0:T(4,128)(2,1)S(1)} %get-tuple-element.76), channel_id=1, source_target_pairs={{0,1},{1,2},{2,3},{4,5},{5,6},{6,7},{8,9},{9,10},{10,11},{12,13},{... | collective-permute-start | bytes 30728 | tf_op jit(solution)/shard_map/ppermute | solution.py:19
  46.7 1.3 collective-permute-start.7
  50.2 4.1 %collective-permute-start.10 = (bf16[6,12,2,32]{3,2,1,0:T(2,128)(2,1)S(1)}, bf16[6,12,2,32]{3,2,1,0:T(2,128)(2,1)S(1)}, u32[]{:S(2)}, u32[]{:S(2)}) collective-permute-start(bf16[6,12,2,32]{3,2,1,0:T(2,128)(2,1)S(1)} %copy.97), channel_id=1, source_target_pairs={{0,1},{1,2},{2,3},{4,5},{5,6},{6,7},{8,9},{9,10},{10,11},{12,13},{... | collective-permute-start | bytes 27656 | tf_op jit(solution)/shard_map/ppermute | solution.py:19
  56.7 2.8 %collective-permute-done.11.refs_8_ = bf16[6,12,2,32]{3,2,1,0:T(2,128)(2,1)S(1)} collective-permute-done((bf16[6,12,2,32]{3,2,1,0:T(2,128)(2,1)S(1)}, bf16[6,12,2,32]{3,2,1,0:T(2,128)(2,1)S(1)}, u32[]{:S(2)}, u32[]{:S(2)}) %collective-permute-start.11) | collective-permute-done | bytes 9248 | tf_op jit(solution)/shard_map/ppermute | solution.py:19
  59.5 15.6 %forward.1 = (bf16[2,8,32,128]{3,2,1,0:T(8,128)(2,1)S(1)}, bf16[4,64,128]{2,1,0:T(8,128)(2,1)S(1)}, bf16[4,64,128]{2,1,0:T(8,128)(2,1)S(1)}, f32[192,288]{1,0:T(...) custom-call(s32[3]{0:T(128)S(1)} %pad_add_fusion.refs_0_, ...), custom_call_target="tpu_custom_call" | custom-call | flops 4000000000 | bytes 12000000 | tf_op jit(solution)/shard_map/forward/pallas_call | solution.py:362
  75.2 3.6 %collective-permute-start.12 = (bf16[1,4,64,128]{3,2,1,0:T(8,128)(2,1)S(1)}, bf16[1,4,64,128]{3,2,1,0:T(8,128)(2,1)S(1)}, u32[]{:S(2)}, u32[]{:S(2)}) collective-permute-start(bf16[1,4,64,128]{3,2,1,0:T(8,128)(2,1)S(1)} %bitcast.77), channel_id=1, source_target_pairs={{0,64},{32,96},{64,128},{96,160},{128,192},{160,224},{192,256},{22... | collective-permute-start | bytes 196616 | tf_op jit(solution)/shard_map/ppermute | solution.py:19
  78.8 7.5 %collective-permute-start.13 = (bf16[1,4,64,128]{3,2,1,0:T(8,128)(2,1)S(1)}, bf16[1,4,64,128]{3,2,1,0:T(8,128)(2,1)S(1)}, u32[]{:S(2)}, u32[]{:S(2)}) collective-permute-start(bf16[1,4,64,128]{3,2,1,0:T(8,128)(2,1)S(1)} %bitcast.78), channel_id=1, source_target_pairs={{0,32},{32,64},{64,96},{96,128},{128,160},{160,192},{192,224},{224... | collective-permute-start | bytes 196616 | tf_op jit(solution)/shard_map/ppermute | solution.py:19
  86.3 1.3 collective-permute-start.14
  87.6 1.3 collective-permute-start.15
  90.1 1.9 select_maximum_fusion.refs_3_
  92.3 3.9 %collective-permute-done.14 = bf16[1,4,64,128]{3,2,1,0:T(8,128)(2,1)S(1)} collective-permute-done((bf16[1,4,64,128]{3,2,1,0:T(8,128)(2,1)S(1)}, bf16[1,4,64,128]{3,2,1,0:T(8,128)(2,1)S(1)}, u32[]{:S(2)}, u32[]{:S(2)}) %collective-permute-start.14) | collective-permute-done | bytes 65568 | tf_op jit(solution)/shard_map/ppermute | solution.py:19
  96.3 6.8 %collective-permute-start.16 = (bf16[5,2,64,128]{3,2,1,0:T(8,128)(2,1)S(1)}, bf16[5,2,64,128]{3,2,1,0:T(8,128)(2,1)S(1)}, u32[]{:S(2)}, u32[]{:S(2)}) collective-permute-start(bf16[5,2,64,128]{3,2,1,0:T(8,128)(2,1)S(1)} %get-tuple-element.70), channel_id=1, source_target_pairs={{0,4},{4,8},{8,12},{12,16},{16,20},{20,24},{24,28},{1,5},{5,9},{9,... | collective-permute-start | bytes 491528 | tf_op jit(solution)/shard_map/ppermute | solution.py:19
  103.1 1.9 collective-permute-start.17
  105.3 4.4 %collective-permute-done.17 = bf16[5,2,64,128]{3,2,1,0:T(8,128)(2,1)S(1)} collective-permute-done((bf16[5,2,64,128]{3,2,1,0:T(8,128)(2,1)S(1)}, bf16[5,2,64,128]{3,2,1,0:T(8,128)(2,1)S(1)}, u32[]{:S(2)}, u32[]{:S(2)}) %collective-permute-start.17) | collective-permute-done | bytes 163872 | tf_op jit(solution)/shard_map/ppermute | solution.py:19
  109.8 9.3 %second.1 = (bf16[6,12,96,256]{3,2,1,0:T(8,128)(2,1)}, f32[96,288]{1,0:T(8,128)S(1)}) custom-call(s32[3]{0:T(128)S(1)} %pad_add_fusion.refs_0_, bf16[5,8,64,128]{3,2,1,0:T(8,128)(2,1)S(1)} %pad_maximum_fusion.refs_1_, f32[6,12,32,256]{3,2,1,0:T(8,128)} %get-tuple-element.21.refs_2_, bf16[6,12,32,256]{3,2,1,0:T(8,128)(2,1)S(1)} %select_maximum_fusion.refs_3_, ...), custom_call_target="tpu_custom_call" | custom-call | flops 1000000000 | bytes 10000000 | tf_op jit(solution)/shard_map/second/pallas_call | solution.py:401
  120.1 6.4 %all-to-all-start.1 = ((bf16[32,56,128]{2,1,0:T(8,128)(2,1)}), bf16[32,56,128]{2,1,0:T(8,128)(2,1)}, u32[]{:S(2)}, u32[]{:S(2)}) async-start(bf16[32,56,128]{2,1,0:T(8,128)(2,1)} %pad_maximum_fusion.2), calls=%async_computation.1 | async-start | bytes 917504 | tf_op jit(solution)/shard_map/all_to_all | solution.py:275
  126.9 1.3 copy-done.1
  128.2 7.0 %first.1 = (bf16[4,10,96,256]{3,2,1,0:T(8,128)(2,1)S(1)}, bf16[32,128]{1,0:T(8,128)(2,1)S(1)}) custom-call(s32[3]{0:T(128)S(1)} %pad_add_fusion.refs_0_, bf16[6,12,96,256]{3,2,1,0:T(8,128)(2,1)} %get-tuple-element.25.refs_1_, f32[4,10,32,256]{3,2,1,0:T(8,128)S(1)} %copy-done.1, bf16[4,10,16,256]{3,2,1,0:T(8,128)(2,1)S(1)} %get-tuple-element.27.refs_3_, ...), custom_call_target="tpu_custom_call" | custom-call | flops 2000000000 | bytes 10000000 | tf_op jit(solution)/shard_map/first/pallas_call | solution.py:439
  135.2 6.4 %all-to-all-done.1 = bf16[32,56,128]{2,1,0:T(8,128)(2,1)} async-done(((bf16[32,56,128]{2,1,0:T(8,128)(2,1)}), bf16[32,56,128]{2,1,0:T(8,128)(2,1)}, u32[]{:S(2)}, u32[]{:S(2)}) %all-to-all-start.1) | async-done | bytes 458784 | tf_op jit(solution)/shard_map/all_to_all | solution.py:275
  142.6 27.4 %all_to_all.20 = bf16[16,56,128]{2,1,0:T(8,128)(2,1)S(1)} all-to-all(bf16[16,56,128]{2,1,0:T(8,128)(2,1)S(1)} %broadcast_in_dim.59), channel_id=1, replica_groups=mesh['gx'=16,'gy'=8,'gz'=4] {'gx'}, dimensions={0} | all-to-all | bytes 458752 | tf_op jit(solution)/shard_map/all_to_all | solution.py:275
  170.9 4.0 %all-to-all-start.3 = ((bf16[32,56,128]{2,1,0:T(8,128)(2,1)}), bf16[32,56,128]{2,1,0:T(8,128)(2,1)S(1)}, u32[]{:S(2)}, u32[]{:S(2)}) async-start(bf16[32,56,128]{2,1,0:T(8,128)(2,1)} %broadcast_in_dim.60), calls=%async_computation.3 | async-start | bytes 917504 | tf_op jit(solution)/shard_map/all_to_all | solution.py:275
  175.9 1.4 volume.1
  179.8 10.3 %all-to-all-done.3 = bf16[32,56,128]{2,1,0:T(8,128)(2,1)S(1)} async-done(((bf16[32,56,128]{2,1,0:T(8,128)(2,1)}), bf16[32,56,128]{2,1,0:T(8,128)(2,1)S(1)}, u32[]{:S(2)}, u32[]{:S(2)}) %all-to-all-start.3) | async-done | bytes 458784 | tf_op jit(solution)/shard_map/all_to_all | solution.py:275
  (133 shorter events, 23.1 us)
Async XLA Ops:
  0.6 27.6 %copy-start.2 = (bf16[64,3,3,3,32]{0,4,3,2,1:T(8,128)(2,1)S(1)}, bf16[64,3,3,3,32]{0,4,3,2,1:T(8,128)(2,1)}, u32[]{:S(2)}) copy-start(bf16[64,3,3,3,32]{0,4,3,2,1:T(8,128)(2,1)} %param.9) | copy-start | bytes 331780
  0.6 27.8 %copy-start.4 = (bf16[32,3,3,3,4]{0,4,3,2,1:T(4,128)(2,1)S(1)}, bf16[32,3,3,3,4]{0,4,3,2,1:T(4,128)(2,1)}, u32[]{:S(2)}) copy-start(bf16[32,3,3,3,4]{0,4,3,2,1:T(4,128)(2,1)} %param.7) | copy-start | bytes 20740
  1.4 27.8 %copy-start.5 = (bf16[4,2,8,128]{3,2,1,0:T(8,128)(2,1)S(1)}, bf16[4,2,8,128]{3,2,1,0:T(8,128)(2,1)}, u32[]{:S(2)}) copy-start(bf16[4,2,8,128]{3,2,1,0:T(8,128)(2,1)} %param.6) | copy-start | bytes 49156
  1.4 27.8 %collective-permute-start = (bf16[2,8,4,128]{3,2,1,0:T(4,128)(2,1)S(1)}, bf16[2,8,4,128]{3,2,1,0:T(4,128)(2,1)S(1)}, u32[]{:S(2)}, u32[]{:S(2)}) collective-permute-start(bf16[2,8,4,128]{3,2,1,0:T(4,128)(2,1)S(1)} %bitcast.103), channel_id=1, source_target_pairs={{0,64},{32,96},{64,128},{96,160},{128,192},{160,224},{192,256},{22... | collective-permute-start | bytes 49160 | tf_op jit(solution)/shard_map/ppermute | solution.py:19
  6.4 22.8 %collective-permute-start.1 = (bf16[2,8,36,128]{3,2,1,0:T(8,128)(2,1)S(1)}, bf16[2,8,36,128]{3,2,1,0:T(8,128)(2,1)S(1)}, u32[]{:S(2)}, u32[]{:S(2)}) collective-permute-start(bf16[2,8,36,128]{3,2,1,0:T(8,128)(2,1)S(1)} %pad_maximum_fusion.7), channel_id=1, source_target_pairs={{0,32},{32,64},{64,96},{96,128},{128,160},{160,192},{192,224},{224... | collective-permute-start | bytes 442376 | tf_op jit(solution)/shard_map/ppermute | solution.py:19
  17.1 12.2 %collective-permute-start.2 = (bf16[2,8,36,128]{3,2,1,0:T(8,128)(2,1)S(1)}, bf16[2,8,36,128]{3,2,1,0:T(8,128)(2,1)S(1)}, u32[]{:S(2)}, u32[]{:S(2)}) collective-permute-start(bf16[2,8,36,128]{3,2,1,0:T(8,128)(2,1)S(1)} %pad_maximum_fusion.7), channel_id=1, source_target_pairs={{32,0},{64,32},{96,64},{128,96},{160,128},{192,160},{224,192},{256... | collective-permute-start | bytes 442376 | tf_op jit(solution)/shard_map/ppermute | solution.py:19
  18.4 10.9 %collective-permute-start.3 = (bf16[2,8,4,128]{3,2,1,0:T(4,128)(2,1)S(1)}, bf16[2,8,4,128]{3,2,1,0:T(4,128)(2,1)S(1)}, u32[]{:S(2)}, u32[]{:S(2)}) collective-permute-start(bf16[2,8,4,128]{3,2,1,0:T(4,128)(2,1)S(1)} %bitcast.105), channel_id=1, source_target_pairs={{64,0},{96,32},{128,64},{160,96},{192,128},{224,160},{256,192},{28... | collective-permute-start | bytes 49160 | tf_op jit(solution)/shard_map/ppermute | solution.py:19
  21.4 27.8 %all-to-all-start = ((bf16[4,16,4,68]{3,2,1,0:T(4,128)(2,1)}), bf16[4,16,4,68]{3,2,1,0:T(4,128)(2,1)S(1)}, u32[]{:S(2)}, u32[]{:S(2)}) async-start(bf16[4,16,4,68]{3,2,1,0:T(4,128)(2,1)} %pad_maximum_fusion.12), calls=%async_computation | async-start | bytes 131072 | tf_op jit(solution)/shard_map/all_to_all | solution.py:275
  29.4 12.9 %collective-permute-start.4 = (bf16[10,4,4,128]{3,2,1,0:T(4,128)(2,1)S(1)}, bf16[10,4,4,128]{3,2,1,0:T(4,128)(2,1)S(1)}, u32[]{:S(2)}, u32[]{:S(2)}) collective-permute-start(bf16[10,4,4,128]{3,2,1,0:T(4,128)(2,1)S(1)} %get-tuple-element.80), channel_id=1, source_target_pairs={{0,4},{4,8},{8,12},{12,16},{16,20},{20,24},{24,28},{1,5},{5,9},{9,... | collective-permute-start | bytes 122888 | tf_op jit(solution)/shard_map/ppermute | solution.py:19
  34.7 7.6 %collective-permute-start.5 = (bf16[10,4,4,128]{3,2,1,0:T(4,128)(2,1)S(1)}, bf16[10,4,4,128]{3,2,1,0:T(4,128)(2,1)S(1)}, u32[]{:S(2)}, u32[]{:S(2)}) collective-permute-start(bf16[10,4,4,128]{3,2,1,0:T(4,128)(2,1)S(1)} %get-tuple-element.81), channel_id=1, source_target_pairs={{4,0},{8,4},{12,8},{16,12},{20,16},{24,20},{28,24},{5,1},{9,5},{13... | collective-permute-start | bytes 122888 | tf_op jit(solution)/shard_map/ppermute | solution.py:19
  36.7 12.7 %collective-permute-start.8 = (bf16[6,2,32,128]{3,2,1,0:T(8,128)(2,1)S(1)}, bf16[6,2,32,128]{3,2,1,0:T(8,128)(2,1)S(1)}, u32[]{:S(2)}, u32[]{:S(2)}) collective-permute-start(bf16[6,2,32,128]{3,2,1,0:T(8,128)(2,1)S(1)} %get-tuple-element.68), channel_id=1, source_target_pairs={{0,4},{4,8},{8,12},{12,16},{16,20},{20,24},{24,28},{1,5},{5,9},{9,... | collective-permute-start | bytes 294920 | tf_op jit(solution)/shard_map/ppermute | solution.py:19
  40.4 9.0 %collective-permute-start.9 = (bf16[6,2,32,128]{3,2,1,0:T(8,128)(2,1)S(1)}, bf16[6,2,32,128]{3,2,1,0:T(8,128)(2,1)S(1)}, u32[]{:S(2)}, u32[]{:S(2)}) collective-permute-start(bf16[6,2,32,128]{3,2,1,0:T(8,128)(2,1)S(1)} %get-tuple-element.69), channel_id=1, source_target_pairs={{4,0},{8,4},{12,8},{16,12},{20,16},{24,20},{28,24},{5,1},{9,5},{13... | collective-permute-start | bytes 294920 | tf_op jit(solution)/shard_map/ppermute | solution.py:19
  42.6 13.5 %collective-permute-start.6 = (bf16[10,16,4,8]{3,2,1,0:T(4,128)(2,1)S(1)}, bf16[10,16,4,8]{3,2,1,0:T(4,128)(2,1)S(1)}, u32[]{:S(2)}, u32[]{:S(2)}) collective-permute-start(bf16[10,16,4,8]{3,2,1,0:T(4,128)(2,1)S(1)} %get-tuple-element.76), channel_id=1, source_target_pairs={{0,1},{1,2},{2,3},{4,5},{5,6},{6,7},{8,9},{9,10},{10,11},{12,13},{... | collective-permute-start | bytes 30728 | tf_op jit(solution)/shard_map/ppermute | solution.py:19
  46.7 9.4 %collective-permute-start.7 = (bf16[10,16,4,8]{3,2,1,0:T(4,128)(2,1)S(1)}, bf16[10,16,4,8]{3,2,1,0:T(4,128)(2,1)S(1)}, u32[]{:S(2)}, u32[]{:S(2)}) collective-permute-start(bf16[10,16,4,8]{3,2,1,0:T(4,128)(2,1)S(1)} %get-tuple-element.77), channel_id=1, source_target_pairs={{1,0},{2,1},{3,2},{5,4},{6,5},{7,6},{9,8},{10,9},{11,10},{13,12},{... | collective-permute-start | bytes 30728 | tf_op jit(solution)/shard_map/ppermute | solution.py:19
  50.2 6.5 %collective-permute-start.10 = (bf16[6,12,2,32]{3,2,1,0:T(2,128)(2,1)S(1)}, bf16[6,12,2,32]{3,2,1,0:T(2,128)(2,1)S(1)}, u32[]{:S(2)}, u32[]{:S(2)}) collective-permute-start(bf16[6,12,2,32]{3,2,1,0:T(2,128)(2,1)S(1)} %copy.97), channel_id=1, source_target_pairs={{0,1},{1,2},{2,3},{4,5},{5,6},{6,7},{8,9},{9,10},{10,11},{12,13},{... | collective-permute-start | bytes 27656 | tf_op jit(solution)/shard_map/ppermute | solution.py:19
  54.8 4.7 %collective-permute-start.11 = (bf16[6,12,2,32]{3,2,1,0:T(2,128)(2,1)S(1)}, bf16[6,12,2,32]{3,2,1,0:T(2,128)(2,1)S(1)}, u32[]{:S(2)}, u32[]{:S(2)}) collective-permute-start(bf16[6,12,2,32]{3,2,1,0:T(2,128)(2,1)S(1)} %copy.98), channel_id=1, source_target_pairs={{1,0},{2,1},{3,2},{5,4},{6,5},{7,6},{9,8},{10,9},{11,10},{13,12},{... | collective-permute-start | bytes 27656 | tf_op jit(solution)/shard_map/ppermute | solution.py:19
  75.2 17.0 %collective-permute-start.12 = (bf16[1,4,64,128]{3,2,1,0:T(8,128)(2,1)S(1)}, bf16[1,4,64,128]{3,2,1,0:T(8,128)(2,1)S(1)}, u32[]{:S(2)}, u32[]{:S(2)}) collective-permute-start(bf16[1,4,64,128]{3,2,1,0:T(8,128)(2,1)S(1)} %bitcast.77), channel_id=1, source_target_pairs={{0,64},{32,96},{64,128},{96,160},{128,192},{160,224},{192,256},{22... | collective-permute-start | bytes 196616 | tf_op jit(solution)/shard_map/ppermute | solution.py:19
  78.8 13.5 %collective-permute-start.13 = (bf16[1,4,64,128]{3,2,1,0:T(8,128)(2,1)S(1)}, bf16[1,4,64,128]{3,2,1,0:T(8,128)(2,1)S(1)}, u32[]{:S(2)}, u32[]{:S(2)}) collective-permute-start(bf16[1,4,64,128]{3,2,1,0:T(8,128)(2,1)S(1)} %bitcast.78), channel_id=1, source_target_pairs={{0,32},{32,64},{64,96},{96,128},{128,160},{160,192},{192,224},{224... | collective-permute-start | bytes 196616 | tf_op jit(solution)/shard_map/ppermute | solution.py:19
  86.3 9.9 %collective-permute-start.14 = (bf16[1,4,64,128]{3,2,1,0:T(8,128)(2,1)S(1)}, bf16[1,4,64,128]{3,2,1,0:T(8,128)(2,1)S(1)}, u32[]{:S(2)}, u32[]{:S(2)}) collective-permute-start(bf16[1,4,64,128]{3,2,1,0:T(8,128)(2,1)S(1)} %bitcast.79), channel_id=1, source_target_pairs={{32,0},{64,32},{96,64},{128,96},{160,128},{192,160},{224,192},{256... | collective-permute-start | bytes 196616 | tf_op jit(solution)/shard_map/ppermute | solution.py:19
  87.6 8.6 %collective-permute-start.15 = (bf16[1,4,64,128]{3,2,1,0:T(8,128)(2,1)S(1)}, bf16[1,4,64,128]{3,2,1,0:T(8,128)(2,1)S(1)}, u32[]{:S(2)}, u32[]{:S(2)}) collective-permute-start(bf16[1,4,64,128]{3,2,1,0:T(8,128)(2,1)S(1)} %bitcast.80), channel_id=1, source_target_pairs={{64,0},{96,32},{128,64},{160,96},{192,128},{224,160},{256,192},{28... | collective-permute-start | bytes 196616 | tf_op jit(solution)/shard_map/ppermute | solution.py:19
  92.0 17.8 %copy-start = (bf16[4,10,96,256]{3,2,1,0:T(8,128)(2,1)S(1)}, bf16[4,10,96,256]{3,2,1,0:T(8,128)(2,1)}, u32[]{:S(2)}) copy-start(bf16[4,10,96,256]{3,2,1,0:T(8,128)(2,1)} %get-tuple-element.22.refs_4_) | copy-start | bytes 5898244
  96.3 9.0 %collective-permute-start.16 = (bf16[5,2,64,128]{3,2,1,0:T(8,128)(2,1)S(1)}, bf16[5,2,64,128]{3,2,1,0:T(8,128)(2,1)S(1)}, u32[]{:S(2)}, u32[]{:S(2)}) collective-permute-start(bf16[5,2,64,128]{3,2,1,0:T(8,128)(2,1)S(1)} %get-tuple-element.70), channel_id=1, source_target_pairs={{0,4},{4,8},{8,12},{12,16},{16,20},{20,24},{24,28},{1,5},{5,9},{9,... | collective-permute-start | bytes 491528 | tf_op jit(solution)/shard_map/ppermute | solution.py:19
  103.1 6.6 %collective-permute-start.17 = (bf16[5,2,64,128]{3,2,1,0:T(8,128)(2,1)S(1)}, bf16[5,2,64,128]{3,2,1,0:T(8,128)(2,1)S(1)}, u32[]{:S(2)}, u32[]{:S(2)}) collective-permute-start(bf16[5,2,64,128]{3,2,1,0:T(8,128)(2,1)S(1)} %get-tuple-element.71), channel_id=1, source_target_pairs={{4,0},{8,4},{12,8},{16,12},{20,16},{24,20},{28,24},{5,1},{9,5},{13... | collective-permute-start | bytes 491528 | tf_op jit(solution)/shard_map/ppermute | solution.py:19
  119.1 7.4 %copy-start.3 = (bf16[32,3,3,3,32]{4,0,3,2,1:T(8,128)(2,1)S(1)}, bf16[32,3,3,3,32]{4,0,3,2,1:T(8,128)(2,1)}, u32[]{:S(2)}) copy-start(bf16[32,3,3,3,32]{4,0,3,2,1:T(8,128)(2,1)} %param.8) | copy-start | bytes 165892
  120.1 21.6 %all-to-all-start.1 = ((bf16[32,56,128]{2,1,0:T(8,128)(2,1)}), bf16[32,56,128]{2,1,0:T(8,128)(2,1)}, u32[]{:S(2)}, u32[]{:S(2)}) async-start(bf16[32,56,128]{2,1,0:T(8,128)(2,1)} %pad_maximum_fusion.2), calls=%async_computation.1 | async-start | bytes 917504 | tf_op jit(solution)/shard_map/all_to_all | solution.py:275
  126.9 1.3 copy-start.1
  170.9 19.1 %all-to-all-start.3 = ((bf16[32,56,128]{2,1,0:T(8,128)(2,1)}), bf16[32,56,128]{2,1,0:T(8,128)(2,1)S(1)}, u32[]{:S(2)}, u32[]{:S(2)}) async-start(bf16[32,56,128]{2,1,0:T(8,128)(2,1)} %broadcast_in_dim.60), calls=%async_computation.3 | async-start | bytes 917504 | tf_op jit(solution)/shard_map/all_to_all | solution.py:275
